TPU v7x, 256 devices: a whole 4x4x8 slice. The times are simulated.
256 devices in a mesh: gx: 8 (over x, core), gy: 32 (over z, y).
Axes of the slice: x: 4, y: 4, z: 8, core: 2. Of those that a mesh axis runs over, the one named last changes fastest.
Arguments:
- volume: bfloat16 [64, 64, 64, 128], P('gx', 'gy'), may hold values from -6 to 6
- weight_entry: bfloat16 [3, 3, 3, 128, 128], replicated, may hold values from -0.15625 to 0.15625
- weight_down: bfloat16 [2, 2, 2, 128, 256], replicated, may hold values from -0.25 to 0.25
- weight_deep_first: bfloat16 [3, 3, 3, 256, 256], replicated, may hold values from -0.109375 to 0.109375
- weight_deep_second: bfloat16 [3, 3, 3, 256, 256], replicated, may hold values from -0.109375 to 0.109375
- weight_upward: bfloat16 [2, 2, 2, 256, 128], replicated, may hold values from -0.5 to 0.5
- weight_decoder: bfloat16 [3, 3, 3, 256, 128], replicated, may hold values from -0.109375 to 0.109375
Outputs:
- decoded: bfloat16 [64, 64, 64, 128], P('gx', 'gy')
All inputs are finite; a program needn't handle non-finite values.
Results may differ from a plain program's by a relative error of at most 0.013.
Values may be sent and summed in bfloat16 or wider, within the bound.
No kernel may reach another device: no remote copies, remote signals or barrier semaphores. Data moves between devices by JAX's collectives and lax.ppermute only.
A program may use at most 64 MiB of HBM per device.

v0:
```python
import jax
import jax.numpy as jnp
from jax import lax
from jax.sharding import PartitionSpec as P


def with_halo(block, sides, width):
    for axis, dim in sides:
        count = lax.axis_size(axis)
        forward = [(i, i + 1) for i in range(count - 1)]
        backward = [(target, source) for source, target in forward]
        low = lax.ppermute(
            lax.slice_in_dim(block, block.shape[dim] - width, None, axis=dim), axis, forward
        )
        high = lax.ppermute(lax.slice_in_dim(block, 0, width, axis=dim), axis, backward)
        block = jnp.concatenate([low, block, high], axis=dim)
    return block


def leaky_unit(values):
    return jnp.where(values > 0, values, 0.1 * values)


def conv_cube(extended, weight):
    width_x = extended.shape[0] - 2
    width_y = extended.shape[1] - 2
    z_cells = extended.shape[2]
    channels = extended.shape[3]
    outputs = weight.shape[4]
    padded = jnp.pad(extended, ((0, 0), (0, 0), (1, 1), (0, 0)))
    stacked = jnp.concatenate(
        [padded[:, :, 0:z_cells], padded[:, :, 1 : z_cells + 1], padded[:, :, 2 : z_cells + 2]],
        axis=3,
    )
    flat_weight = weight.reshape(3, 3, 3 * channels, outputs)
    summed = jnp.zeros((width_x * width_y * z_cells, outputs), jnp.float32)
    for row_off in range(3):
        for col_off in range(3):
            window = stacked[row_off : row_off + width_x, col_off : col_off + width_y].reshape(
                -1, 3 * channels
            )
            summed = summed + jnp.dot(
                window, flat_weight[row_off, col_off], preferred_element_type=jnp.float32
            )
    return summed.reshape(width_x, width_y, z_cells, outputs)


def down_sample(inputs, weight):
    blocks = inputs.reshape(
        inputs.shape[0] // 2, 2, inputs.shape[1] // 2, 2, inputs.shape[2] // 2, 2, inputs.shape[3]
    )
    return jnp.einsum("iajbkdc,abdco->ijko", blocks, weight, preferred_element_type=jnp.float32)


def up_sample(inputs, weight):
    result = jnp.einsum("ijkc,abdco->iajbkdo", inputs, weight, preferred_element_type=jnp.float32)
    return result.reshape(
        2 * inputs.shape[0], 2 * inputs.shape[1], 2 * inputs.shape[2], weight.shape[4]
    )


def local(
    volume,
    weight_entry,
    weight_down,
    weight_deep_first,
    weight_deep_second,
    weight_upward,
    weight_decoder,
):
    volume_ext = with_halo(volume, (("gx", 0), ("gy", 1)), 1)
    encoded = leaky_unit(conv_cube(volume_ext, weight_entry)).astype(jnp.bfloat16)
    skip_ext = with_halo(encoded, (("gx", 0), ("gy", 1)), 1)
    coarse = leaky_unit(down_sample(encoded, weight_down)).astype(jnp.bfloat16)
    coarse_ext = with_halo(coarse, (("gx", 0), ("gy", 1)), 1)
    deep_one = leaky_unit(conv_cube(coarse_ext, weight_deep_first)).astype(jnp.bfloat16)
    deep_ext = with_halo(deep_one, (("gx", 0), ("gy", 1)), 1)
    deep_two = leaky_unit(conv_cube(deep_ext, weight_deep_second)).astype(jnp.bfloat16)
    upward = leaky_unit(up_sample(deep_two, weight_upward)).astype(jnp.bfloat16)
    upward_ext = with_halo(upward, (("gx", 0), ("gy", 1)), 1)
    joined = jnp.concatenate([upward_ext, skip_ext], axis=3)
    return leaky_unit(conv_cube(joined, weight_decoder)).astype(jnp.bfloat16)


def solution(mesh):
    return jax.shard_map(
        local,
        mesh=mesh,
        in_specs=(P("gx", "gy", None, None), P(), P(), P(), P(), P(), P()),
        out_specs=P("gx", "gy", None, None),
        check_vma=False,
    )
```

profile of v0, /device:TPU:122, one launch (start us, length us, event | category | flops | bytes accessed | tf_op | source)
XLA Modules:
  0.0 127.8 jit_solution(15042148939616108291)
XLA Ops:
  0.8 1.9 %collective-permute-start = (bf16[1,2,64,128]{3,2,1,0:T(8,128)(2,1)S(1)}, bf16[1,2,64,128]{3,2,1,0:T(8,128)(2,1)S(1)}, u32[]{:S(2)}, u32[]{:S(2)}) collective-permute-start(bf16[1,2,64,128]{3,2,1,0:T(8,128)(2,1)S(1)} %get-tuple-element.60), channel_id=1, source_target_pairs={{0,32},{32,64},{64,96},{96,128},{128,160},{160,192},{192,224},{1,3... | collective-permute-start | bytes 98312 | tf_op jit(solution)/shard_map/ppermute | solution.py:12
  2.8 3.6 %collective-permute-start.1 = (bf16[1,2,64,128]{3,2,1,0:T(8,128)(2,1)S(1)}, bf16[1,2,64,128]{3,2,1,0:T(8,128)(2,1)S(1)}, u32[]{:S(2)}, u32[]{:S(2)}) collective-permute-start(bf16[1,2,64,128]{3,2,1,0:T(8,128)(2,1)S(1)} %get-tuple-element.59), channel_id=1, source_target_pairs={{32,0},{64,32},{96,64},{128,96},{160,128},{192,160},{224,192},{33,... | collective-permute-start | bytes 98312 | tf_op jit(solution)/shard_map/ppermute | solution.py:15
  8.0 4.7 %collective-permute-start.2 = (bf16[10,1,64,128]{3,2,1,0:T(8,128)(2,1)S(1)}, bf16[10,1,64,128]{3,2,1,0:T(8,128)(2,1)S(1)}, u32[]{:S(2)}, u32[]{:S(2)}) collective-permute-start(bf16[10,1,64,128]{3,2,1,0:T(8,128)(2,1)S(1)} %get-tuple-element.53), channel_id=1, source_target_pairs={{0,1},{1,2},{2,3},{3,4},{4,5},{5,6},{6,7},{7,8},{8,9},{9,10},{10,1... | collective-permute-start | bytes 491528 | tf_op jit(solution)/shard_map/ppermute | solution.py:12
  12.7 1.9 %collective-permute-start.3 = (bf16[10,1,64,128]{3,2,1,0:T(8,128)(2,1)S(1)}, bf16[10,1,64,128]{3,2,1,0:T(8,128)(2,1)S(1)}, u32[]{:S(2)}, u32[]{:S(2)}) collective-permute-start(bf16[10,1,64,128]{3,2,1,0:T(8,128)(2,1)S(1)} %get-tuple-element.54), channel_id=1, source_target_pairs={{1,0},{2,1},{3,2},{4,3},{5,4},{6,5},{7,6},{8,7},{9,8},{10,9},{11,1... | collective-permute-start | bytes 491528 | tf_op jit(solution)/shard_map/ppermute | solution.py:15
  14.7 2.1 %collective-permute-done.2 = bf16[10,1,64,128]{3,2,1,0:T(8,128)(2,1)S(1)} collective-permute-done((bf16[10,1,64,128]{3,2,1,0:T(8,128)(2,1)S(1)}, bf16[10,1,64,128]{3,2,1,0:T(8,128)(2,1)S(1)}, u32[]{:S(2)}, u32[]{:S(2)}) %collective-permute-start.2) | collective-permute-done | bytes 163872 | tf_op jit(solution)/shard_map/ppermute | solution.py:12
  16.7 8.0 %collective-permute-done.3 = bf16[10,1,64,128]{3,2,1,0:T(8,128)(2,1)S(1)} collective-permute-done((bf16[10,1,64,128]{3,2,1,0:T(8,128)(2,1)S(1)}, bf16[10,1,64,128]{3,2,1,0:T(8,128)(2,1)S(1)}, u32[]{:S(2)}, u32[]{:S(2)}) %collective-permute-start.3) | collective-permute-done | bytes 163872 | tf_op jit(solution)/shard_map/ppermute | solution.py:15
  25.7 1.2 fusion.94
  31.2 2.0 %collective-permute-start.4 = (bf16[1,1,32,256]{3,2,0,1:T(8,128)(2,1)S(1)}, bf16[1,1,32,256]{3,2,0,1:T(8,128)(2,1)S(1)}, u32[]{:S(2)}, u32[]{:S(2)}) collective-permute-start(bf16[1,1,32,256]{3,2,0,1:T(8,128)(2,1)S(1)} %get-tuple-element.63), channel_id=1, source_target_pairs={{0,32},{32,64},{64,96},{96,128},{128,160},{160,192},{192,224},{1,3... | collective-permute-start | bytes 49160 | tf_op jit(solution)/shard_map/ppermute | solution.py:12
  33.2 3.5 %collective-permute-start.5 = (bf16[1,1,32,256]{3,2,1,0:T(8,128)(2,1)S(1)}, bf16[1,1,32,256]{3,2,1,0:T(8,128)(2,1)S(1)}, u32[]{:S(2)}, u32[]{:S(2)}) collective-permute-start(bf16[1,1,32,256]{3,2,1,0:T(8,128)(2,1)S(1)} %get-tuple-element.64), channel_id=1, source_target_pairs={{32,0},{64,32},{96,64},{128,96},{160,128},{192,160},{224,192},{33,... | collective-permute-start | bytes 49160 | tf_op jit(solution)/shard_map/ppermute | solution.py:15
  36.8 1.4 %collective-permute-done.5 = bf16[1,1,32,256]{3,2,1,0:T(8,128)(2,1)S(1)} collective-permute-done((bf16[1,1,32,256]{3,2,1,0:T(8,128)(2,1)S(1)}, bf16[1,1,32,256]{3,2,1,0:T(8,128)(2,1)S(1)}, u32[]{:S(2)}, u32[]{:S(2)}) %collective-permute-start.5) | collective-permute-done | bytes 16416 | tf_op jit(solution)/shard_map/ppermute | solution.py:15
  38.2 1.9 %collective-permute-start.7 = (bf16[6,1,32,256]{3,2,0,1:T(8,128)(2,1)S(1)}, bf16[6,1,32,256]{3,2,0,1:T(8,128)(2,1)S(1)}, u32[]{:S(2)}, u32[]{:S(2)}) collective-permute-start(bf16[6,1,32,256]{3,2,0,1:T(8,128)(2,1)S(1)} %pad_maximum_fusion.6), channel_id=1, source_target_pairs={{1,0},{2,1},{3,2},{4,3},{5,4},{6,5},{7,6},{8,7},{9,8},{10,9},{11,1... | collective-permute-start | bytes 294920 | tf_op jit(solution)/shard_map/ppermute | solution.py:15
  40.2 7.2 %collective-permute-start.6 = (bf16[6,1,32,256]{3,2,0,1:T(8,128)(2,1)S(1)}, bf16[6,1,32,256]{3,2,0,1:T(8,128)(2,1)S(1)}, u32[]{:S(2)}, u32[]{:S(2)}) collective-permute-start(bf16[6,1,32,256]{3,2,0,1:T(8,128)(2,1)S(1)} %pad_maximum_fusion.6), channel_id=1, source_target_pairs={{0,1},{1,2},{2,3},{3,4},{4,5},{5,6},{6,7},{7,8},{8,9},{9,10},{10,1... | collective-permute-start | bytes 294920 | tf_op jit(solution)/shard_map/ppermute | solution.py:12
  48.3 1.8 %collective-permute-done.6 = bf16[6,1,32,256]{3,2,0,1:T(8,128)(2,1)S(1)} collective-permute-done((bf16[6,1,32,256]{3,2,0,1:T(8,128)(2,1)S(1)}, bf16[6,1,32,256]{3,2,0,1:T(8,128)(2,1)S(1)}, u32[]{:S(2)}, u32[]{:S(2)}) %collective-permute-start.6) | collective-permute-done | bytes 98336 | tf_op jit(solution)/shard_map/ppermute | solution.py:12
  50.7 1.8 %copy-done.2 = bf16[3,3,3,256,256]{4,3,2,1,0:T(8,128)(2,1)S(1)} copy-done((bf16[3,3,3,256,256]{4,3,2,1,0:T(8,128)(2,1)S(1)}, bf16[3,3,3,256,256]{4,3,2,1,0:T(8,128)(2,1)}, u32[]{:S(2)}) %copy-start.2) | copy-done | bytes 3538968
  54.5 2.5 %collective-permute-start.8 = (bf16[1,1,32,256]{3,2,0,1:T(8,128)(2,1)S(1)}, bf16[1,1,32,256]{3,2,0,1:T(8,128)(2,1)S(1)}, u32[]{:S(2)}, u32[]{:S(2)}) collective-permute-start(bf16[1,1,32,256]{3,2,0,1:T(8,128)(2,1)S(1)} %get-tuple-element.61), channel_id=1, source_target_pairs={{0,32},{32,64},{64,96},{96,128},{128,160},{160,192},{192,224},{1,3... | collective-permute-start | bytes 49160 | tf_op jit(solution)/shard_map/ppermute | solution.py:12
  57.0 3.1 %collective-permute-start.9 = (bf16[1,1,32,256]{3,2,0,1:T(8,128)(2,1)S(1)}, bf16[1,1,32,256]{3,2,0,1:T(8,128)(2,1)S(1)}, u32[]{:S(2)}, u32[]{:S(2)}) collective-permute-start(bf16[1,1,32,256]{3,2,0,1:T(8,128)(2,1)S(1)} %get-tuple-element.62), channel_id=1, source_target_pairs={{32,0},{64,32},{96,64},{128,96},{160,128},{192,160},{224,192},{33,... | collective-permute-start | bytes 49160 | tf_op jit(solution)/shard_map/ppermute | solution.py:15
  60.1 1.9 %collective-permute-start.16 = (bf16[1,2,64,128]{3,2,1,0:T(8,128)(2,1)S(1)}, bf16[1,2,64,128]{3,2,1,0:T(8,128)(2,1)S(1)}, u32[]{:S(2)}, u32[]{:S(2)}) collective-permute-start(bf16[1,2,64,128]{3,2,1,0:T(8,128)(2,1)S(1)} %get-tuple-element.57), channel_id=1, source_target_pairs={{0,32},{32,64},{64,96},{96,128},{128,160},{160,192},{192,224},{1,3... | collective-permute-start | bytes 98312 | tf_op jit(solution)/shard_map/ppermute | solution.py:12
  62.0 3.6 %collective-permute-start.17 = (bf16[1,2,64,128]{3,2,1,0:T(8,128)(2,1)S(1)}, bf16[1,2,64,128]{3,2,1,0:T(8,128)(2,1)S(1)}, u32[]{:S(2)}, u32[]{:S(2)}) collective-permute-start(bf16[1,2,64,128]{3,2,1,0:T(8,128)(2,1)S(1)} %get-tuple-element.58), channel_id=1, source_target_pairs={{32,0},{64,32},{96,64},{128,96},{160,128},{192,160},{224,192},{33,... | collective-permute-start | bytes 98312 | tf_op jit(solution)/shard_map/ppermute | solution.py:15
  65.7 1.9 %collective-permute-start.11 = (bf16[6,1,32,256]{3,2,0,1:T(8,128)(2,1)S(1)}, bf16[6,1,32,256]{3,2,0,1:T(8,128)(2,1)S(1)}, u32[]{:S(2)}, u32[]{:S(2)}) collective-permute-start(bf16[6,1,32,256]{3,2,0,1:T(8,128)(2,1)S(1)} %pad_maximum_fusion.7), channel_id=1, source_target_pairs={{1,0},{2,1},{3,2},{4,3},{5,4},{6,5},{7,6},{8,7},{9,8},{10,9},{11,1... | collective-permute-start | bytes 294920 | tf_op jit(solution)/shard_map/ppermute | solution.py:15
  67.7 7.7 %collective-permute-start.10 = (bf16[6,1,32,256]{3,2,0,1:T(8,128)(2,1)S(1)}, bf16[6,1,32,256]{3,2,0,1:T(8,128)(2,1)S(1)}, u32[]{:S(2)}, u32[]{:S(2)}) collective-permute-start(bf16[6,1,32,256]{3,2,0,1:T(8,128)(2,1)S(1)} %pad_maximum_fusion.7), channel_id=1, source_target_pairs={{0,1},{1,2},{2,3},{3,4},{4,5},{5,6},{6,7},{7,8},{8,9},{9,10},{10,1... | collective-permute-start | bytes 294920 | tf_op jit(solution)/shard_map/ppermute | solution.py:12
  76.0 1.5 %collective-permute-done.10 = bf16[6,1,32,256]{3,2,0,1:T(8,128)(2,1)S(1)} collective-permute-done((bf16[6,1,32,256]{3,2,0,1:T(8,128)(2,1)S(1)}, bf16[6,1,32,256]{3,2,0,1:T(8,128)(2,1)S(1)}, u32[]{:S(2)}, u32[]{:S(2)}) %collective-permute-start.10) | collective-permute-done | bytes 98336 | tf_op jit(solution)/shard_map/ppermute | solution.py:12
  78.2 1.8 %copy-done.3 = bf16[3,3,3,256,256]{4,3,2,1,0:T(8,128)(2,1)S(1)} copy-done((bf16[3,3,3,256,256]{4,3,2,1,0:T(8,128)(2,1)S(1)}, bf16[3,3,3,256,256]{4,3,2,1,0:T(8,128)(2,1)}, u32[]{:S(2)}) %copy-start.3) | copy-done | bytes 3538968
  82.7 1.9 %collective-permute-start.12 = (bf16[1,2,64,128]{3,2,1,0:T(8,128)(2,1)S(1)}, bf16[1,2,64,128]{3,2,1,0:T(8,128)(2,1)S(1)}, u32[]{:S(2)}, u32[]{:S(2)}) collective-permute-start(bf16[1,2,64,128]{3,2,1,0:T(8,128)(2,1)S(1)} %get-tuple-element.55), channel_id=1, source_target_pairs={{0,32},{32,64},{64,96},{96,128},{128,160},{160,192},{192,224},{1,3... | collective-permute-start | bytes 98312 | tf_op jit(solution)/shard_map/ppermute | solution.py:12
  84.6 3.6 %collective-permute-start.13 = (bf16[1,2,64,128]{3,2,1,0:T(8,128)(2,1)S(1)}, bf16[1,2,64,128]{3,2,1,0:T(8,128)(2,1)S(1)}, u32[]{:S(2)}, u32[]{:S(2)}) collective-permute-start(bf16[1,2,64,128]{3,2,1,0:T(8,128)(2,1)S(1)} %get-tuple-element.56), channel_id=1, source_target_pairs={{32,0},{64,32},{96,64},{128,96},{160,128},{192,160},{224,192},{33,... | collective-permute-start | bytes 98312 | tf_op jit(solution)/shard_map/ppermute | solution.py:15
  88.3 7.6 %collective-permute-start.18 = (bf16[10,1,64,128]{3,2,1,0:T(8,128)(2,1)S(1)}, bf16[10,1,64,128]{3,2,1,0:T(8,128)(2,1)S(1)}, u32[]{:S(2)}, u32[]{:S(2)}) collective-permute-start(bf16[10,1,64,128]{3,2,1,0:T(8,128)(2,1)S(1)} %get-tuple-element.51), channel_id=1, source_target_pairs={{0,1},{1,2},{2,3},{3,4},{4,5},{5,6},{6,7},{7,8},{8,9},{9,10},{10,1... | collective-permute-start | bytes 491528 | tf_op jit(solution)/shard_map/ppermute | solution.py:12
  96.0 1.9 %collective-permute-start.19 = (bf16[10,1,64,128]{3,2,1,0:T(8,128)(2,1)S(1)}, bf16[10,1,64,128]{3,2,1,0:T(8,128)(2,1)S(1)}, u32[]{:S(2)}, u32[]{:S(2)}) collective-permute-start(bf16[10,1,64,128]{3,2,1,0:T(8,128)(2,1)S(1)} %get-tuple-element.52), channel_id=1, source_target_pairs={{1,0},{2,1},{3,2},{4,3},{5,4},{6,5},{7,6},{8,7},{9,8},{10,9},{11,1... | collective-permute-start | bytes 491528 | tf_op jit(solution)/shard_map/ppermute | solution.py:15
  98.0 7.2 %collective-permute-start.14 = (bf16[10,1,64,128]{3,2,1,0:T(8,128)(2,1)S(1)}, bf16[10,1,64,128]{3,2,1,0:T(8,128)(2,1)S(1)}, u32[]{:S(2)}, u32[]{:S(2)}) collective-permute-start(bf16[10,1,64,128]{3,2,1,0:T(8,128)(2,1)S(1)} %get-tuple-element.49), channel_id=1, source_target_pairs={{0,1},{1,2},{2,3},{3,4},{4,5},{5,6},{6,7},{7,8},{8,9},{9,10},{10,1... | collective-permute-start | bytes 491528 | tf_op jit(solution)/shard_map/ppermute | solution.py:12
  105.2 2.1 %collective-permute-start.15 = (bf16[10,1,64,128]{3,2,1,0:T(8,128)(2,1)S(1)}, bf16[10,1,64,128]{3,2,1,0:T(8,128)(2,1)S(1)}, u32[]{:S(2)}, u32[]{:S(2)}) collective-permute-start(bf16[10,1,64,128]{3,2,1,0:T(8,128)(2,1)S(1)} %get-tuple-element.50), channel_id=1, source_target_pairs={{1,0},{2,1},{3,2},{4,3},{5,4},{6,5},{7,6},{8,7},{9,8},{10,9},{11,1... | collective-permute-start | bytes 491528 | tf_op jit(solution)/shard_map/ppermute | solution.py:15
  108.1 7.7 %collective-permute-done.15 = bf16[10,1,64,128]{3,2,1,0:T(8,128)(2,1)S(1)} collective-permute-done((bf16[10,1,64,128]{3,2,1,0:T(8,128)(2,1)S(1)}, bf16[10,1,64,128]{3,2,1,0:T(8,128)(2,1)S(1)}, u32[]{:S(2)}, u32[]{:S(2)}) %collective-permute-start.15) | collective-permute-done | bytes 163872 | tf_op jit(solution)/shard_map/ppermute | solution.py:15
  115.8 1.8 %fusion.1 = bf16[10,4,66,256]{3,2,1,0:T(8,128)(2,1)S(1)} fusion(bf16[10,1,64,128]{3,2,1,0:T(8,128)(2,1)S(1)} %collective-permute-done.19, bf16[10,1,64,128]{3,2,1,0:T(8,128)(2,1)S(1)} %collective-permute-done.15, bf16[10,1,64,128]{3,2,1,0:T(8,128)(2,1)S(1)} %collective-permute-done.18, bf16[10,1,64,128]{3,2,1,0:T(8,128)(2,1)S(1)} %collective-permute-done.14, ...), kind=kLoop, calls=%fused_computation.12 | loop fusion | flops 22302720 | bytes 2662400 | tf_op jit(solution)/shard_map/concatenate | solution.py:81
  118.4 1.6 %pad_maximum_fusion = bf16[10,4,64,768]{3,2,1,0:T(8,128)(2,1)S(1)} fusion(bf16[10,4,64,256]{3,2,1,0:T(8,128)(2,1)S(1)} %get-tuple-element.24, bf16[10,1,64,128]{3,2,1,0:T(8,128)(2,1)S(1)} %collective-permute-done.19, bf16[1,2,64,128]{3,2,1,0:T(8,128)(2,1)S(1)} %collective-permute-done.17, bf16[8,2,64,128]{3,2,1,0:T(8,128)(2,1)S(1)} %fusion.35, ...), kind=kLoop, calls=%fused_computation.2 | loop fusion | flops 47185920 | bytes 7864320 | tf_op jit(solution)/shard_map/concatenate | solution.py:31
  120.0 1.8 %fusion.93 = (bf16[8,2,64,768]{3,2,1,0:T(8,128)(2,1)S(1)}, bf16[8,2,64,768]{3,2,1,0:T(8,128)(2,1)S(1)}, bf16[8,2,64,768]{3,2,1,0:T(8,128)(2,1)S(1)}, bf16[8,2,64...) fusion(bf16[10,4,64,768]{3,2,1,0:T(8,128)(2,1)S(1)} %pad_maximu, ...), kind=kLoop, calls=%fused_computation.171 | loop fusion | bytes 28311552 | tf_op jit(solution)/shard_map/slice | solution.py:39
  (96 shorter events, 22.5 us)
Async XLA Ops:
  0.0 82.0 %copy-start = (bf16[2,2,2,256,128]{4,3,2,1,0:T(8,128)(2,1)S(1)}, bf16[2,2,2,256,128]{4,3,2,1,0:T(8,128)(2,1)}, u32[]{:S(2)}) copy-start(bf16[2,2,2,256,128]{4,3,2,1,0:T(8,128)(2,1)} %param.12) | copy-start | bytes 1572868
  0.8 5.6 %collective-permute-start = (bf16[1,2,64,128]{3,2,1,0:T(8,128)(2,1)S(1)}, bf16[1,2,64,128]{3,2,1,0:T(8,128)(2,1)S(1)}, u32[]{:S(2)}, u32[]{:S(2)}) collective-permute-start(bf16[1,2,64,128]{3,2,1,0:T(8,128)(2,1)S(1)} %get-tuple-element.60), channel_id=1, source_target_pairs={{0,32},{32,64},{64,96},{96,128},{128,160},{160,192},{192,224},{1,3... | collective-permute-start | bytes 98312 | tf_op jit(solution)/shard_map/ppermute | solution.py:12
  2.8 5.2 %collective-permute-start.1 = (bf16[1,2,64,128]{3,2,1,0:T(8,128)(2,1)S(1)}, bf16[1,2,64,128]{3,2,1,0:T(8,128)(2,1)S(1)}, u32[]{:S(2)}, u32[]{:S(2)}) collective-permute-start(bf16[1,2,64,128]{3,2,1,0:T(8,128)(2,1)S(1)} %get-tuple-element.59), channel_id=1, source_target_pairs={{32,0},{64,32},{96,64},{128,96},{160,128},{192,160},{224,192},{33,... | collective-permute-start | bytes 98312 | tf_op jit(solution)/shard_map/ppermute | solution.py:15
  8.0 8.7 %collective-permute-start.2 = (bf16[10,1,64,128]{3,2,1,0:T(8,128)(2,1)S(1)}, bf16[10,1,64,128]{3,2,1,0:T(8,128)(2,1)S(1)}, u32[]{:S(2)}, u32[]{:S(2)}) collective-permute-start(bf16[10,1,64,128]{3,2,1,0:T(8,128)(2,1)S(1)} %get-tuple-element.53), channel_id=1, source_target_pairs={{0,1},{1,2},{2,3},{3,4},{4,5},{5,6},{6,7},{7,8},{8,9},{9,10},{10,1... | collective-permute-start | bytes 491528 | tf_op jit(solution)/shard_map/ppermute | solution.py:12
  12.7 12.0 %collective-permute-start.3 = (bf16[10,1,64,128]{3,2,1,0:T(8,128)(2,1)S(1)}, bf16[10,1,64,128]{3,2,1,0:T(8,128)(2,1)S(1)}, u32[]{:S(2)}, u32[]{:S(2)}) collective-permute-start(bf16[10,1,64,128]{3,2,1,0:T(8,128)(2,1)S(1)} %get-tuple-element.54), channel_id=1, source_target_pairs={{1,0},{2,1},{3,2},{4,3},{5,4},{6,5},{7,6},{8,7},{9,8},{10,9},{11,1... | collective-permute-start | bytes 491528 | tf_op jit(solution)/shard_map/ppermute | solution.py:15
  25.7 1.2 copy-start.5
  29.9 1.0 copy-start.6
  31.2 5.6 %collective-permute-start.4 = (bf16[1,1,32,256]{3,2,0,1:T(8,128)(2,1)S(1)}, bf16[1,1,32,256]{3,2,0,1:T(8,128)(2,1)S(1)}, u32[]{:S(2)}, u32[]{:S(2)}) collective-permute-start(bf16[1,1,32,256]{3,2,0,1:T(8,128)(2,1)S(1)} %get-tuple-element.63), channel_id=1, source_target_pairs={{0,32},{32,64},{64,96},{96,128},{128,160},{160,192},{192,224},{1,3... | collective-permute-start | bytes 49160 | tf_op jit(solution)/shard_map/ppermute | solution.py:12
  33.2 5.0 %collective-permute-start.5 = (bf16[1,1,32,256]{3,2,1,0:T(8,128)(2,1)S(1)}, bf16[1,1,32,256]{3,2,1,0:T(8,128)(2,1)S(1)}, u32[]{:S(2)}, u32[]{:S(2)}) collective-permute-start(bf16[1,1,32,256]{3,2,1,0:T(8,128)(2,1)S(1)} %get-tuple-element.64), channel_id=1, source_target_pairs={{32,0},{64,32},{96,64},{128,96},{160,128},{192,160},{224,192},{33,... | collective-permute-start | bytes 49160 | tf_op jit(solution)/shard_map/ppermute | solution.py:15
  38.2 10.1 %collective-permute-start.7 = (bf16[6,1,32,256]{3,2,0,1:T(8,128)(2,1)S(1)}, bf16[6,1,32,256]{3,2,0,1:T(8,128)(2,1)S(1)}, u32[]{:S(2)}, u32[]{:S(2)}) collective-permute-start(bf16[6,1,32,256]{3,2,0,1:T(8,128)(2,1)S(1)} %pad_maximum_fusion.6), channel_id=1, source_target_pairs={{1,0},{2,1},{3,2},{4,3},{5,4},{6,5},{7,6},{8,7},{9,8},{10,9},{11,1... | collective-permute-start | bytes 294920 | tf_op jit(solution)/shard_map/ppermute | solution.py:15
  40.2 9.9 %collective-permute-start.6 = (bf16[6,1,32,256]{3,2,0,1:T(8,128)(2,1)S(1)}, bf16[6,1,32,256]{3,2,0,1:T(8,128)(2,1)S(1)}, u32[]{:S(2)}, u32[]{:S(2)}) collective-permute-start(bf16[6,1,32,256]{3,2,0,1:T(8,128)(2,1)S(1)} %pad_maximum_fusion.6), channel_id=1, source_target_pairs={{0,1},{1,2},{2,3},{3,4},{4,5},{5,6},{6,7},{7,8},{8,9},{9,10},{10,1... | collective-permute-start | bytes 294920 | tf_op jit(solution)/shard_map/ppermute | solution.py:12
  50.5 2.0 %copy-start.2 = (bf16[3,3,3,256,256]{4,3,2,1,0:T(8,128)(2,1)S(1)}, bf16[3,3,3,256,256]{4,3,2,1,0:T(8,128)(2,1)}, u32[]{:S(2)}) copy-start(bf16[3,3,3,256,256]{4,3,2,1,0:T(8,128)(2,1)} %param.10) | copy-start | bytes 10616836
  54.5 11.2 %collective-permute-start.8 = (bf16[1,1,32,256]{3,2,0,1:T(8,128)(2,1)S(1)}, bf16[1,1,32,256]{3,2,0,1:T(8,128)(2,1)S(1)}, u32[]{:S(2)}, u32[]{:S(2)}) collective-permute-start(bf16[1,1,32,256]{3,2,0,1:T(8,128)(2,1)S(1)} %get-tuple-element.61), channel_id=1, source_target_pairs={{0,32},{32,64},{64,96},{96,128},{128,160},{160,192},{192,224},{1,3... | collective-permute-start | bytes 49160 | tf_op jit(solution)/shard_map/ppermute | solution.py:12
  57.0 8.7 %collective-permute-start.9 = (bf16[1,1,32,256]{3,2,0,1:T(8,128)(2,1)S(1)}, bf16[1,1,32,256]{3,2,0,1:T(8,128)(2,1)S(1)}, u32[]{:S(2)}, u32[]{:S(2)}) collective-permute-start(bf16[1,1,32,256]{3,2,0,1:T(8,128)(2,1)S(1)} %get-tuple-element.62), channel_id=1, source_target_pairs={{32,0},{64,32},{96,64},{128,96},{160,128},{192,160},{224,192},{33,... | collective-permute-start | bytes 49160 | tf_op jit(solution)/shard_map/ppermute | solution.py:15
  60.1 15.3 %collective-permute-start.16 = (bf16[1,2,64,128]{3,2,1,0:T(8,128)(2,1)S(1)}, bf16[1,2,64,128]{3,2,1,0:T(8,128)(2,1)S(1)}, u32[]{:S(2)}, u32[]{:S(2)}) collective-permute-start(bf16[1,2,64,128]{3,2,1,0:T(8,128)(2,1)S(1)} %get-tuple-element.57), channel_id=1, source_target_pairs={{0,32},{32,64},{64,96},{96,128},{128,160},{160,192},{192,224},{1,3... | collective-permute-start | bytes 98312 | tf_op jit(solution)/shard_map/ppermute | solution.py:12
  62.0 13.4 %collective-permute-start.17 = (bf16[1,2,64,128]{3,2,1,0:T(8,128)(2,1)S(1)}, bf16[1,2,64,128]{3,2,1,0:T(8,128)(2,1)S(1)}, u32[]{:S(2)}, u32[]{:S(2)}) collective-permute-start(bf16[1,2,64,128]{3,2,1,0:T(8,128)(2,1)S(1)} %get-tuple-element.58), channel_id=1, source_target_pairs={{32,0},{64,32},{96,64},{128,96},{160,128},{192,160},{224,192},{33,... | collective-permute-start | bytes 98312 | tf_op jit(solution)/shard_map/ppermute | solution.py:15
  65.7 10.3 %collective-permute-start.11 = (bf16[6,1,32,256]{3,2,0,1:T(8,128)(2,1)S(1)}, bf16[6,1,32,256]{3,2,0,1:T(8,128)(2,1)S(1)}, u32[]{:S(2)}, u32[]{:S(2)}) collective-permute-start(bf16[6,1,32,256]{3,2,0,1:T(8,128)(2,1)S(1)} %pad_maximum_fusion.7), channel_id=1, source_target_pairs={{1,0},{2,1},{3,2},{4,3},{5,4},{6,5},{7,6},{8,7},{9,8},{10,9},{11,1... | collective-permute-start | bytes 294920 | tf_op jit(solution)/shard_map/ppermute | solution.py:15
  67.7 9.9 %collective-permute-start.10 = (bf16[6,1,32,256]{3,2,0,1:T(8,128)(2,1)S(1)}, bf16[6,1,32,256]{3,2,0,1:T(8,128)(2,1)S(1)}, u32[]{:S(2)}, u32[]{:S(2)}) collective-permute-start(bf16[6,1,32,256]{3,2,0,1:T(8,128)(2,1)S(1)} %pad_maximum_fusion.7), channel_id=1, source_target_pairs={{0,1},{1,2},{2,3},{3,4},{4,5},{5,6},{6,7},{7,8},{8,9},{9,10},{10,1... | collective-permute-start | bytes 294920 | tf_op jit(solution)/shard_map/ppermute | solution.py:12
  77.9 2.0 %copy-start.3 = (bf16[3,3,3,256,256]{4,3,2,1,0:T(8,128)(2,1)S(1)}, bf16[3,3,3,256,256]{4,3,2,1,0:T(8,128)(2,1)}, u32[]{:S(2)}) copy-start(bf16[3,3,3,256,256]{4,3,2,1,0:T(8,128)(2,1)} %param.11) | copy-start | bytes 10616836
  82.7 15.2 %collective-permute-start.12 = (bf16[1,2,64,128]{3,2,1,0:T(8,128)(2,1)S(1)}, bf16[1,2,64,128]{3,2,1,0:T(8,128)(2,1)S(1)}, u32[]{:S(2)}, u32[]{:S(2)}) collective-permute-start(bf16[1,2,64,128]{3,2,1,0:T(8,128)(2,1)S(1)} %get-tuple-element.55), channel_id=1, source_target_pairs={{0,32},{32,64},{64,96},{96,128},{128,160},{160,192},{192,224},{1,3... | collective-permute-start | bytes 98312 | tf_op jit(solution)/shard_map/ppermute | solution.py:12
  84.6 13.3 %collective-permute-start.13 = (bf16[1,2,64,128]{3,2,1,0:T(8,128)(2,1)S(1)}, bf16[1,2,64,128]{3,2,1,0:T(8,128)(2,1)S(1)}, u32[]{:S(2)}, u32[]{:S(2)}) collective-permute-start(bf16[1,2,64,128]{3,2,1,0:T(8,128)(2,1)S(1)} %get-tuple-element.56), channel_id=1, source_target_pairs={{32,0},{64,32},{96,64},{128,96},{160,128},{192,160},{224,192},{33,... | collective-permute-start | bytes 98312 | tf_op jit(solution)/shard_map/ppermute | solution.py:15
  88.3 19.0 %collective-permute-start.18 = (bf16[10,1,64,128]{3,2,1,0:T(8,128)(2,1)S(1)}, bf16[10,1,64,128]{3,2,1,0:T(8,128)(2,1)S(1)}, u32[]{:S(2)}, u32[]{:S(2)}) collective-permute-start(bf16[10,1,64,128]{3,2,1,0:T(8,128)(2,1)S(1)} %get-tuple-element.51), channel_id=1, source_target_pairs={{0,1},{1,2},{2,3},{3,4},{4,5},{5,6},{6,7},{7,8},{8,9},{9,10},{10,1... | collective-permute-start | bytes 491528 | tf_op jit(solution)/shard_map/ppermute | solution.py:12
  96.0 11.4 %collective-permute-start.19 = (bf16[10,1,64,128]{3,2,1,0:T(8,128)(2,1)S(1)}, bf16[10,1,64,128]{3,2,1,0:T(8,128)(2,1)S(1)}, u32[]{:S(2)}, u32[]{:S(2)}) collective-permute-start(bf16[10,1,64,128]{3,2,1,0:T(8,128)(2,1)S(1)} %get-tuple-element.52), channel_id=1, source_target_pairs={{1,0},{2,1},{3,2},{4,3},{5,4},{6,5},{7,6},{8,7},{9,8},{10,9},{11,1... | collective-permute-start | bytes 491528 | tf_op jit(solution)/shard_map/ppermute | solution.py:15
  98.0 10.1 %collective-permute-start.14 = (bf16[10,1,64,128]{3,2,1,0:T(8,128)(2,1)S(1)}, bf16[10,1,64,128]{3,2,1,0:T(8,128)(2,1)S(1)}, u32[]{:S(2)}, u32[]{:S(2)}) collective-permute-start(bf16[10,1,64,128]{3,2,1,0:T(8,128)(2,1)S(1)} %get-tuple-element.49), channel_id=1, source_target_pairs={{0,1},{1,2},{2,3},{3,4},{4,5},{5,6},{6,7},{7,8},{8,9},{9,10},{10,1... | collective-permute-start | bytes 491528 | tf_op jit(solution)/shard_map/ppermute | solution.py:12
  105.2 10.5 %collective-permute-start.15 = (bf16[10,1,64,128]{3,2,1,0:T(8,128)(2,1)S(1)}, bf16[10,1,64,128]{3,2,1,0:T(8,128)(2,1)S(1)}, u32[]{:S(2)}, u32[]{:S(2)}) collective-permute-start(bf16[10,1,64,128]{3,2,1,0:T(8,128)(2,1)S(1)} %get-tuple-element.50), channel_id=1, source_target_pairs={{1,0},{2,1},{3,2},{4,3},{5,4},{6,5},{7,6},{8,7},{9,8},{10,9},{11,1... | collective-permute-start | bytes 491528 | tf_op jit(solution)/shard_map/ppermute | solution.py:15
  120.0 1.8 %copy-start.4 = (bf16[3,3,3,256,128]{4,3,2,1,0:T(8,128)(2,1)S(1)}, bf16[3,3,3,256,128]{4,3,2,1,0:T(8,128)(2,1)}, u32[]{:S(2)}) copy-start(bf16[3,3,3,256,128]{4,3,2,1,0:T(8,128)(2,1)} %param.13) | copy-start | bytes 5308420
  126.4 1.4 %copy-start.1 = (bf16[2,2,2,256,128]{4,3,2,1,0:T(8,128)(2,1)S(1)}, bf16[2,2,2,256,128]{4,3,2,1,0:T(8,128)(2,1)}, u32[]{:S(2)}) copy-start(bf16[2,2,2,256,128]{4,3,2,1,0:T(8,128)(2,1)} %param.12) | copy-start | bytes 1572868
where the time goes:
time: 129 us; the launch traced here: 128 us
  starting transfers between devices  72.1 us (56%)
  waiting for transfers between devices  25.2 us (20%)
  matrix products  12.8 us (10%)
  local copies, waits for them, and re-layouts  11.5 us (9%)
  other arithmetic  5.36 us (4%)
    ppermute x10, starting transfers between devices, with_halo(): lax.ppermute(lax.slice_in_dim(block, block.shape[dim] - width, None, axis...  44.8 us
    ppermute x10, starting transfers between devices, with_halo(): lax.ppermute(lax.slice_in_dim(block, 0, width, axis=dim), axis, backward)  27.3 us
    ppermute x10, waiting for transfers between devices, with_halo(): lax.ppermute(lax.slice_in_dim(block, 0, width, axis=dim), axis, backward)  19.2 us
    dot_general x36, matrix products, conv_cube(): jnp.dot(window, flat_weight[row_off, col_off], preferred_element_type=jnp...  12.4 us
    ppermute x10, waiting for transfers between devices, with_halo(): lax.ppermute(lax.slice_in_dim(block, block.shape[dim] - width, None, axis...  6.08 us
    unnamed x16, local copies, waits for them, and re-layouts  5.18 us
    slice x4, local copies, waits for them, and re-layouts, conv_cube(): stacked[row_off:row_off + width_x, col_off:col_off + width_y]  3.38 us
  transfers between devices with their start and end apart: 20, of which 10 were waited for; matrix products, arithmetic and copies ran while one was open for 1% of the time, Pallas kernels for 0%

commit v1 on v0

v1 whole, which is shorter than its diff:
```python
import jax
import jax.numpy as jnp
from jax import lax
from jax.experimental import pallas as pl
from jax.experimental.pallas import tpu as pltpu
from jax.sharding import PartitionSpec as P

BF = jnp.bfloat16
F32 = jnp.float32
LIMIT = 48 * 1024 * 1024


def leaky_unit(values):
    return jnp.where(values > 0, values, 0.1 * values)


def inside(index, count):
    return (index >= 0) & (index < count)


def depth_taps(cells):
    depth = cells.shape[0]
    at = lax.broadcasted_iota(jnp.int32, cells.shape, 0)
    before = jnp.where(at == 0, 0.0, pltpu.roll(cells, 1, axis=0))
    after = jnp.where(at == depth - 1, 0.0, pltpu.roll(cells, depth - 1, axis=0))
    return before.astype(BF), cells.astype(BF), after.astype(BF)


def entry_kernel(own, y1, y2, x1, x2, weight, down, encoded, coarse, stacked, fine):
    gx, gy = lax.axis_index("gx"), lax.axis_index("gy")
    odd_x, odd_y = lax.rem(gx, 2) == 1, lax.rem(gy, 2) == 1
    nx, ny = lax.axis_size("gx"), lax.axis_size("gy")

    def put(row, col, cells):
        for tap, part in enumerate(depth_taps(cells)):
            lane = (col * 3 + tap) * 128
            stacked[row, :, lane : lane + 128] = part

    def one_row(i, carry):
        first, second = y1[i].astype(F32), y2[i].astype(F32)
        low = jnp.where(odd_y, first, second)
        high = jnp.where(odd_y, second, first)
        put(i + 1, 0, jnp.where(gy > 0, low, 0.0))
        put(i + 1, 1, own[i, 0].astype(F32))
        put(i + 1, 2, own[i, 1].astype(F32))
        put(i + 1, 3, jnp.where(gy < ny - 1, high, 0.0))
        return carry

    lax.fori_loop(0, 8, one_row, 0)
    for col in range(4):
        first, second = x1[col].astype(F32), x2[col].astype(F32)
        low = jnp.where(odd_x, first, second)
        high = jnp.where(odd_x, second, first)
        ok = inside(gy * 2 - 1 + col, ny * 2)
        put(0, col, jnp.where(ok & (gx > 0), low, 0.0))
        put(9, col, jnp.where(ok & (gx < nx - 1), high, 0.0))

    total = jnp.zeros((512, 256), F32)
    for off in range(3):
        total = total + jnp.dot(
            stacked[off : off + 8].reshape(512, 1536), weight[off], preferred_element_type=F32
        )
    result = leaky_unit(total).astype(BF).reshape(8, 64, 256)
    for b in range(2):
        half = result[:, :, b * 128 : b * 128 + 128]
        encoded[:, b] = half
        fine[:, b] = half.astype(F32)
    small = jnp.zeros((128, 256), F32)
    for a in range(2):
        for d in range(2):
            cells = jnp.concatenate(
                [
                    jnp.concatenate(
                        [fine[2 * i + a, b, pl.ds(d, 32, stride=2), :] for b in range(2)], axis=1
                    )
                    for i in range(4)
                ],
                axis=0,
            ).astype(BF)
            small = small + jnp.dot(
                cells, down[a, :, d].reshape(256, 256), preferred_element_type=F32
            )
    coarse[...] = leaky_unit(small).astype(BF).reshape(4, 32, 256)


def fill_deep(rows, first_row, planes, stacked):
    gy = lax.axis_index("gy")
    nx, ny = lax.axis_size("gx"), lax.axis_size("gy")

    for row in range(rows):
        ok_row = inside(first_row + row, nx * 4)
        for plane, cells in enumerate(planes(row)):
            ok = ok_row & inside(gy - 1 + plane, ny)
            for tap, part in enumerate(depth_taps(jnp.where(ok, cells, 0.0))):
                lane = (plane * 3 + tap) * 256
                stacked[row, :, lane : lane + 256] = part


def deep_conv(rows, stacked, weight, out):
    total = jnp.zeros((rows * 32, 256), F32)
    for off in range(3):
        total = total + jnp.dot(
            stacked[off : off + rows].reshape(rows * 32, 2304),
            weight[off],
            preferred_element_type=F32,
        )
    out[...] = leaky_unit(total).astype(BF).reshape(rows, 32, 256)


def first_kernel(own, y1, y2, x1, x2, weight, out, stacked):
    gx, gy = lax.axis_index("gx"), lax.axis_index("gy")
    odd_x, odd_y = lax.rem(gx, 2) == 1, lax.rem(gy, 2) == 1

    def planes(row):
        if 3 <= row < 7:
            first, second = y1[row - 3].astype(F32), y2[row - 3].astype(F32)
            return (
                jnp.where(odd_y, first, second),
                own[row - 3].astype(F32),
                jnp.where(odd_y, second, first),
            )
        result = []
        for plane in range(3):
            at = row if row < 3 else row - 7
            first, second = x1[at, plane].astype(F32), x2[at, plane].astype(F32)
            if row < 3:
                result.append(jnp.where(odd_x, first, second))
            else:
                result.append(jnp.where(odd_x, second, first))
        return result

    fill_deep(10, gx * 4 - 3, planes, stacked)
    deep_conv(8, stacked, weight, out)


def second_kernel(own, y1, y2, weight, out, stacked):
    gx, gy = lax.axis_index("gx"), lax.axis_index("gy")
    odd_y = lax.rem(gy, 2) == 1

    def planes(row):
        first, second = y1[row].astype(F32), y2[row].astype(F32)
        return (
            jnp.where(odd_y, first, second),
            own[row].astype(F32),
            jnp.where(odd_y, second, first),
        )

    fill_deep(8, gx * 4 - 2, planes, stacked)
    deep_conv(6, stacked, weight, out)


def decode_kernel(
    own, y1, y2, encoded, ex1, ex2, ey1, ey2, up, weight, decoded, stacked, upward
):
    gx, gy = lax.axis_index("gx"), lax.axis_index("gy")
    odd_x, odd_y = lax.rem(gx, 2) == 1, lax.rem(gy, 2) == 1
    nx, ny = lax.axis_size("gx"), lax.axis_size("gy")

    low = jnp.where(odd_y, y1[...].astype(F32), y2[...].astype(F32)).astype(BF).reshape(192, 256)
    high = jnp.where(odd_y, y2[...].astype(F32), y1[...].astype(F32)).astype(BF).reshape(192, 256)
    mid = own[...].reshape(192, 256)
    for col, (cells, b) in enumerate(((low, 1), (mid, 0), (mid, 1), (high, 0))):
        for a in range(2):
            for d in range(2):
                part = leaky_unit(
                    jnp.dot(cells, up[a, b, d], preferred_element_type=F32)
                ).reshape(6, 32, 128)
                for i in range(6):
                    row = 2 * i + a - 1
                    if 0 <= row < 10:
                        upward[row, col, pl.ds(d, 32, stride=2), :] = part[i]

    def put(row, col, half, cells):
        for tap, part in enumerate(depth_taps(cells)):
            lane = (col * 3 + tap) * 256 + half * 128
            stacked[row, :, lane : lane + 128] = part

    def one_row(row, carry):
        ok_row = inside(gx * 8 - 1 + row, nx * 8)
        for col in range(4):
            ok = ok_row & inside(gy * 2 - 1 + col, ny * 2)
            put(row, col, 0, jnp.where(ok, upward[row, col], 0.0))
        first, second = ey1[row].astype(F32), ey2[row].astype(F32)
        put(row, 0, 1, jnp.where(ok_row & (gy > 0), jnp.where(odd_y, first, second), 0.0))
        put(row, 3, 1, jnp.where(ok_row & (gy < ny - 1), jnp.where(odd_y, second, first), 0.0))
        return carry

    lax.fori_loop(0, 10, one_row, 0)

    def center(row, carry):
        put(row + 1, 1, 1, encoded[row, 0].astype(F32))
        put(row + 1, 2, 1, encoded[row, 1].astype(F32))
        return carry

    lax.fori_loop(0, 8, center, 0)
    for col in range(2):
        first, second = ex1[col].astype(F32), ex2[col].astype(F32)
        put(0, col + 1, 1, jnp.where(gx > 0, jnp.where(odd_x, first, second), 0.0))
        put(9, col + 1, 1, jnp.where(gx < nx - 1, jnp.where(odd_x, second, first), 0.0))

    total = jnp.zeros((512, 256), F32)
    for off in range(3):
        total = total + jnp.dot(
            stacked[off : off + 8].reshape(512, 3072), weight[off], preferred_element_type=F32
        )
    result = leaky_unit(total).astype(BF).reshape(8, 64, 256)
    decoded[:, 0] = result[:, :, :128]
    decoded[:, 1] = result[:, :, 128:]


def call(kernel, outs, scratch, name, flops, *operands):
    vmem = pl.BlockSpec(memory_space=pltpu.VMEM)
    return pl.pallas_call(
        kernel,
        out_shape=[jax.ShapeDtypeStruct(shape, BF) for shape in outs],
        in_specs=[vmem] * len(operands),
        out_specs=[vmem] * len(outs),
        scratch_shapes=[pltpu.VMEM(shape, dtype) for shape, dtype in scratch],
        compiler_params=pltpu.CompilerParams(vmem_limit_bytes=LIMIT),
        cost_estimate=pl.CostEstimate(flops=flops, bytes_accessed=4 << 20, transcendentals=0),
        name=name,
    )(*operands)


def pair_columns(weight):
    depth = 3 * weight.shape[3]
    flat = weight.reshape(3, 3 * depth, 128)
    first = jnp.pad(flat, ((0, 0), (0, depth), (0, 0)))
    second = jnp.pad(flat, ((0, 0), (depth, 0), (0, 0)))
    return jnp.concatenate([first, second], axis=2)


def near(count):
    return [(i, i ^ 1) for i in range(count)]


def far(count):
    return [(i, (((i + 1) ^ 1) - 1) % count) for i in range(count)]


def swap_y(first, second):
    count = lax.axis_size("gy")
    return lax.ppermute(first, "gy", near(count)), lax.ppermute(second, "gy", far(count))


def swap_x(first, second):
    count = lax.axis_size("gx")
    return lax.ppermute(first, "gx", near(count)), lax.ppermute(second, "gx", far(count))


def local(
    volume,
    weight_entry,
    weight_down,
    weight_deep_first,
    weight_deep_second,
    weight_upward,
    weight_decoder,
):
    odd_x = lax.rem(lax.axis_index("gx"), 2)
    odd_y = lax.rem(lax.axis_index("gy"), 2)

    def column(array, at):
        return lax.dynamic_index_in_dim(array, at, axis=1, keepdims=False)

    def rows(array, at, count):
        return lax.dynamic_slice_in_dim(array, at, count, axis=0)

    y1, y2 = swap_y(column(volume, 1 - odd_y), column(volume, odd_y))
    low = jnp.where(odd_y == 1, y1, y2)
    high = jnp.where(odd_y == 1, y2, y1)

    def edge(at):
        return jnp.concatenate(
            [rows(low, at, 1), rows(volume, at, 1)[0], rows(high, at, 1)], axis=0
        )

    x1, x2 = swap_x(edge(7 * (1 - odd_x)), edge(7 * odd_x))
    encoded, coarse = call(
        entry_kernel,
        [(8, 2, 64, 128), (4, 32, 256)],
        [((10, 64, 1536), BF), ((8, 2, 64, 128), F32)],
        "entry",
        1_300_000_000,
        volume,
        y1,
        y2,
        x1,
        x2,
        pair_columns(weight_entry),
        weight_down,
    )

    c1, c2 = swap_y(coarse, coarse)
    c_low = jnp.where(odd_y == 1, c1, c2)
    c_high = jnp.where(odd_y == 1, c2, c1)

    def coarse_edge(at):
        return jnp.stack([rows(c_low, at, 3), rows(coarse, at, 3), rows(c_high, at, 3)], axis=1)

    d1, d2 = swap_x(coarse_edge(1 - odd_x), coarse_edge(odd_x))
    e1, e2 = swap_x(rows(encoded, 7 * (1 - odd_x), 1)[0], rows(encoded, 7 * odd_x, 1)[0])
    (deep_one,) = call(
        first_kernel,
        [(8, 32, 256)],
        [((10, 32, 2304), BF)],
        "first",
        1_000_000_000,
        coarse,
        c1,
        c2,
        d1,
        d2,
        weight_deep_first.reshape(3, 2304, 256),
    )
    f1, f2 = swap_y(deep_one, deep_one)

    e_low = jnp.where(odd_x == 1, e1, e2)
    e_high = jnp.where(odd_x == 1, e2, e1)

    def encoded_edge(at):
        return jnp.concatenate(
            [rows(e_low, at, 1), column(encoded, at), rows(e_high, at, 1)], axis=0
        )

    g1, g2 = swap_y(encoded_edge(1 - odd_y), encoded_edge(odd_y))
    (deep_two,) = call(
        second_kernel,
        [(6, 32, 256)],
        [((8, 32, 2304), BF)],
        "second",
        700_000_000,
        deep_one,
        f1,
        f2,
        weight_deep_second.reshape(3, 2304, 256),
    )
    h1, h2 = swap_y(deep_two, deep_two)
    (decoded,) = call(
        decode_kernel,
        [(8, 2, 64, 128)],
        [((10, 64, 3072), BF), ((10, 4, 64, 128), F32)],
        "decode",
        2_700_000_000,
        deep_two,
        h1,
        h2,
        encoded,
        e1,
        e2,
        g1,
        g2,
        weight_upward,
        pair_columns(weight_decoder),
    )
    return decoded


def solution(mesh):
    return jax.shard_map(
        local,
        mesh=mesh,
        in_specs=(P("gx", "gy", None, None), P(), P(), P(), P(), P(), P()),
        out_specs=P("gx", "gy", None, None),
        check_vma=False,
    )
```

time: 129 us -> 67.6 us (0.52)
  the two profiles are of different devices: /device:TPU:122 before, /device:TPU:0 now
where the time goes in v1:
time: 67.6 us; the launch traced here: 67.3 us
  starting transfers between devices  26.4 us (39%)
  waiting for transfers between devices  16.4 us (24%)
  Pallas kernels  9.59 us (14%)
  local copies, waits for them, and re-layouts  7.36 us (11%)
  other arithmetic  7.28 us (11%)
    ppermute x5, starting transfers between devices, swap_y(): lax.ppermute(second, 'gy', far(count))  18.1 us
    pallas_call x4, Pallas kernels, call(): pl.pallas_call(kernel, out_shape=[jax.ShapeDtypeStruct(shape, BF) for sha...  9.59 us
    ppermute x5, waiting for transfers between devices, swap_y(): lax.ppermute(second, 'gy', far(count))  8.79 us
    ppermute x3, starting transfers between devices, swap_x(): lax.ppermute(second, 'gx', far(count))  6.08 us
    concatenate x2, other arithmetic, pair_columns(): return jnp.concatenate([first, second], axis=2)  5.9 us
    unnamed x22, local copies, waits for them, and re-layouts  5.49 us
    ppermute x3, waiting for transfers between devices, swap_x(): lax.ppermute(second, 'gx', far(count))  4.38 us
    ppermute x5, waiting for transfers between devices, swap_y(): lax.ppermute(first, 'gy', near(count))  3.21 us
  transfers between devices with their start and end apart: 16, of which 8 were waited for; matrix products, arithmetic and copies ran while one was open for 11% of the time, Pallas kernels for 1%

profile of v1, /device:TPU:0, one launch (start us, length us, event | category | flops | bytes accessed | tf_op | source)
XLA Modules:
  0.0 67.3 jit_solution(12494454227144331033)
XLA Ops:
  0.0 1.0 %dynamic-slice_bitcast_fusion.2 = (bf16[8,64,128]{2,1,0:T(8,128)(2,1)S(1)}, bf16[8,64,128]{2,1,0:T(8,128)(2,1)S(1)}) fusion(bf16[8,2,64,128]{3,2,1,0:T(8,128)(2,1)} %own.1, s32[]{:T(128)S(6)} %select_n.72, s32[]{:T(128)S(6)} %select_n.71), kind=kLoop, calls=%fused_computation.16 | loop fusion | bytes 524296 | tf_op jit(solution)/shard_map/jit(dynamic_index_in_dim)/squeeze | solution.py:264
  1.0 6.7 %collective-permute-start.1 = (bf16[8,64,128]{2,1,0:T(8,128)(2,1)S(1)}, bf16[8,64,128]{2,1,0:T(8,128)(2,1)S(1)}, u32[]{:S(2)}, u32[]{:S(2)}) collective-permute-start(bf16[8,64,128]{2,1,0:T(8,128)(2,1)S(1)} %get-tuple-element.17), channel_id=1, source_target_pairs={{0,31},{1,2},{2,1},{3,4},{4,3},{5,6},{6,5},{7,8},{8,7},{9,10},{10,... | collective-permute-start | bytes 393224 | tf_op jit(solution)/shard_map/ppermute | solution.py:243
  7.7 0.8 %dynamic-slice_bitcast_fusion.12 = (bf16[2,64,128]{2,1,0:T(8,128)(2,1)S(1)}, bf16[2,64,128]{2,1,0:T(8,128)(2,1)S(1)}) fusion(bf16[8,2,64,128]{3,2,1,0:T(8,128)(2,1)} %own.1, s32[]{:T(128)S(6)} %select_n.77, s32[]{:T(128)S(6)} %select_n.75), kind=kLoop, calls=%fused_computation.32 | loop fusion | bytes 131080 | tf_op jit(solution)/shard_map/squeeze | solution.py:275
  8.4 2.7 %collective-permute-done.1.y2 = bf16[8,64,128]{2,1,0:T(8,128)(2,1)S(1)} collective-permute-done((bf16[8,64,128]{2,1,0:T(8,128)(2,1)S(1)}, bf16[8,64,128]{2,1,0:T(8,128)(2,1)S(1)}, u32[]{:S(2)}, u32[]{:S(2)}) %collective-permute-start.1) | collective-permute-done | bytes 131104 | tf_op jit(solution)/shard_map/ppermute | solution.py:243
  11.1 1.5 %collective-permute-done.y1 = bf16[8,64,128]{2,1,0:T(8,128)(2,1)S(1)} collective-permute-done((bf16[8,64,128]{2,1,0:T(8,128)(2,1)S(1)}, bf16[8,64,128]{2,1,0:T(8,128)(2,1)S(1)}, u32[]{:S(2)}, u32[]{:S(2)}) %collective-permute-start) | collective-permute-done | bytes 131104 | tf_op jit(solution)/shard_map/ppermute | solution.py:243
  12.7 0.6 pad_maximum_fusion.4
  13.3 0.6 pad_maximum_fusion.5
  13.9 2.9 %collective-permute-start.3 = (bf16[4,64,128]{2,1,0:T(8,128)(2,1)}, bf16[4,64,128]{2,1,0:T(8,128)(2,1)}, u32[]{:S(2)}, u32[]{:S(2)}) collective-permute-start(bf16[4,64,128]{2,1,0:T(8,128)(2,1)} %pad_maximum_fusion.5), channel_id=1, source_target_pairs={{0,224},{32,64},{64,32},{96,128},{128,96},{160,192},{192,160},{224... | collective-permute-start | bytes 196616 | tf_op jit(solution)/shard_map/ppermute | solution.py:248
  16.8 3.2 %fusion.5.weight = bf16[3,1536,256]{2,1,0:T(8,128)(2,1)} fusion(bf16[3,1152,128]{2,1,0:T(8,128)(2,1)} %bitcast.35), kind=kLoop, calls=%fused_computation.9 | loop fusion | flops 9437184 | bytes 3244032 | tf_op jit(solution)/shard_map/concatenate | solution.py:230
  20.1 1.7 %copy-done.2 = bf16[3,1536,256]{2,1,0:T(8,128)(2,1)S(1)} copy-done((bf16[3,1536,256]{2,1,0:T(8,128)(2,1)S(1)}, bf16[3,1536,256]{2,1,0:T(8,128)(2,1)}, u32[]{:S(2)}) %copy-start.2) | copy-done | bytes 2359320
  21.7 0.9 %copy-done.3 = bf16[8,2,64,128]{3,2,1,0:T(8,128)(2,1)S(1)} copy-done((bf16[8,2,64,128]{3,2,1,0:T(8,128)(2,1)S(1)}, bf16[8,2,64,128]{3,2,1,0:T(8,128)(2,1)}, u32[]{:S(2)}) %copy-start.3) | copy-done | bytes 262168
  22.7 0.9 %copy-done.5 = bf16[8,64,128]{2,1,0:T(8,128)(2,1)S(1)} copy-done((bf16[8,64,128]{2,1,0:T(8,128)(2,1)S(1)}, bf16[8,64,128]{2,1,0:T(8,128)(2,1)}, u32[]{:S(2)}) %copy-start.5) | copy-done | bytes 131096
  23.6 0.9 %copy-done.7 = bf16[8,64,128]{2,1,0:T(8,128)(2,1)S(1)} copy-done((bf16[8,64,128]{2,1,0:T(8,128)(2,1)S(1)}, bf16[8,64,128]{2,1,0:T(8,128)(2,1)}, u32[]{:S(2)}) %copy-start.7) | copy-done | bytes 131096
  24.5 1.0 %copy-done.8 = bf16[2,2,2,128,256]{4,3,2,1,0:T(8,128)(2,1)S(1)} copy-done((bf16[2,2,2,128,256]{4,3,2,1,0:T(8,128)(2,1)S(1)}, bf16[2,2,2,128,256]{4,3,2,1,0:T(8,128)(2,1)}, u32[]{:S(2)}) %copy-start.8) | copy-done | bytes 524312
  25.5 2.9 %entry.1 = (bf16[8,2,64,128]{3,2,1,0:T(8,128)(2,1)S(1)}, bf16[4,32,256]{2,1,0:T(8,128)(2,1)S(1)}) custom-call(bf16[8,2,64,128]{3,2,1,0:T(8,128)(2,1)S(1)} %copy-done.3, bf16[8,64,128]{2,1,0:T(8,128)(2,1)S(1)} %copy-done.7, bf16[8,64,128]{2,1,0:T(8,128)(2,1)S(1)} %copy-done.5, bf16[4,64,128]{2,1,0:T(8,128)(2,1)} %collective-permute-done.2.x1, ...), custom_call_target="tpu_custom_call" | custom-call | flops 1300000000 | bytes 4194304 | tf_op jit(solution)/shard_map/entry/pallas_call | solution.py:213
  28.5 3.7 %collective-permute-start.5 = (bf16[4,32,256]{2,1,0:T(8,128)(2,1)S(1)}, bf16[4,32,256]{2,1,0:T(8,128)(2,1)S(1)}, u32[]{:S(2)}, u32[]{:S(2)}) collective-permute-start(bf16[4,32,256]{2,1,0:T(8,128)(2,1)S(1)} %get-tuple-element.7.own), channel_id=1, source_target_pairs={{0,31},{1,2},{2,1},{3,4},{4,3},{5,6},{6,5},{7,8},{8,7},{9,10},{10,... | collective-permute-start | bytes 196616 | tf_op jit(solution)/shard_map/ppermute | solution.py:243
  32.2 1.8 %collective-permute-start.13 = (bf16[2,64,128]{2,1,0:T(8,128)(2,1)S(1)}, bf16[2,64,128]{2,1,0:T(8,128)(2,1)S(1)}, u32[]{:S(2)}, u32[]{:S(2)}) collective-permute-start(bf16[2,64,128]{2,1,0:T(8,128)(2,1)S(1)} %get-tuple-element.11), channel_id=1, source_target_pairs={{0,224},{32,64},{64,32},{96,128},{128,96},{160,192},{192,160},{224... | collective-permute-start | bytes 98312 | tf_op jit(solution)/shard_map/ppermute | solution.py:248
  34.0 2.2 %collective-permute-done.5.y2 = bf16[4,32,256]{2,1,0:T(8,128)(2,1)S(1)} collective-permute-done((bf16[4,32,256]{2,1,0:T(8,128)(2,1)S(1)}, bf16[4,32,256]{2,1,0:T(8,128)(2,1)S(1)}, u32[]{:S(2)}, u32[]{:S(2)}) %collective-permute-start.5) | collective-permute-done | bytes 65568 | tf_op jit(solution)/shard_map/ppermute | solution.py:243
  36.1 0.3 collective-permute-done.4.y1
  36.6 1.4 %collective-permute-start.7 = (bf16[3,3,32,256]{3,2,1,0:T(8,128)(2,1)S(1)}, bf16[3,3,32,256]{3,2,1,0:T(8,128)(2,1)S(1)}, u32[]{:S(2)}, u32[]{:S(2)}) collective-permute-start(bf16[3,3,32,256]{3,2,1,0:T(8,128)(2,1)S(1)} %pad_maximum_fusion.3), channel_id=1, source_target_pairs={{0,224},{32,64},{64,32},{96,128},{128,96},{160,192},{192,160},{224... | collective-permute-start | bytes 442376 | tf_op jit(solution)/shard_map/ppermute | solution.py:248
  38.1 4.4 %collective-permute-done.7.x2 = bf16[3,3,32,256]{3,2,1,0:T(8,128)(2,1)S(1)} collective-permute-done((bf16[3,3,32,256]{3,2,1,0:T(8,128)(2,1)S(1)}, bf16[3,3,32,256]{3,2,1,0:T(8,128)(2,1)S(1)}, u32[]{:S(2)}, u32[]{:S(2)}) %collective-permute-start.7) | collective-permute-done | bytes 147488 | tf_op jit(solution)/shard_map/ppermute | solution.py:248
  42.5 1.1 %first.1.own = bf16[8,32,256]{2,1,0:T(8,128)(2,1)S(1)} custom-call(bf16[4,32,256]{2,1,0:T(8,128)(2,1)S(1)} %get-tuple-element.7.own, bf16[4,32,256]{2,1,0:T(8,128)(2,1)S(1)} %collective-permute-done.4.y1, bf16[4,32,256]{2,1,0:T(8,128)(2,1)S(1)} %collective-permute-done.5.y2, bf16[3,3,32,256]{3,2,1,0:T(8,128)(2,1)S(1)} %collective-permute-done.6.x1, ...), custom_call_target="tpu_custom_call" | custom-call | flops 1000000000 | bytes 4194304 | tf_op jit(solution)/shard_map/first/pallas_call | solution.py:213
  43.6 3.4 %collective-permute-start.9 = (bf16[8,32,256]{2,1,0:T(8,128)(2,1)S(1)}, bf16[8,32,256]{2,1,0:T(8,128)(2,1)S(1)}, u32[]{:S(2)}, u32[]{:S(2)}) collective-permute-start(bf16[8,32,256]{2,1,0:T(8,128)(2,1)S(1)} %first.1.own), channel_id=1, source_target_pairs={{0,31},{1,2},{2,1},{3,4},{4,3},{5,6},{6,5},{7,8},{8,7},{9,10},{10,... | collective-permute-start | bytes 393224 | tf_op jit(solution)/shard_map/ppermute | solution.py:243
  47.1 2.1 %collective-permute-start.14 = (bf16[10,64,128]{2,1,0:T(8,128)(2,1)S(1)}, bf16[10,64,128]{2,1,0:T(8,128)(2,1)S(1)}, u32[]{:S(2)}, u32[]{:S(2)}) collective-permute-start(bf16[10,64,128]{2,1,0:T(8,128)(2,1)S(1)} %pad_maximum_fusion), channel_id=1, source_target_pairs={{0,1},{1,0},{2,3},{3,2},{4,5},{5,4},{6,7},{7,6},{8,9},{9,8},{10,11... | collective-permute-start | bytes 491528 | tf_op jit(solution)/shard_map/ppermute | solution.py:243
  49.2 2.1 %collective-permute-start.15 = (bf16[10,64,128]{2,1,0:T(8,128)(2,1)S(1)}, bf16[10,64,128]{2,1,0:T(8,128)(2,1)S(1)}, u32[]{:S(2)}, u32[]{:S(2)}) collective-permute-start(bf16[10,64,128]{2,1,0:T(8,128)(2,1)S(1)} %pad_maximum_fusion.1), channel_id=1, source_target_pairs={{0,31},{1,2},{2,1},{3,4},{4,3},{5,6},{6,5},{7,8},{8,7},{9,10},{10,... | collective-permute-start | bytes 491528 | tf_op jit(solution)/shard_map/ppermute | solution.py:243
  51.3 0.7 %collective-permute-done.9.y2 = bf16[8,32,256]{2,1,0:T(8,128)(2,1)S(1)} collective-permute-done((bf16[8,32,256]{2,1,0:T(8,128)(2,1)S(1)}, bf16[8,32,256]{2,1,0:T(8,128)(2,1)S(1)}, u32[]{:S(2)}, u32[]{:S(2)}) %collective-permute-start.9) | collective-permute-done | bytes 131104 | tf_op jit(solution)/shard_map/ppermute | solution.py:243
  52.0 1.5 %collective-permute-done.8.y1 = bf16[8,32,256]{2,1,0:T(8,128)(2,1)S(1)} collective-permute-done((bf16[8,32,256]{2,1,0:T(8,128)(2,1)S(1)}, bf16[8,32,256]{2,1,0:T(8,128)(2,1)S(1)}, u32[]{:S(2)}, u32[]{:S(2)}) %collective-permute-start.8) | collective-permute-done | bytes 131104 | tf_op jit(solution)/shard_map/ppermute | solution.py:243
  53.5 0.9 %second.1.own = bf16[6,32,256]{2,1,0:T(8,128)(2,1)S(1)} custom-call(bf16[8,32,256]{2,1,0:T(8,128)(2,1)S(1)} %first.1.own, bf16[8,32,256]{2,1,0:T(8,128)(2,1)S(1)} %collective-permute-done.8.y1, bf16[8,32,256]{2,1,0:T(8,128)(2,1)S(1)} %collective-permute-done.9.y2, bf16[3,2304,256]{2,1,0:T(8,128)(2,1)S(1)} %bitcast.33), custom_call_target="tpu_custom_call" | custom-call | flops 700000000 | bytes 4194304 | tf_op jit(solution)/shard_map/second/pallas_call | solution.py:213
  54.4 2.3 %collective-permute-start.11 = (bf16[6,32,256]{2,1,0:T(8,128)(2,1)S(1)}, bf16[6,32,256]{2,1,0:T(8,128)(2,1)S(1)}, u32[]{:S(2)}, u32[]{:S(2)}) collective-permute-start(bf16[6,32,256]{2,1,0:T(8,128)(2,1)S(1)} %second.1.own), channel_id=1, source_target_pairs={{0,31},{1,2},{2,1},{3,4},{4,3},{5,6},{6,5},{7,8},{8,7},{9,10},{10,... | collective-permute-start | bytes 294920 | tf_op jit(solution)/shard_map/ppermute | solution.py:243
  56.7 2.7 %fusion.2.weight = bf16[3,3072,256]{2,1,0:T(8,128)(2,1)S(1)} fusion(bf16[3,2304,128]{2,1,0:T(8,128)(2,1)S(1)} %bitcast.34), kind=kLoop, calls=%fused_computation.4 | loop fusion | flops 18874368 | bytes 6488064 | tf_op jit(solution)/shard_map/concatenate | solution.py:230
  59.4 3.2 %collective-permute-done.11.y2 = bf16[6,32,256]{2,1,0:T(8,128)(2,1)S(1)} collective-permute-done((bf16[6,32,256]{2,1,0:T(8,128)(2,1)S(1)}, bf16[6,32,256]{2,1,0:T(8,128)(2,1)S(1)}, u32[]{:S(2)}, u32[]{:S(2)}) %collective-permute-start.11) | collective-permute-done | bytes 98336 | tf_op jit(solution)/shard_map/ppermute | solution.py:243
  62.6 4.7 %decode.1 = bf16[8,2,64,128]{3,2,1,0:T(8,128)(2,1)} custom-call(bf16[6,32,256]{2,1,0:T(8,128)(2,1)S(1)} %second.1.own, bf16[6,32,256]{2,1,0:T(8,128)(2,1)S(1)} %collective-permute-done.10.y1, bf16[6,32,256]{2,1,0:T(8,128)(2,1)S(1)} %collective-permute-done.11.y2, bf16[8,2,64,128]{3,2,1,0:T(8,128)(2,1)S(1)} %get-tuple-element.8.encoded, ...), custom_call_target="tpu_custom_call" | custom-call | flops 2700000000 | bytes 4194304 | tf_op jit(solution)/shard_map/decode/pallas_call | solution.py:213
  (46 shorter events, 0.4 us)
Async XLA Ops:
  1.0 10.2 %collective-permute-start.1 = (bf16[8,64,128]{2,1,0:T(8,128)(2,1)S(1)}, bf16[8,64,128]{2,1,0:T(8,128)(2,1)S(1)}, u32[]{:S(2)}, u32[]{:S(2)}) collective-permute-start(bf16[8,64,128]{2,1,0:T(8,128)(2,1)S(1)} %get-tuple-element.17), channel_id=1, source_target_pairs={{0,31},{1,2},{2,1},{3,4},{4,3},{5,6},{6,5},{7,8},{8,7},{9,10},{10,... | collective-permute-start | bytes 393224 | tf_op jit(solution)/shard_map/ppermute | solution.py:243
  7.6 5.0 %collective-permute-start = (bf16[8,64,128]{2,1,0:T(8,128)(2,1)S(1)}, bf16[8,64,128]{2,1,0:T(8,128)(2,1)S(1)}, u32[]{:S(2)}, u32[]{:S(2)}) collective-permute-start(bf16[8,64,128]{2,1,0:T(8,128)(2,1)S(1)} %get-tuple-element.18), channel_id=1, source_target_pairs={{0,1},{1,0},{2,3},{3,2},{4,5},{5,4},{6,7},{7,6},{8,9},{9,8},{10,11... | collective-permute-start | bytes 393224 | tf_op jit(solution)/shard_map/ppermute | solution.py:243
  11.1 5.7 %copy-start.4 = (bf16[8,64,128]{2,1,0:T(8,128)(2,1)}, bf16[8,64,128]{2,1,0:T(8,128)(2,1)S(1)}, u32[]{:S(2)}) copy-start(bf16[8,64,128]{2,1,0:T(8,128)(2,1)S(1)} %collective-permute-done.1.y2) | copy-start | bytes 393220
  12.6 4.2 %copy-start.6 = (bf16[8,64,128]{2,1,0:T(8,128)(2,1)}, bf16[8,64,128]{2,1,0:T(8,128)(2,1)S(1)}, u32[]{:S(2)}) copy-start(bf16[8,64,128]{2,1,0:T(8,128)(2,1)S(1)} %collective-permute-done.y1) | copy-start | bytes 393220
  13.3 6.7 %collective-permute-start.2 = (bf16[4,64,128]{2,1,0:T(8,128)(2,1)}, bf16[4,64,128]{2,1,0:T(8,128)(2,1)}, u32[]{:S(2)}, u32[]{:S(2)}) collective-permute-start(bf16[4,64,128]{2,1,0:T(8,128)(2,1)} %pad_maximum_fusion.4), channel_id=1, source_target_pairs={{0,32},{32,0},{64,96},{96,64},{128,160},{160,128},{192,224},{224,1... | collective-permute-start | bytes 196616 | tf_op jit(solution)/shard_map/ppermute | solution.py:248
  13.9 6.1 %collective-permute-start.3 = (bf16[4,64,128]{2,1,0:T(8,128)(2,1)}, bf16[4,64,128]{2,1,0:T(8,128)(2,1)}, u32[]{:S(2)}, u32[]{:S(2)}) collective-permute-start(bf16[4,64,128]{2,1,0:T(8,128)(2,1)} %pad_maximum_fusion.5), channel_id=1, source_target_pairs={{0,224},{32,64},{64,32},{96,128},{128,96},{160,192},{192,160},{224... | collective-permute-start | bytes 196616 | tf_op jit(solution)/shard_map/ppermute | solution.py:248
  16.8 25.7 %copy-start = (bf16[3,3,3,256,256]{4,3,2,1,0:T(8,128)(2,1)S(1)}, bf16[3,3,3,256,256]{4,3,2,1,0:T(8,128)(2,1)}, u32[]{:S(2)}) copy-start(bf16[3,3,3,256,256]{4,3,2,1,0:T(8,128)(2,1)} %param.10) | copy-start | bytes 10616836
  20.1 1.7 %copy-start.2 = (bf16[3,1536,256]{2,1,0:T(8,128)(2,1)S(1)}, bf16[3,1536,256]{2,1,0:T(8,128)(2,1)}, u32[]{:S(2)}) copy-start(bf16[3,1536,256]{2,1,0:T(8,128)(2,1)} %fusion.5.weight) | copy-start | bytes 7077892
  21.7 0.9 %copy-start.3 = (bf16[8,2,64,128]{3,2,1,0:T(8,128)(2,1)S(1)}, bf16[8,2,64,128]{3,2,1,0:T(8,128)(2,1)}, u32[]{:S(2)}) copy-start(bf16[8,2,64,128]{3,2,1,0:T(8,128)(2,1)} %own.1) | copy-start | bytes 786436
  22.7 0.9 %copy-start.5 = (bf16[8,64,128]{2,1,0:T(8,128)(2,1)S(1)}, bf16[8,64,128]{2,1,0:T(8,128)(2,1)}, u32[]{:S(2)}) copy-start(bf16[8,64,128]{2,1,0:T(8,128)(2,1)} %copy-done.4) | copy-start | bytes 393220
  23.6 0.9 %copy-start.7 = (bf16[8,64,128]{2,1,0:T(8,128)(2,1)S(1)}, bf16[8,64,128]{2,1,0:T(8,128)(2,1)}, u32[]{:S(2)}) copy-start(bf16[8,64,128]{2,1,0:T(8,128)(2,1)} %copy-done.6) | copy-start | bytes 393220
  24.5 1.0 %copy-start.8 = (bf16[2,2,2,128,256]{4,3,2,1,0:T(8,128)(2,1)S(1)}, bf16[2,2,2,128,256]{4,3,2,1,0:T(8,128)(2,1)}, u32[]{:S(2)}) copy-start(bf16[2,2,2,128,256]{4,3,2,1,0:T(8,128)(2,1)} %down.1) | copy-start | bytes 1572868
  28.4 25.0 %copy-start.1 = (bf16[3,3,3,256,256]{4,3,2,1,0:T(8,128)(2,1)S(1)}, bf16[3,3,3,256,256]{4,3,2,1,0:T(8,128)(2,1)}, u32[]{:S(2)}) copy-start(bf16[3,3,3,256,256]{4,3,2,1,0:T(8,128)(2,1)} %param.11) | copy-start | bytes 10616836
  28.5 7.7 %collective-permute-start.5 = (bf16[4,32,256]{2,1,0:T(8,128)(2,1)S(1)}, bf16[4,32,256]{2,1,0:T(8,128)(2,1)S(1)}, u32[]{:S(2)}, u32[]{:S(2)}) collective-permute-start(bf16[4,32,256]{2,1,0:T(8,128)(2,1)S(1)} %get-tuple-element.7.own), channel_id=1, source_target_pairs={{0,31},{1,2},{2,1},{3,4},{4,3},{5,6},{6,5},{7,8},{8,7},{9,10},{10,... | collective-permute-start | bytes 196616 | tf_op jit(solution)/shard_map/ppermute | solution.py:243
  32.1 4.3 %collective-permute-start.4 = (bf16[4,32,256]{2,1,0:T(8,128)(2,1)S(1)}, bf16[4,32,256]{2,1,0:T(8,128)(2,1)S(1)}, u32[]{:S(2)}, u32[]{:S(2)}) collective-permute-start(bf16[4,32,256]{2,1,0:T(8,128)(2,1)S(1)} %get-tuple-element.7.own), channel_id=1, source_target_pairs={{0,1},{1,0},{2,3},{3,2},{4,5},{5,4},{6,7},{7,6},{8,9},{9,8},{10,11... | collective-permute-start | bytes 196616 | tf_op jit(solution)/shard_map/ppermute | solution.py:243
  32.2 5.9 %collective-permute-start.13 = (bf16[2,64,128]{2,1,0:T(8,128)(2,1)S(1)}, bf16[2,64,128]{2,1,0:T(8,128)(2,1)S(1)}, u32[]{:S(2)}, u32[]{:S(2)}) collective-permute-start(bf16[2,64,128]{2,1,0:T(8,128)(2,1)S(1)} %get-tuple-element.11), channel_id=1, source_target_pairs={{0,224},{32,64},{64,32},{96,128},{128,96},{160,192},{192,160},{224... | collective-permute-start | bytes 98312 | tf_op jit(solution)/shard_map/ppermute | solution.py:248
  34.0 4.1 %collective-permute-start.12 = (bf16[2,64,128]{2,1,0:T(8,128)(2,1)S(1)}, bf16[2,64,128]{2,1,0:T(8,128)(2,1)S(1)}, u32[]{:S(2)}, u32[]{:S(2)}) collective-permute-start(bf16[2,64,128]{2,1,0:T(8,128)(2,1)S(1)} %get-tuple-element.12), channel_id=1, source_target_pairs={{0,32},{32,0},{64,96},{96,64},{128,160},{160,128},{192,224},{224,1... | collective-permute-start | bytes 98312 | tf_op jit(solution)/shard_map/ppermute | solution.py:248
  36.5 20.2 %copy-start.10 = (bf16[3,3,3,256,128]{4,3,2,1,0:T(8,128)(2,1)S(1)}, bf16[3,3,3,256,128]{4,3,2,1,0:T(8,128)(2,1)}, u32[]{:S(2)}) copy-start(bf16[3,3,3,256,128]{4,3,2,1,0:T(8,128)(2,1)} %param.13) | copy-start | bytes 5308420
  36.5 1.6 %collective-permute-start.6 = (bf16[3,3,32,256]{3,2,1,0:T(8,128)(2,1)S(1)}, bf16[3,3,32,256]{3,2,1,0:T(8,128)(2,1)S(1)}, u32[]{:S(2)}, u32[]{:S(2)}) collective-permute-start(bf16[3,3,32,256]{3,2,1,0:T(8,128)(2,1)S(1)} %pad_maximum_fusion.2), channel_id=1, source_target_pairs={{0,32},{32,0},{64,96},{96,64},{128,160},{160,128},{192,224},{224,1... | collective-permute-start | bytes 442376 | tf_op jit(solution)/shard_map/ppermute | solution.py:248
  36.6 5.9 %collective-permute-start.7 = (bf16[3,3,32,256]{3,2,1,0:T(8,128)(2,1)S(1)}, bf16[3,3,32,256]{3,2,1,0:T(8,128)(2,1)S(1)}, u32[]{:S(2)}, u32[]{:S(2)}) collective-permute-start(bf16[3,3,32,256]{3,2,1,0:T(8,128)(2,1)S(1)} %pad_maximum_fusion.3), channel_id=1, source_target_pairs={{0,224},{32,64},{64,32},{96,128},{128,96},{160,192},{192,160},{224... | collective-permute-start | bytes 442376 | tf_op jit(solution)/shard_map/ppermute | solution.py:248
  43.6 8.4 %collective-permute-start.9 = (bf16[8,32,256]{2,1,0:T(8,128)(2,1)S(1)}, bf16[8,32,256]{2,1,0:T(8,128)(2,1)S(1)}, u32[]{:S(2)}, u32[]{:S(2)}) collective-permute-start(bf16[8,32,256]{2,1,0:T(8,128)(2,1)S(1)} %first.1.own), channel_id=1, source_target_pairs={{0,31},{1,2},{2,1},{3,4},{4,3},{5,6},{6,5},{7,8},{8,7},{9,10},{10,... | collective-permute-start | bytes 393224 | tf_op jit(solution)/shard_map/ppermute | solution.py:243
  47.0 6.4 %collective-permute-start.8 = (bf16[8,32,256]{2,1,0:T(8,128)(2,1)S(1)}, bf16[8,32,256]{2,1,0:T(8,128)(2,1)S(1)}, u32[]{:S(2)}, u32[]{:S(2)}) collective-permute-start(bf16[8,32,256]{2,1,0:T(8,128)(2,1)S(1)} %first.1.own), channel_id=1, source_target_pairs={{0,1},{1,0},{2,3},{3,2},{4,5},{5,4},{6,7},{7,6},{8,9},{9,8},{10,11... | collective-permute-start | bytes 393224 | tf_op jit(solution)/shard_map/ppermute | solution.py:243
  47.1 12.3 %collective-permute-start.14 = (bf16[10,64,128]{2,1,0:T(8,128)(2,1)S(1)}, bf16[10,64,128]{2,1,0:T(8,128)(2,1)S(1)}, u32[]{:S(2)}, u32[]{:S(2)}) collective-permute-start(bf16[10,64,128]{2,1,0:T(8,128)(2,1)S(1)} %pad_maximum_fusion), channel_id=1, source_target_pairs={{0,1},{1,0},{2,3},{3,2},{4,5},{5,4},{6,7},{7,6},{8,9},{9,8},{10,11... | collective-permute-start | bytes 491528 | tf_op jit(solution)/shard_map/ppermute | solution.py:243
  49.2 10.2 %collective-permute-start.15 = (bf16[10,64,128]{2,1,0:T(8,128)(2,1)S(1)}, bf16[10,64,128]{2,1,0:T(8,128)(2,1)S(1)}, u32[]{:S(2)}, u32[]{:S(2)}) collective-permute-start(bf16[10,64,128]{2,1,0:T(8,128)(2,1)S(1)} %pad_maximum_fusion.1), channel_id=1, source_target_pairs={{0,31},{1,2},{2,1},{3,4},{4,3},{5,6},{6,5},{7,8},{8,7},{9,10},{10,... | collective-permute-start | bytes 491528 | tf_op jit(solution)/shard_map/ppermute | solution.py:243
  53.5 9.1 %copy-start.9 = (bf16[2,2,2,256,128]{4,3,2,1,0:T(8,128)(2,1)S(1)}, bf16[2,2,2,256,128]{4,3,2,1,0:T(8,128)(2,1)}, u32[]{:S(2)}) copy-start(bf16[2,2,2,256,128]{4,3,2,1,0:T(8,128)(2,1)} %up.1) | copy-start | bytes 1572868
  54.4 8.2 %collective-permute-start.11 = (bf16[6,32,256]{2,1,0:T(8,128)(2,1)S(1)}, bf16[6,32,256]{2,1,0:T(8,128)(2,1)S(1)}, u32[]{:S(2)}, u32[]{:S(2)}) collective-permute-start(bf16[6,32,256]{2,1,0:T(8,128)(2,1)S(1)} %second.1.own), channel_id=1, source_target_pairs={{0,31},{1,2},{2,1},{3,4},{4,3},{5,6},{6,5},{7,8},{8,7},{9,10},{10,... | collective-permute-start | bytes 294920 | tf_op jit(solution)/shard_map/ppermute | solution.py:243
  56.7 5.9 %collective-permute-start.10 = (bf16[6,32,256]{2,1,0:T(8,128)(2,1)S(1)}, bf16[6,32,256]{2,1,0:T(8,128)(2,1)S(1)}, u32[]{:S(2)}, u32[]{:S(2)}) collective-permute-start(bf16[6,32,256]{2,1,0:T(8,128)(2,1)S(1)} %second.1.own), channel_id=1, source_target_pairs={{0,1},{1,0},{2,3},{3,2},{4,5},{5,4},{6,7},{7,6},{8,9},{9,8},{10,11... | collective-permute-start | bytes 294920 | tf_op jit(solution)/shard_map/ppermute | solution.py:243

commit v2 on v1

v2 whole, which is shorter than its diff:
```python
import jax
import jax.numpy as jnp
from jax import lax
from jax.experimental import pallas as pl
from jax.experimental.pallas import tpu as pltpu
from jax.sharding import PartitionSpec as P

BF = jnp.bfloat16
F32 = jnp.float32
LIMIT = 20 * 1024 * 1024


def leaky_unit(values):
    return jnp.where(values > 0, values, 0.1 * values)


def inside(index, count):
    return (index >= 0) & (index < count)


def depth_taps(cells):
    depth = cells.shape[0]
    at = lax.broadcasted_iota(jnp.int32, cells.shape, 0)
    before = jnp.where(at == 0, 0.0, pltpu.roll(cells, 1, axis=0))
    after = jnp.where(at == depth - 1, 0.0, pltpu.roll(cells, depth - 1, axis=0))
    return before.astype(BF), cells.astype(BF), after.astype(BF)


def own_columns(target, part):
    for off in range(3):
        target[off, :384, :128] = part(off, 1)
        target[off, :384, 128:] = part(off, 0)
        target[off, 384:, :128] = part(off, 2)
        target[off, 384:, 128:] = part(off, 1)


def put_taps(target, row, lane, cells):
    for tap, part in enumerate(depth_taps(cells)):
        target[row, :, lane + tap * 128 : lane + tap * 128 + 128] = part


def side_columns(total, rows, low, high, part):
    extra = low.shape[0] - 8
    for off in range(3):
        if extra == 2:
            source, into = slice(off, off + 8), slice(0, 8)
        else:
            source = slice(max(0, off - 1), 8 + min(0, off - 1))
            into = slice(max(0, 1 - off), 8 - max(0, off - 1))
        count = (into.stop - into.start) * 64
        for half, cells in enumerate((low, high)):
            lanes = slice(half * 128, half * 128 + 128)
            total[into, :, lanes] += jnp.dot(
                cells[source].reshape(count, 384), part(off, 2 * half), preferred_element_type=F32
            ).reshape(count // 64, 64, 128)


def entry_own_kernel(own, weight, total, stacked, wide):
    own_columns(wide, lambda off, col: weight[off, col])

    def one_row(i, carry):
        for col in range(2):
            put_taps(stacked, i, col * 384, own[i, col].astype(F32))
        return carry

    lax.fori_loop(0, 8, one_row, 0)
    total[...] = jnp.dot(
        stacked[...].reshape(512, 768), wide[1], preferred_element_type=F32
    ).reshape(8, 64, 256)
    total[1:8] += jnp.dot(
        stacked[0:7].reshape(448, 768), wide[0], preferred_element_type=F32
    ).reshape(7, 64, 256)
    total[0:7] += jnp.dot(
        stacked[1:8].reshape(448, 768), wide[2], preferred_element_type=F32
    ).reshape(7, 64, 256)


def entry_side_kernel(y1, y2, weight, before, total, low, high):
    gy = lax.axis_index("gy")
    ny = lax.axis_size("gy")
    odd_y = lax.rem(gy, 2) == 1
    total[...] = before[...]

    def one_row(i, carry):
        first, second = y1[i].astype(F32), y2[i].astype(F32)
        put_taps(low, i, 0, jnp.where(gy > 0, jnp.where(odd_y, first, second), 0.0))
        put_taps(high, i, 0, jnp.where(gy < ny - 1, jnp.where(odd_y, second, first), 0.0))
        return carry

    lax.fori_loop(0, 8, one_row, 0)
    side_columns(total, 8, low, high, lambda off, col: weight[off, col])


def entry_last_kernel(x1, x2, weight, down, before, encoded, coarse, stacked, fine):
    gx, gy = lax.axis_index("gx"), lax.axis_index("gy")
    nx, ny = lax.axis_size("gx"), lax.axis_size("gy")
    odd_x = lax.rem(gx, 2) == 1
    for col in range(4):
        first, second = x1[col].astype(F32), x2[col].astype(F32)
        low = jnp.where(odd_x, first, second)
        high = jnp.where(odd_x, second, first)
        ok = inside(gy * 2 - 1 + col, ny * 2)
        put_taps(stacked, 0, col * 384, jnp.where(ok & (gx > 0), low, 0.0))
        put_taps(stacked, 1, col * 384, jnp.where(ok & (gx < nx - 1), high, 0.0))

    def finish(row, values):
        result = leaky_unit(values).astype(BF)
        for b in range(2):
            half = result[..., b * 128 : b * 128 + 128]
            encoded[row, b] = half
            fine[row, b] = half.astype(F32)

    def middle(row, carry):
        finish(row, before[row])
        return carry

    lax.fori_loop(1, 7, middle, 0)
    for side, (row, off) in enumerate(((0, 0), (7, 2))):
        extra = [
            jnp.dot(
                stacked[side, :, b * 384 : b * 384 + 1152],
                weight[off].reshape(1152, 128),
                preferred_element_type=F32,
            )
            for b in range(2)
        ]
        finish(row, before[row] + jnp.concatenate(extra, axis=1))
    small = jnp.zeros((128, 256), F32)
    for a in range(2):
        for d in range(2):
            cells = jnp.concatenate(
                [
                    jnp.concatenate(
                        [fine[2 * i + a, b, pl.ds(d, 32, stride=2), :] for b in range(2)], axis=1
                    )
                    for i in range(4)
                ],
                axis=0,
            ).astype(BF)
            small = small + jnp.dot(
                cells, down[a, :, d].reshape(256, 256), preferred_element_type=F32
            )
    coarse[...] = leaky_unit(small).astype(BF).reshape(4, 32, 256)


def fill_deep(rows, first_row, planes, stacked):
    gy = lax.axis_index("gy")
    nx, ny = lax.axis_size("gx"), lax.axis_size("gy")

    for row in range(rows):
        ok_row = inside(first_row + row, nx * 4)
        for plane, cells in enumerate(planes(row)):
            ok = ok_row & inside(gy - 1 + plane, ny)
            for tap, part in enumerate(depth_taps(jnp.where(ok, cells, 0.0))):
                lane = (plane * 3 + tap) * 256
                stacked[row, :, lane : lane + 256] = part


def deep_conv(rows, stacked, weight, out):
    total = jnp.zeros((rows * 32, 256), F32)
    for off in range(3):
        total = total + jnp.dot(
            stacked[off : off + rows].reshape(rows * 32, 2304),
            weight[off],
            preferred_element_type=F32,
        )
    out[...] = leaky_unit(total).astype(BF).reshape(rows, 32, 256)


def first_kernel(own, y1, y2, x1, x2, weight, out, stacked):
    gx, gy = lax.axis_index("gx"), lax.axis_index("gy")
    odd_x, odd_y = lax.rem(gx, 2) == 1, lax.rem(gy, 2) == 1

    def planes(row):
        if 3 <= row < 7:
            first, second = y1[row - 3].astype(F32), y2[row - 3].astype(F32)
            return (
                jnp.where(odd_y, first, second),
                own[row - 3].astype(F32),
                jnp.where(odd_y, second, first),
            )
        result = []
        for plane in range(3):
            at = row if row < 3 else row - 7
            first, second = x1[at, plane].astype(F32), x2[at, plane].astype(F32)
            if row < 3:
                result.append(jnp.where(odd_x, first, second))
            else:
                result.append(jnp.where(odd_x, second, first))
        return result

    fill_deep(10, gx * 4 - 3, planes, stacked)
    deep_conv(8, stacked, weight, out)


def second_kernel(own, y1, y2, weight, out, stacked):
    gx, gy = lax.axis_index("gx"), lax.axis_index("gy")
    odd_y = lax.rem(gy, 2) == 1

    def planes(row):
        first, second = y1[row].astype(F32), y2[row].astype(F32)
        return (
            jnp.where(odd_y, first, second),
            own[row].astype(F32),
            jnp.where(odd_y, second, first),
        )

    fill_deep(8, gx * 4 - 2, planes, stacked)
    deep_conv(6, stacked, weight, out)


def lift(cells, up, upward, columns):
    for col, b in columns:
        for a in range(2):
            for d in range(2):
                part = leaky_unit(
                    jnp.dot(cells, up[a, b, d], preferred_element_type=F32)
                ).reshape(6, 32, 128)
                for i in range(6):
                    row = 2 * i + a - 1
                    if 0 <= row < 10:
                        upward[row, col, pl.ds(d, 32, stride=2), :] = part[i]


def decode_own_kernel(
    own, encoded, ex1, ex2, ey1, ey2, up, weight, total, stacked, low, high, wide, upward
):
    gx, gy = lax.axis_index("gx"), lax.axis_index("gy")
    nx, ny = lax.axis_size("gx"), lax.axis_size("gy")
    odd_x, odd_y = lax.rem(gx, 2) == 1, lax.rem(gy, 2) == 1

    def weights(half):
        return lambda off, col: weight[off, col, :, half * 128 : half * 128 + 128].reshape(
            384, 128
        )

    own_columns(wide, weights(1))

    def side(row, carry):
        ok = inside(gx * 8 - 1 + row, nx * 8)
        first, second = ey1[row].astype(F32), ey2[row].astype(F32)
        put_taps(low, row, 0, jnp.where(ok & (gy > 0), jnp.where(odd_y, first, second), 0.0))
        put_taps(high, row, 0, jnp.where(ok & (gy < ny - 1), jnp.where(odd_y, second, first), 0.0))
        return carry

    lax.fori_loop(0, 10, side, 0)

    def center(row, carry):
        for col in range(2):
            put_taps(stacked, row + 1, col * 384, encoded[row, col].astype(F32))
        return carry

    lax.fori_loop(0, 8, center, 0)
    for col in range(2):
        first, second = ex1[col].astype(F32), ex2[col].astype(F32)
        lane = col * 384
        put_taps(stacked, 0, lane, jnp.where(gx > 0, jnp.where(odd_x, first, second), 0.0))
        put_taps(stacked, 9, lane, jnp.where(gx < nx - 1, jnp.where(odd_x, second, first), 0.0))

    def add_own(start):
        for off in range(3):
            part = jnp.dot(
                stacked[off : off + 8].reshape(512, 768), wide[off], preferred_element_type=F32
            ).reshape(8, 64, 256)
            if start and off == 0:
                total[...] = part
            else:
                total[...] += part

    add_own(True)
    side_columns(total, 10, low, high, weights(1))
    own_columns(wide, weights(0))
    lift(own[...].reshape(192, 256), up, upward, ((0, 0), (1, 1)))

    def lifted(row, carry):
        ok = inside(gx * 8 - 1 + row, nx * 8)
        for col in range(2):
            put_taps(stacked, row, col * 384, jnp.where(ok, upward[row, col], 0.0))
        return carry

    lax.fori_loop(0, 10, lifted, 0)
    add_own(False)


def decode_last_kernel(y1, y2, up, weight, before, decoded, low, high, upward, total):
    gx, gy = lax.axis_index("gx"), lax.axis_index("gy")
    nx, ny = lax.axis_size("gx"), lax.axis_size("gy")
    odd_y = lax.rem(gy, 2) == 1
    total[...] = before[...]
    first, second = y1[...].astype(F32), y2[...].astype(F32)
    below = jnp.where(odd_y, first, second).astype(BF).reshape(192, 256)
    above = jnp.where(odd_y, second, first).astype(BF).reshape(192, 256)
    lift(below, up, upward, ((0, 1),))
    lift(above, up, upward, ((1, 0),))

    def lifted(row, carry):
        ok = inside(gx * 8 - 1 + row, nx * 8)
        put_taps(low, row, 0, jnp.where(ok & (gy > 0), upward[row, 0], 0.0))
        put_taps(high, row, 0, jnp.where(ok & (gy < ny - 1), upward[row, 1], 0.0))
        return carry

    lax.fori_loop(0, 10, lifted, 0)
    side_columns(
        total, 10, low, high, lambda off, col: weight[off, col, :, :128].reshape(384, 128)
    )
    result = leaky_unit(total[...]).astype(BF)
    decoded[:, 0] = result[:, :, :128]
    decoded[:, 1] = result[:, :, 128:]


def call(kernel, outs, scratch, name, flops, *operands):
    vmem = pl.BlockSpec(memory_space=pltpu.VMEM)
    return pl.pallas_call(
        kernel,
        out_shape=[jax.ShapeDtypeStruct(shape, dtype) for shape, dtype in outs],
        in_specs=[vmem] * len(operands),
        out_specs=[vmem] * len(outs),
        scratch_shapes=[pltpu.VMEM(shape, dtype) for shape, dtype in scratch],
        compiler_params=pltpu.CompilerParams(vmem_limit_bytes=LIMIT),
        cost_estimate=pl.CostEstimate(flops=flops, bytes_accessed=1 << 20, transcendentals=0),
        name=name,
    )(*operands)


def swap_y(first, second):
    nx, ny = lax.axis_size("gx"), lax.axis_size("gy")
    near = [(i, i ^ 1) for i in range(ny)]
    far = []
    for x in range(nx):
        for y in range(ny):
            to = (x ^ 1) * ny + y if y in (0, ny - 1) else x * ny + ((y + 1) ^ 1) - 1
            far.append((x * ny + y, to))
    got = lax.ppermute(second, ("gx", "gy"), far)
    return lax.ppermute(first, "gy", near), got


def swap_x(first, second):
    nx, ny = lax.axis_size("gx"), lax.axis_size("gy")
    near = [(i, i ^ 1) for i in range(nx)]
    far = []
    for x in range(nx):
        for y in range(ny):
            to = x * ny + (y ^ 1) if x in (0, nx - 1) else (((x + 1) ^ 1) - 1) * ny + y
            far.append((x * ny + y, to))
    got = lax.ppermute(second, ("gx", "gy"), far)
    return lax.ppermute(first, "gx", near), got


def local(
    volume,
    weight_entry,
    weight_down,
    weight_deep_first,
    weight_deep_second,
    weight_upward,
    weight_decoder,
):
    odd_x = lax.rem(lax.axis_index("gx"), 2)
    odd_y = lax.rem(lax.axis_index("gy"), 2)

    def column(array, at):
        return lax.dynamic_index_in_dim(array, at, axis=1, keepdims=False)

    def rows(array, at, count):
        return lax.dynamic_slice_in_dim(array, at, count, axis=0)

    entry = weight_entry.reshape(3, 3, 384, 128)
    sums = ((8, 64, 256), F32)
    y1, y2 = swap_y(column(volume, 1 - odd_y), column(volume, odd_y))
    (total,) = call(
        entry_own_kernel,
        [sums],
        [((8, 64, 768), BF), ((3, 768, 256), BF)],
        "entry_own",
        2_000_000_000,
        volume,
        entry,
    )
    low = jnp.where(odd_y == 1, y1, y2)
    high = jnp.where(odd_y == 1, y2, y1)

    def edge(at):
        return jnp.concatenate(
            [rows(low, at, 1), rows(volume, at, 1)[0], rows(high, at, 1)], axis=0
        )

    x1, x2 = swap_x(edge(7 * (1 - odd_x)), edge(7 * odd_x))
    (total,) = call(
        entry_side_kernel,
        [sums],
        [((8, 64, 384), BF), ((8, 64, 384), BF)],
        "entry_side",
        1_000_000_000,
        y1,
        y2,
        entry,
        total,
    )
    encoded, coarse = call(
        entry_last_kernel,
        [((8, 2, 64, 128), BF), ((4, 32, 256), BF)],
        [((2, 64, 1536), BF), ((8, 2, 64, 128), F32)],
        "entry_last",
        1_000_000_000,
        x1,
        x2,
        entry,
        weight_down,
        total,
    )

    c1, c2 = swap_y(coarse, coarse)
    c_low = jnp.where(odd_y == 1, c1, c2)
    c_high = jnp.where(odd_y == 1, c2, c1)

    def coarse_edge(at):
        return jnp.stack([rows(c_low, at, 3), rows(coarse, at, 3), rows(c_high, at, 3)], axis=1)

    d1, d2 = swap_x(coarse_edge(1 - odd_x), coarse_edge(odd_x))
    e1, e2 = swap_x(rows(encoded, 7 * (1 - odd_x), 1)[0], rows(encoded, 7 * odd_x, 1)[0])
    (deep_one,) = call(
        first_kernel,
        [((8, 32, 256), BF)],
        [((10, 32, 2304), BF)],
        "first",
        1_000_000_000,
        coarse,
        c1,
        c2,
        d1,
        d2,
        weight_deep_first.reshape(3, 2304, 256),
    )
    f1, f2 = swap_y(deep_one, deep_one)

    e_low = jnp.where(odd_x == 1, e1, e2)
    e_high = jnp.where(odd_x == 1, e2, e1)

    def encoded_edge(at):
        return jnp.concatenate(
            [rows(e_low, at, 1), column(encoded, at), rows(e_high, at, 1)], axis=0
        )

    g1, g2 = swap_y(encoded_edge(1 - odd_y), encoded_edge(odd_y))
    (deep_two,) = call(
        second_kernel,
        [((6, 32, 256), BF)],
        [((8, 32, 2304), BF)],
        "second",
        700_000_000,
        deep_one,
        f1,
        f2,
        weight_deep_second.reshape(3, 2304, 256),
    )
    h1, h2 = swap_y(deep_two, deep_two)
    (total,) = call(
        decode_own_kernel,
        [sums],
        [
            ((10, 64, 768), BF),
            ((10, 64, 384), BF),
            ((10, 64, 384), BF),
            ((3, 768, 256), BF),
            ((10, 2, 64, 128), F32),
        ],
        "decode_own",
        3_000_000_000,
        deep_two,
        encoded,
        e1,
        e2,
        g1,
        g2,
        weight_upward,
        weight_decoder,
    )
    (decoded,) = call(
        decode_last_kernel,
        [((8, 2, 64, 128), BF)],
        [
            ((10, 64, 384), BF),
            ((10, 64, 384), BF),
            ((10, 2, 64, 128), F32),
            ((8, 64, 256), F32),
        ],
        "decode_last",
        1_000_000_000,
        h1,
        h2,
        weight_upward,
        weight_decoder,
        total,
    )
    return decoded


def solution(mesh):
    return jax.shard_map(
        local,
        mesh=mesh,
        in_specs=(P("gx", "gy", None, None), P(), P(), P(), P(), P(), P()),
        out_specs=P("gx", "gy", None, None),
        check_vma=False,
    )
```

time: 67.6 us -> 50.4 us (0.75)
  the two profiles are of different devices: /device:TPU:0 before, /device:TPU:128 now
where the time goes in v2:
time: 50.4 us; the launch traced here: 50.2 us
  waiting for transfers between devices  19.2 us (38%)
  starting transfers between devices  15.2 us (30%)
  Pallas kernels  11.3 us (22%)
  local copies, waits for them, and re-layouts  4.08 us (8%)
    pallas_call x7, Pallas kernels, call(): pl.pallas_call(kernel, out_shape=[jax.ShapeDtypeStruct(shape, dtype) for...  11.3 us
    ppermute x5, starting transfers between devices, swap_y(): got = lax.ppermute(second, ('gx', 'gy'), far)  9.26 us
    ppermute x5, waiting for transfers between devices, swap_y(): got = lax.ppermute(second, ('gx', 'gy'), far)  8.34 us
    ppermute x3, waiting for transfers between devices, swap_x(): got = lax.ppermute(second, ('gx', 'gy'), far)  6.45 us
    ppermute x5, waiting for transfers between devices, swap_y(): return (lax.ppermute(first, 'gy', near), got)  3.74 us
    ppermute x3, starting transfers between devices, swap_x(): return (lax.ppermute(first, 'gx', near), got)  2.78 us
    ppermute x5, starting transfers between devices, swap_y(): return (lax.ppermute(first, 'gy', near), got)  2.42 us
    unnamed x16, local copies, waits for them, and re-layouts  2.15 us
  transfers between devices with their start and end apart: 16, of which 9 were waited for; matrix products, arithmetic and copies ran while one was open for 2% of the time, Pallas kernels for 17%

profile of v2, /device:TPU:128, one launch (start us, length us, event | category | flops | bytes accessed | tf_op | source)
XLA Modules:
  0.0 50.2 jit_solution(3279707982357199564)
XLA Ops:
  0.0 1.0 %dynamic-slice_bitcast_fusion.3 = (bf16[8,64,128]{2,1,0:T(8,128)(2,1)S(1)}, bf16[8,64,128]{2,1,0:T(8,128)(2,1)S(1)}) fusion(bf16[8,2,64,128]{3,2,1,0:T(8,128)(2,1)} %own.1, s32[]{:T(128)S(6)} %select_n.72, s32[]{:T(128)S(6)} %select_n.73), kind=kLoop, calls=%fused_computation.7 | loop fusion | bytes 524296 | tf_op jit(solution)/shard_map/jit(dynamic_index_in_dim)/squeeze | solution.py:362
  1.0 1.7 %collective-permute-start = (bf16[8,64,128]{2,1,0:T(8,128)(2,1)S(1)}, bf16[8,64,128]{2,1,0:T(8,128)(2,1)S(1)}, u32[]{:S(2)}, u32[]{:S(2)}) collective-permute-start(bf16[8,64,128]{2,1,0:T(8,128)(2,1)S(1)} %get-tuple-element.17), channel_id=1, source_target_pairs={{0,1},{1,0},{2,3},{3,2},{4,5},{5,4},{6,7},{7,6},{8,9},{9,8},{10,11... | collective-permute-start | bytes 393224 | tf_op jit(solution)/shard_map/ppermute | solution.py:334
  2.7 1.7 %collective-permute-start.1 = (bf16[8,64,128]{2,1,0:T(8,128)(2,1)S(1)}, bf16[8,64,128]{2,1,0:T(8,128)(2,1)S(1)}, u32[]{:S(2)}, u32[]{:S(2)}) collective-permute-start(bf16[8,64,128]{2,1,0:T(8,128)(2,1)S(1)} %get-tuple-element.18), channel_id=1, source_target_pairs={{0,32},{1,2},{2,1},{3,4},{4,3},{5,6},{6,5},{7,8},{8,7},{9,10},{10,... | collective-permute-start | bytes 393224 | tf_op jit(solution)/shard_map/ppermute | solution.py:333
  4.4 0.9 %copy-done.2 = bf16[8,2,64,128]{3,2,1,0:T(8,128)(2,1)S(1)} copy-done((bf16[8,2,64,128]{3,2,1,0:T(8,128)(2,1)S(1)}, bf16[8,2,64,128]{3,2,1,0:T(8,128)(2,1)}, u32[]{:S(2)}) %copy-start.2) | copy-done | bytes 262168
  5.3 1.2 %copy-done.4 = bf16[3,3,3,128,128]{4,3,2,1,0:T(8,128)(2,1)S(1)} copy-done((bf16[3,3,3,128,128]{4,3,2,1,0:T(8,128)(2,1)S(1)}, bf16[3,3,3,128,128]{4,3,2,1,0:T(8,128)(2,1)}, u32[]{:S(2)}) %copy-start.4) | copy-done | bytes 884760
  6.5 1.1 %entry_own.1.before = f32[8,64,256]{2,1,0:T(8,128)S(1)} custom-call(bf16[8,2,64,128]{3,2,1,0:T(8,128)(2,1)S(1)} %copy-done.2, bf16[3,3,384,128]{3,2,1,0:T(8,128)(2,1)S(1)} %bitcast.33), custom_call_target="tpu_custom_call" | custom-call | flops 2000000000 | bytes 1048576 | tf_op jit(solution)/shard_map/entry_own/pallas_call | solution.py:313
  7.6 0.8 %dynamic-slice_bitcast_fusion.12 = (bf16[2,64,128]{2,1,0:T(8,128)(2,1)S(1)}, bf16[2,64,128]{2,1,0:T(8,128)(2,1)S(1)}) fusion(bf16[8,2,64,128]{3,2,1,0:T(8,128)(2,1)} %own.1, s32[]{:T(128)S(6)} %select_n.77, s32[]{:T(128)S(6)} %select_n.75), kind=kLoop, calls=%fused_computation.22 | loop fusion | bytes 131080 | tf_op jit(solution)/shard_map/squeeze | solution.py:384
  8.5 2.5 %collective-permute-done.1.y2 = bf16[8,64,128]{2,1,0:T(8,128)(2,1)S(1)} collective-permute-done((bf16[8,64,128]{2,1,0:T(8,128)(2,1)S(1)}, bf16[8,64,128]{2,1,0:T(8,128)(2,1)S(1)}, u32[]{:S(2)}, u32[]{:S(2)}) %collective-permute-start.1) | collective-permute-done | bytes 131104 | tf_op jit(solution)/shard_map/ppermute | solution.py:333
  11.0 0.1 collective-permute-start.3
  11.1 1.7 %collective-permute-start.2 = (bf16[4,64,128]{2,1,0:T(8,128)(2,1)S(1)}, bf16[4,64,128]{2,1,0:T(8,128)(2,1)S(1)}, u32[]{:S(2)}, u32[]{:S(2)}) collective-permute-start(bf16[4,64,128]{2,1,0:T(8,128)(2,1)S(1)} %pad_maximum_fusion.4), channel_id=1, source_target_pairs={{0,32},{32,0},{64,96},{96,64},{128,160},{160,128},{192,224},{224,1... | collective-permute-start | bytes 196616 | tf_op jit(solution)/shard_map/ppermute | solution.py:346
  12.8 1.0 %entry_side.1.before = f32[8,64,256]{2,1,0:T(8,128)S(1)} custom-call(bf16[8,64,128]{2,1,0:T(8,128)(2,1)S(1)} %collective-permute-done.y1, bf16[8,64,128]{2,1,0:T(8,128)(2,1)S(1)} %collective-permute-done.1.y2, bf16[3,3,384,128]{3,2,1,0:T(8,128)(2,1)S(1)} %bitcast.34, f32[8,64,256]{2,1,0:T(8,128)S(1)} %entry_own.1.before), custom_call_target="tpu_custom_call" | custom-call | flops 1000000000 | bytes 1048576 | tf_op jit(solution)/shard_map/entry_side/pallas_call | solution.py:313
  13.8 1.6 %collective-permute-done.3.x2 = bf16[4,64,128]{2,1,0:T(8,128)(2,1)S(1)} collective-permute-done((bf16[4,64,128]{2,1,0:T(8,128)(2,1)S(1)}, bf16[4,64,128]{2,1,0:T(8,128)(2,1)S(1)}, u32[]{:S(2)}, u32[]{:S(2)}) %collective-permute-start.3) | collective-permute-done | bytes 65568 | tf_op jit(solution)/shard_map/ppermute | solution.py:345
  15.4 0.7 %entry_last.1 = (bf16[8,2,64,128]{3,2,1,0:T(8,128)(2,1)S(1)}, bf16[4,32,256]{2,1,0:T(8,128)(2,1)S(1)}) custom-call(bf16[4,64,128]{2,1,0:T(8,128)(2,1)S(1)} %collective-permute-done.2.x1, bf16[4,64,128]{2,1,0:T(8,128)(2,1)S(1)} %collective-permute-done.3.x2, bf16[3,3,384,128]{3,2,1,0:T(8,128)(2,1)S(1)} %bitcast.35, ...), custom_call_target="tpu_custom_call" | custom-call | flops 1000000000 | bytes 1048576 | tf_op jit(solution)/shard_map/entry_last/pallas_call | solution.py:313
  16.2 1.8 %collective-permute-start.5 = (bf16[4,32,256]{2,1,0:T(8,128)(2,1)S(1)}, bf16[4,32,256]{2,1,0:T(8,128)(2,1)S(1)}, u32[]{:S(2)}, u32[]{:S(2)}) collective-permute-start(bf16[4,32,256]{2,1,0:T(8,128)(2,1)S(1)} %get-tuple-element.7.own), channel_id=1, source_target_pairs={{0,32},{1,2},{2,1},{3,4},{4,3},{5,6},{6,5},{7,8},{8,7},{9,10},{10,... | collective-permute-start | bytes 196616 | tf_op jit(solution)/shard_map/ppermute | solution.py:333
  18.1 0.6 %collective-permute-start.13 = (bf16[2,64,128]{2,1,0:T(8,128)(2,1)S(1)}, bf16[2,64,128]{2,1,0:T(8,128)(2,1)S(1)}, u32[]{:S(2)}, u32[]{:S(2)}) collective-permute-start(bf16[2,64,128]{2,1,0:T(8,128)(2,1)S(1)} %get-tuple-element.11), channel_id=1, source_target_pairs={{0,1},{1,0},{2,3},{3,2},{4,5},{5,4},{6,7},{7,6},{8,9},{9,8},{10,11... | collective-permute-start | bytes 98312 | tf_op jit(solution)/shard_map/ppermute | solution.py:345
  18.6 0.6 %collective-permute-done.12.ex1 = bf16[2,64,128]{2,1,0:T(8,128)(2,1)S(1)} collective-permute-done((bf16[2,64,128]{2,1,0:T(8,128)(2,1)S(1)}, bf16[2,64,128]{2,1,0:T(8,128)(2,1)S(1)}, u32[]{:S(2)}, u32[]{:S(2)}) %collective-permute-start.12) | collective-permute-done | bytes 32800 | tf_op jit(solution)/shard_map/ppermute | solution.py:346
  19.3 2.7 %collective-permute-done.13.ex2 = bf16[2,64,128]{2,1,0:T(8,128)(2,1)S(1)} collective-permute-done((bf16[2,64,128]{2,1,0:T(8,128)(2,1)S(1)}, bf16[2,64,128]{2,1,0:T(8,128)(2,1)S(1)}, u32[]{:S(2)}, u32[]{:S(2)}) %collective-permute-start.13) | collective-permute-done | bytes 32800 | tf_op jit(solution)/shard_map/ppermute | solution.py:345
  22.0 1.9 %collective-permute-done.5.y2 = bf16[4,32,256]{2,1,0:T(8,128)(2,1)S(1)} collective-permute-done((bf16[4,32,256]{2,1,0:T(8,128)(2,1)S(1)}, bf16[4,32,256]{2,1,0:T(8,128)(2,1)S(1)}, u32[]{:S(2)}, u32[]{:S(2)}) %collective-permute-start.5) | collective-permute-done | bytes 65568 | tf_op jit(solution)/shard_map/ppermute | solution.py:333
  24.1 1.1 %collective-permute-start.6 = (bf16[3,3,32,256]{3,2,1,0:T(8,128)(2,1)S(1)}, bf16[3,3,32,256]{3,2,1,0:T(8,128)(2,1)S(1)}, u32[]{:S(2)}, u32[]{:S(2)}) collective-permute-start(bf16[3,3,32,256]{3,2,1,0:T(8,128)(2,1)S(1)} %pad_maximum_fusion.2), channel_id=1, source_target_pairs={{0,32},{32,0},{64,96},{96,64},{128,160},{160,128},{192,224},{224,1... | collective-permute-start | bytes 442376 | tf_op jit(solution)/shard_map/ppermute | solution.py:346
  25.3 1.8 %collective-permute-start.15 = (bf16[10,64,128]{2,1,0:T(8,128)(2,1)S(1)}, bf16[10,64,128]{2,1,0:T(8,128)(2,1)S(1)}, u32[]{:S(2)}, u32[]{:S(2)}) collective-permute-start(bf16[10,64,128]{2,1,0:T(8,128)(2,1)S(1)} %pad_maximum_fusion.1), channel_id=1, source_target_pairs={{0,32},{1,2},{2,1},{3,4},{4,3},{5,6},{6,5},{7,8},{8,7},{9,10},{10,... | collective-permute-start | bytes 491528 | tf_op jit(solution)/shard_map/ppermute | solution.py:333
  27.1 2.2 %collective-permute-done.7.x2 = bf16[3,3,32,256]{3,2,1,0:T(8,128)(2,1)S(1)} collective-permute-done((bf16[3,3,32,256]{3,2,1,0:T(8,128)(2,1)S(1)}, bf16[3,3,32,256]{3,2,1,0:T(8,128)(2,1)S(1)}, u32[]{:S(2)}, u32[]{:S(2)}) %collective-permute-start.7) | collective-permute-done | bytes 147488 | tf_op jit(solution)/shard_map/ppermute | solution.py:345
  29.2 1.1 %first.1.own = bf16[8,32,256]{2,1,0:T(8,128)(2,1)S(1)} custom-call(bf16[4,32,256]{2,1,0:T(8,128)(2,1)S(1)} %get-tuple-element.7.own, bf16[4,32,256]{2,1,0:T(8,128)(2,1)S(1)} %collective-permute-done.4.y1, bf16[4,32,256]{2,1,0:T(8,128)(2,1)S(1)} %collective-permute-done.5.y2, bf16[3,3,32,256]{3,2,1,0:T(8,128)(2,1)S(1)} %collective-permute-done.6.x1, ...), custom_call_target="tpu_custom_call" | custom-call | flops 1000000000 | bytes 1048576 | tf_op jit(solution)/shard_map/first/pallas_call | solution.py:313
  30.5 1.8 %collective-permute-start.9 = (bf16[8,32,256]{2,1,0:T(8,128)(2,1)S(1)}, bf16[8,32,256]{2,1,0:T(8,128)(2,1)S(1)}, u32[]{:S(2)}, u32[]{:S(2)}) collective-permute-start(bf16[8,32,256]{2,1,0:T(8,128)(2,1)S(1)} %first.1.own), channel_id=1, source_target_pairs={{0,32},{1,2},{2,1},{3,4},{4,3},{5,6},{6,5},{7,8},{8,7},{9,10},{10,... | collective-permute-start | bytes 393224 | tf_op jit(solution)/shard_map/ppermute | solution.py:333
  32.3 0.3 collective-permute-start.14
  32.6 3.7 %collective-permute-done.8.y1 = bf16[8,32,256]{2,1,0:T(8,128)(2,1)S(1)} collective-permute-done((bf16[8,32,256]{2,1,0:T(8,128)(2,1)S(1)}, bf16[8,32,256]{2,1,0:T(8,128)(2,1)S(1)}, u32[]{:S(2)}, u32[]{:S(2)}) %collective-permute-start.8) | collective-permute-done | bytes 131104 | tf_op jit(solution)/shard_map/ppermute | solution.py:334
  36.3 2.5 %collective-permute-done.9.y2 = bf16[8,32,256]{2,1,0:T(8,128)(2,1)S(1)} collective-permute-done((bf16[8,32,256]{2,1,0:T(8,128)(2,1)S(1)}, bf16[8,32,256]{2,1,0:T(8,128)(2,1)S(1)}, u32[]{:S(2)}, u32[]{:S(2)}) %collective-permute-start.9) | collective-permute-done | bytes 131104 | tf_op jit(solution)/shard_map/ppermute | solution.py:333
  38.9 0.9 %second.1.own = bf16[6,32,256]{2,1,0:T(8,128)(2,1)S(1)} custom-call(bf16[8,32,256]{2,1,0:T(8,128)(2,1)S(1)} %first.1.own, bf16[8,32,256]{2,1,0:T(8,128)(2,1)S(1)} %collective-permute-done.8.y1, bf16[8,32,256]{2,1,0:T(8,128)(2,1)S(1)} %collective-permute-done.9.y2, bf16[3,2304,256]{2,1,0:T(8,128)(2,1)S(1)} %bitcast.32), custom_call_target="tpu_custom_call" | custom-call | flops 700000000 | bytes 1048576 | tf_op jit(solution)/shard_map/second/pallas_call | solution.py:313
  39.8 0.3 collective-permute-start.10
  40.0 2.1 %collective-permute-start.11 = (bf16[6,32,256]{2,1,0:T(8,128)(2,1)S(1)}, bf16[6,32,256]{2,1,0:T(8,128)(2,1)S(1)}, u32[]{:S(2)}, u32[]{:S(2)}) collective-permute-start(bf16[6,32,256]{2,1,0:T(8,128)(2,1)S(1)} %second.1.own), channel_id=1, source_target_pairs={{0,32},{1,2},{2,1},{3,4},{4,3},{5,6},{6,5},{7,8},{8,7},{9,10},{10,... | collective-permute-start | bytes 294920 | tf_op jit(solution)/shard_map/ppermute | solution.py:333
  42.2 4.5 %decode_own.1.before = f32[8,64,256]{2,1,0:T(8,128)S(1)} custom-call(bf16[6,32,256]{2,1,0:T(8,128)(2,1)S(1)} %second.1.own, bf16[8,2,64,128]{3,2,1,0:T(8,128)(2,1)S(1)} %get-tuple-element.8.encoded, bf16[2,64,128]{2,1,0:T(8,128)(2,1)S(1)} %collective-permute-done.12.ex1, bf16[2,64,128]{2,1,0:T(8,128)(2,1)S(1)} %collective-permute-done.13.ex2, ...), custom_call_target="tpu_custom_call" | custom-call | flops 3000000000 | bytes 1048576 | tf_op jit(solution)/shard_map/decode_own/pallas_call | solution.py:313
  46.7 1.4 %collective-permute-done.11.y2 = bf16[6,32,256]{2,1,0:T(8,128)(2,1)S(1)} collective-permute-done((bf16[6,32,256]{2,1,0:T(8,128)(2,1)S(1)}, bf16[6,32,256]{2,1,0:T(8,128)(2,1)S(1)}, u32[]{:S(2)}, u32[]{:S(2)}) %collective-permute-start.11) | collective-permute-done | bytes 98336 | tf_op jit(solution)/shard_map/ppermute | solution.py:333
  48.1 2.1 %decode_last.1 = bf16[8,2,64,128]{3,2,1,0:T(8,128)(2,1)} custom-call(bf16[6,32,256]{2,1,0:T(8,128)(2,1)S(1)} %collective-permute-done.10.y1, bf16[6,32,256]{2,1,0:T(8,128)(2,1)S(1)} %collective-permute-done.11.y2, bf16[2,2,2,256,128]{4,3,2,1,0:T(8,128)(2,1)S(1)} %copy-done.7, bf16[3,3,3,256,128]{4,3,2,1,0:T(8,128)(2,1)S(1)} %copy-done.3, ...), custom_call_target="tpu_custom_call" | custom-call | flops 1000000000 | bytes 1048576 | tf_op jit(solution)/shard_map/decode_last/pallas_call | solution.py:313
  (41 shorter events, 0.6 us)
Async XLA Ops:
  1.0 7.5 %collective-permute-start = (bf16[8,64,128]{2,1,0:T(8,128)(2,1)S(1)}, bf16[8,64,128]{2,1,0:T(8,128)(2,1)S(1)}, u32[]{:S(2)}, u32[]{:S(2)}) collective-permute-start(bf16[8,64,128]{2,1,0:T(8,128)(2,1)S(1)} %get-tuple-element.17), channel_id=1, source_target_pairs={{0,1},{1,0},{2,3},{3,2},{4,5},{5,4},{6,7},{7,6},{8,9},{9,8},{10,11... | collective-permute-start | bytes 393224 | tf_op jit(solution)/shard_map/ppermute | solution.py:334
  2.7 8.3 %collective-permute-start.1 = (bf16[8,64,128]{2,1,0:T(8,128)(2,1)S(1)}, bf16[8,64,128]{2,1,0:T(8,128)(2,1)S(1)}, u32[]{:S(2)}, u32[]{:S(2)}) collective-permute-start(bf16[8,64,128]{2,1,0:T(8,128)(2,1)S(1)} %get-tuple-element.18), channel_id=1, source_target_pairs={{0,32},{1,2},{2,1},{3,4},{4,3},{5,6},{6,5},{7,8},{8,7},{9,10},{10,... | collective-permute-start | bytes 393224 | tf_op jit(solution)/shard_map/ppermute | solution.py:333
  4.4 0.9 %copy-start.2 = (bf16[8,2,64,128]{3,2,1,0:T(8,128)(2,1)S(1)}, bf16[8,2,64,128]{3,2,1,0:T(8,128)(2,1)}, u32[]{:S(2)}) copy-start(bf16[8,2,64,128]{3,2,1,0:T(8,128)(2,1)} %own.1) | copy-start | bytes 786436
  5.3 1.2 %copy-start.4 = (bf16[3,3,3,128,128]{4,3,2,1,0:T(8,128)(2,1)S(1)}, bf16[3,3,3,128,128]{4,3,2,1,0:T(8,128)(2,1)}, u32[]{:S(2)}) copy-start(bf16[3,3,3,128,128]{4,3,2,1,0:T(8,128)(2,1)} %param.8) | copy-start | bytes 2654212
  6.5 6.3 %copy-start.5 = (bf16[3,3,3,128,128]{4,3,2,1,0:T(8,128)(2,1)S(1)}, bf16[3,3,3,128,128]{4,3,2,1,0:T(8,128)(2,1)}, u32[]{:S(2)}) copy-start(bf16[3,3,3,128,128]{4,3,2,1,0:T(8,128)(2,1)} %param.8) | copy-start | bytes 2654212
  7.6 7.8 %copy-start.6 = (bf16[2,2,2,128,256]{4,3,2,1,0:T(8,128)(2,1)S(1)}, bf16[2,2,2,128,256]{4,3,2,1,0:T(8,128)(2,1)}, u32[]{:S(2)}) copy-start(bf16[2,2,2,128,256]{4,3,2,1,0:T(8,128)(2,1)} %down.1) | copy-start | bytes 1572868
  11.0 4.4 %collective-permute-start.3 = (bf16[4,64,128]{2,1,0:T(8,128)(2,1)S(1)}, bf16[4,64,128]{2,1,0:T(8,128)(2,1)S(1)}, u32[]{:S(2)}, u32[]{:S(2)}) collective-permute-start(bf16[4,64,128]{2,1,0:T(8,128)(2,1)S(1)} %pad_maximum_fusion.5), channel_id=1, source_target_pairs={{0,1},{1,0},{2,3},{3,2},{4,5},{5,4},{6,7},{7,6},{8,9},{9,8},{10,11... | collective-permute-start | bytes 196616 | tf_op jit(solution)/shard_map/ppermute | solution.py:345
  11.1 4.2 %collective-permute-start.2 = (bf16[4,64,128]{2,1,0:T(8,128)(2,1)S(1)}, bf16[4,64,128]{2,1,0:T(8,128)(2,1)S(1)}, u32[]{:S(2)}, u32[]{:S(2)}) collective-permute-start(bf16[4,64,128]{2,1,0:T(8,128)(2,1)S(1)} %pad_maximum_fusion.4), channel_id=1, source_target_pairs={{0,32},{32,0},{64,96},{96,64},{128,160},{160,128},{192,224},{224,1... | collective-permute-start | bytes 196616 | tf_op jit(solution)/shard_map/ppermute | solution.py:346
  13.8 15.4 %copy-start = (bf16[3,3,3,256,256]{4,3,2,1,0:T(8,128)(2,1)S(1)}, bf16[3,3,3,256,256]{4,3,2,1,0:T(8,128)(2,1)}, u32[]{:S(2)}) copy-start(bf16[3,3,3,256,256]{4,3,2,1,0:T(8,128)(2,1)} %param.10) | copy-start | bytes 10616836
  16.1 22.8 %copy-start.1 = (bf16[3,3,3,256,256]{4,3,2,1,0:T(8,128)(2,1)S(1)}, bf16[3,3,3,256,256]{4,3,2,1,0:T(8,128)(2,1)}, u32[]{:S(2)}) copy-start(bf16[3,3,3,256,256]{4,3,2,1,0:T(8,128)(2,1)} %param.11) | copy-start | bytes 10616836
  16.1 5.8 %collective-permute-start.4 = (bf16[4,32,256]{2,1,0:T(8,128)(2,1)S(1)}, bf16[4,32,256]{2,1,0:T(8,128)(2,1)S(1)}, u32[]{:S(2)}, u32[]{:S(2)}) collective-permute-start(bf16[4,32,256]{2,1,0:T(8,128)(2,1)S(1)} %get-tuple-element.7.own), channel_id=1, source_target_pairs={{0,1},{1,0},{2,3},{3,2},{4,5},{5,4},{6,7},{7,6},{8,9},{9,8},{10,11... | collective-permute-start | bytes 196616 | tf_op jit(solution)/shard_map/ppermute | solution.py:334
  16.2 7.7 %collective-permute-start.5 = (bf16[4,32,256]{2,1,0:T(8,128)(2,1)S(1)}, bf16[4,32,256]{2,1,0:T(8,128)(2,1)S(1)}, u32[]{:S(2)}, u32[]{:S(2)}) collective-permute-start(bf16[4,32,256]{2,1,0:T(8,128)(2,1)S(1)} %get-tuple-element.7.own), channel_id=1, source_target_pairs={{0,32},{1,2},{2,1},{3,4},{4,3},{5,6},{6,5},{7,8},{8,7},{9,10},{10,... | collective-permute-start | bytes 196616 | tf_op jit(solution)/shard_map/ppermute | solution.py:333
  18.1 1.2 %collective-permute-start.12 = (bf16[2,64,128]{2,1,0:T(8,128)(2,1)S(1)}, bf16[2,64,128]{2,1,0:T(8,128)(2,1)S(1)}, u32[]{:S(2)}, u32[]{:S(2)}) collective-permute-start(bf16[2,64,128]{2,1,0:T(8,128)(2,1)S(1)} %get-tuple-element.12), channel_id=1, source_target_pairs={{0,32},{32,0},{64,96},{96,64},{128,160},{160,128},{192,224},{224,1... | collective-permute-start | bytes 98312 | tf_op jit(solution)/shard_map/ppermute | solution.py:346
  18.1 3.9 %collective-permute-start.13 = (bf16[2,64,128]{2,1,0:T(8,128)(2,1)S(1)}, bf16[2,64,128]{2,1,0:T(8,128)(2,1)S(1)}, u32[]{:S(2)}, u32[]{:S(2)}) collective-permute-start(bf16[2,64,128]{2,1,0:T(8,128)(2,1)S(1)} %get-tuple-element.11), channel_id=1, source_target_pairs={{0,1},{1,0},{2,3},{3,2},{4,5},{5,4},{6,7},{7,6},{8,9},{9,8},{10,11... | collective-permute-start | bytes 98312 | tf_op jit(solution)/shard_map/ppermute | solution.py:345
  24.0 5.2 %collective-permute-start.7 = (bf16[3,3,32,256]{3,2,1,0:T(8,128)(2,1)S(1)}, bf16[3,3,32,256]{3,2,1,0:T(8,128)(2,1)S(1)}, u32[]{:S(2)}, u32[]{:S(2)}) collective-permute-start(bf16[3,3,32,256]{3,2,1,0:T(8,128)(2,1)S(1)} %pad_maximum_fusion.3), channel_id=1, source_target_pairs={{0,1},{1,0},{2,3},{3,2},{4,5},{5,4},{6,7},{7,6},{8,9},{9,8},{10,11... | collective-permute-start | bytes 442376 | tf_op jit(solution)/shard_map/ppermute | solution.py:345
  24.1 5.1 %collective-permute-start.6 = (bf16[3,3,32,256]{3,2,1,0:T(8,128)(2,1)S(1)}, bf16[3,3,32,256]{3,2,1,0:T(8,128)(2,1)S(1)}, u32[]{:S(2)}, u32[]{:S(2)}) collective-permute-start(bf16[3,3,32,256]{3,2,1,0:T(8,128)(2,1)S(1)} %pad_maximum_fusion.2), channel_id=1, source_target_pairs={{0,32},{32,0},{64,96},{96,64},{128,160},{160,128},{192,224},{224,1... | collective-permute-start | bytes 442376 | tf_op jit(solution)/shard_map/ppermute | solution.py:346
  25.3 16.9 %collective-permute-start.15 = (bf16[10,64,128]{2,1,0:T(8,128)(2,1)S(1)}, bf16[10,64,128]{2,1,0:T(8,128)(2,1)S(1)}, u32[]{:S(2)}, u32[]{:S(2)}) collective-permute-start(bf16[10,64,128]{2,1,0:T(8,128)(2,1)S(1)} %pad_maximum_fusion.1), channel_id=1, source_target_pairs={{0,32},{1,2},{2,1},{3,4},{4,3},{5,6},{6,5},{7,8},{8,7},{9,10},{10,... | collective-permute-start | bytes 491528 | tf_op jit(solution)/shard_map/ppermute | solution.py:333
  29.2 12.9 %copy-start.3 = (bf16[3,3,3,256,128]{4,3,2,1,0:T(8,128)(2,1)S(1)}, bf16[3,3,3,256,128]{4,3,2,1,0:T(8,128)(2,1)}, u32[]{:S(2)}) copy-start(bf16[3,3,3,256,128]{4,3,2,1,0:T(8,128)(2,1)} %weight.3) | copy-start | bytes 5308420
  29.2 12.9 %copy-start.7 = (bf16[2,2,2,256,128]{4,3,2,1,0:T(8,128)(2,1)S(1)}, bf16[2,2,2,256,128]{4,3,2,1,0:T(8,128)(2,1)}, u32[]{:S(2)}) copy-start(bf16[2,2,2,256,128]{4,3,2,1,0:T(8,128)(2,1)} %up.3) | copy-start | bytes 1572868
  30.4 6.0 %collective-permute-start.8 = (bf16[8,32,256]{2,1,0:T(8,128)(2,1)S(1)}, bf16[8,32,256]{2,1,0:T(8,128)(2,1)S(1)}, u32[]{:S(2)}, u32[]{:S(2)}) collective-permute-start(bf16[8,32,256]{2,1,0:T(8,128)(2,1)S(1)} %first.1.own), channel_id=1, source_target_pairs={{0,1},{1,0},{2,3},{3,2},{4,5},{5,4},{6,7},{7,6},{8,9},{9,8},{10,11... | collective-permute-start | bytes 393224 | tf_op jit(solution)/shard_map/ppermute | solution.py:334
  30.5 8.4 %collective-permute-start.9 = (bf16[8,32,256]{2,1,0:T(8,128)(2,1)S(1)}, bf16[8,32,256]{2,1,0:T(8,128)(2,1)S(1)}, u32[]{:S(2)}, u32[]{:S(2)}) collective-permute-start(bf16[8,32,256]{2,1,0:T(8,128)(2,1)S(1)} %first.1.own), channel_id=1, source_target_pairs={{0,32},{1,2},{2,1},{3,4},{4,3},{5,6},{6,5},{7,8},{8,7},{9,10},{10,... | collective-permute-start | bytes 393224 | tf_op jit(solution)/shard_map/ppermute | solution.py:333
  32.3 9.9 %collective-permute-start.14 = (bf16[10,64,128]{2,1,0:T(8,128)(2,1)S(1)}, bf16[10,64,128]{2,1,0:T(8,128)(2,1)S(1)}, u32[]{:S(2)}, u32[]{:S(2)}) collective-permute-start(bf16[10,64,128]{2,1,0:T(8,128)(2,1)S(1)} %pad_maximum_fusion), channel_id=1, source_target_pairs={{0,1},{1,0},{2,3},{3,2},{4,5},{5,4},{6,7},{7,6},{8,9},{9,8},{10,11... | collective-permute-start | bytes 491528 | tf_op jit(solution)/shard_map/ppermute | solution.py:334
  39.8 6.9 %collective-permute-start.10 = (bf16[6,32,256]{2,1,0:T(8,128)(2,1)S(1)}, bf16[6,32,256]{2,1,0:T(8,128)(2,1)S(1)}, u32[]{:S(2)}, u32[]{:S(2)}) collective-permute-start(bf16[6,32,256]{2,1,0:T(8,128)(2,1)S(1)} %second.1.own), channel_id=1, source_target_pairs={{0,1},{1,0},{2,3},{3,2},{4,5},{5,4},{6,7},{7,6},{8,9},{9,8},{10,11... | collective-permute-start | bytes 294920 | tf_op jit(solution)/shard_map/ppermute | solution.py:334
  40.0 8.0 %collective-permute-start.11 = (bf16[6,32,256]{2,1,0:T(8,128)(2,1)S(1)}, bf16[6,32,256]{2,1,0:T(8,128)(2,1)S(1)}, u32[]{:S(2)}, u32[]{:S(2)}) collective-permute-start(bf16[6,32,256]{2,1,0:T(8,128)(2,1)S(1)} %second.1.own), channel_id=1, source_target_pairs={{0,32},{1,2},{2,1},{3,4},{4,3},{5,6},{6,5},{7,8},{8,7},{9,10},{10,... | collective-permute-start | bytes 294920 | tf_op jit(solution)/shard_map/ppermute | solution.py:333

commit v3 on v2

v3 whole, which is shorter than its diff:
```python
import jax
import jax.numpy as jnp
from jax import lax
from jax.experimental import pallas as pl
from jax.experimental.pallas import tpu as pltpu
from jax.sharding import PartitionSpec as P

BF = jnp.bfloat16
F32 = jnp.float32
LIMIT = 20 * 1024 * 1024


def leaky_unit(values):
    return jnp.where(values > 0, values, 0.1 * values)


def inside(index, count):
    return (index >= 0) & (index < count)


def depth_taps(cells):
    depth = cells.shape[0]
    at = lax.broadcasted_iota(jnp.int32, cells.shape, 0)
    before = jnp.where(at == 0, 0.0, pltpu.roll(cells, 1, axis=0))
    after = jnp.where(at == depth - 1, 0.0, pltpu.roll(cells, depth - 1, axis=0))
    return before.astype(BF), cells.astype(BF), after.astype(BF)


def own_columns(target, part):
    for off in range(3):
        target[off, :384, :128] = part(off, 1)
        target[off, :384, 128:] = part(off, 0)
        target[off, 384:, :128] = part(off, 2)
        target[off, 384:, 128:] = part(off, 1)


def put_taps(target, row, lane, cells):
    for tap, part in enumerate(depth_taps(cells)):
        target[row, :, lane + tap * 128 : lane + tap * 128 + 128] = part


def spans(cells, off):
    if cells.shape[0] == 10:
        return slice(off, off + 8), slice(0, 8)
    return slice(max(0, off - 1), min(8, 7 + off)), slice(max(0, 1 - off), min(8, 9 - off))


def add_own(total, cells, wide, start=False):
    for off in (1, 0, 2):
        source, into = spans(cells, off)
        rows = into.stop - into.start
        part = jnp.dot(
            cells[source].reshape(rows * 64, 768), wide[off], preferred_element_type=F32
        ).reshape(rows, 64, 256)
        for b in range(2):
            half = part[:, :, b * 128 : b * 128 + 128]
            if start and off == 1:
                total[b] = half
            else:
                total[b, into] += half


def add_side(total, cells, part, side):
    for off in (1, 0, 2):
        source, into = spans(cells, off)
        rows = into.stop - into.start
        total[side, into] += jnp.dot(
            cells[source].reshape(rows * 64, 384), part(off, 2 * side), preferred_element_type=F32
        ).reshape(rows, 64, 128)


def add_rows(total, x_near, x_far, stacked, part):
    gx, gy = lax.axis_index("gx"), lax.axis_index("gy")
    nx, ny = lax.axis_size("gx"), lax.axis_size("gy")
    odd_x = lax.rem(gx, 2) == 1
    for col in range(4):
        first, second = x_near[col].astype(F32), x_far[col].astype(F32)
        low = jnp.where(odd_x, first, second)
        high = jnp.where(odd_x, second, first)
        ok = inside(gy * 2 - 1 + col, ny * 2)
        put_taps(stacked, 0, col * 384, jnp.where(ok & (gx > 0), low, 0.0))
        put_taps(stacked, 1, col * 384, jnp.where(ok & (gx < nx - 1), high, 0.0))
    for side, (row, off) in enumerate(((0, 0), (7, 2))):
        for b in range(2):
            total[b, row] += jnp.dot(
                stacked[side, :, b * 384 : b * 384 + 1152],
                part(off).reshape(1152, 128),
                preferred_element_type=F32,
            )


def sides():
    gy = lax.axis_index("gy")
    odd = lax.rem(gy, 2)
    return 1 - odd, odd, (gy > 0) & (gy < lax.axis_size("gy") - 1)


def prep_kernel(volume, own, near, far, edge_near, edge_far, sem):
    copy = pltpu.make_async_copy(volume, own, sem)
    copy.start()
    odd_x, odd_y = lax.rem(lax.axis_index("gx"), 2), lax.rem(lax.axis_index("gy"), 2)
    copy.wait()
    near[...] = own[:, 1 - odd_y]
    far[...] = own[:, odd_y]
    edge_near[...] = own[7 * (1 - odd_x)]
    edge_far[...] = own[7 * odd_x]


def entry_own_kernel(own, weight_hbm, total, weight, stacked, wide, sem):
    copy = pltpu.make_async_copy(weight_hbm, weight, sem)
    copy.start()

    def one_row(i, carry):
        for col in range(2):
            put_taps(stacked, i, col * 384, own[i, col].astype(F32))
        return carry

    lax.fori_loop(0, 8, one_row, 0)
    copy.wait()
    own_columns(wide, lambda off, col: weight[off, col])
    add_own(total, stacked, wide, start=True)


def entry_side_kernel(y_near, y_far, weight, before, total, near, far):
    side_near, side_far, far_ok = sides()
    total[...] = before[...]

    def one_row(i, carry):
        put_taps(near, i, 0, y_near[i].astype(F32))
        put_taps(far, i, 0, jnp.where(far_ok, y_far[i].astype(F32), 0.0))
        return carry

    lax.fori_loop(0, 8, one_row, 0)
    add_side(total, near, lambda off, col: weight[off, col], side_near)
    add_side(total, far, lambda off, col: weight[off, col], side_far)


def entry_last_kernel(x_near, x_far, weight, down, before, encoded, coarse, stacked, fine, total):
    total[:, 0] = before[:, 0]
    total[:, 7] = before[:, 7]
    add_rows(total, x_near, x_far, stacked, lambda off: weight[off])

    def finish(row, source):
        for b in range(2):
            half = leaky_unit(source[b, row]).astype(BF)
            encoded[row, b] = half
            fine[row, b] = half.astype(F32)

    def middle(row, carry):
        finish(row, before)
        return carry

    lax.fori_loop(1, 7, middle, 0)
    finish(0, total)
    finish(7, total)
    small = jnp.zeros((128, 256), F32)
    for a in range(2):
        for d in range(2):
            cells = jnp.concatenate(
                [
                    jnp.concatenate(
                        [fine[2 * i + a, b, pl.ds(d, 32, stride=2), :] for b in range(2)], axis=1
                    )
                    for i in range(4)
                ],
                axis=0,
            ).astype(BF)
            small = small + jnp.dot(
                cells, down[a, :, d].reshape(256, 256), preferred_element_type=F32
            )
    coarse[...] = leaky_unit(small).astype(BF).reshape(4, 32, 256)


def fill_deep(rows, first_row, planes, stacked):
    gy = lax.axis_index("gy")
    nx, ny = lax.axis_size("gx"), lax.axis_size("gy")

    for row in range(rows):
        ok_row = inside(first_row + row, nx * 4)
        for plane, cells in enumerate(planes(row)):
            ok = ok_row & inside(gy - 1 + plane, ny)
            for tap, part in enumerate(depth_taps(jnp.where(ok, cells, 0.0))):
                lane = (plane * 3 + tap) * 256
                stacked[row, :, lane : lane + 256] = part


def deep_conv(rows, stacked, weight, out):
    total = jnp.zeros((rows * 32, 256), F32)
    for off in range(3):
        total = total + jnp.dot(
            stacked[off : off + rows].reshape(rows * 32, 2304),
            weight[off],
            preferred_element_type=F32,
        )
    out[...] = leaky_unit(total).astype(BF).reshape(rows, 32, 256)


def first_kernel(own, y1, y2, x1, x2, weight, out, stacked):
    gx, gy = lax.axis_index("gx"), lax.axis_index("gy")
    odd_x, odd_y = lax.rem(gx, 2) == 1, lax.rem(gy, 2) == 1

    def planes(row):
        if 3 <= row < 7:
            first, second = y1[row - 3].astype(F32), y2[row - 3].astype(F32)
            return (
                jnp.where(odd_y, first, second),
                own[row - 3].astype(F32),
                jnp.where(odd_y, second, first),
            )
        result = []
        for plane in range(3):
            at = row if row < 3 else row - 7
            first, second = x1[at, plane].astype(F32), x2[at, plane].astype(F32)
            if row < 3:
                result.append(jnp.where(odd_x, first, second))
            else:
                result.append(jnp.where(odd_x, second, first))
        return result

    fill_deep(10, gx * 4 - 3, planes, stacked)
    deep_conv(8, stacked, weight, out)


def second_kernel(own, y1, y2, weight, out, stacked):
    gx, gy = lax.axis_index("gx"), lax.axis_index("gy")
    odd_y = lax.rem(gy, 2) == 1

    def planes(row):
        first, second = y1[row].astype(F32), y2[row].astype(F32)
        return (
            jnp.where(odd_y, first, second),
            own[row].astype(F32),
            jnp.where(odd_y, second, first),
        )

    fill_deep(8, gx * 4 - 2, planes, stacked)
    deep_conv(6, stacked, weight, out)


def half_weights(weight, half):
    return lambda off, col: weight[off, col, :, half * 128 : half * 128 + 128].reshape(384, 128)


def lift(cells, up, b, upward, col):
    for a in range(2):
        for d in range(2):
            part = leaky_unit(jnp.dot(cells, up[a, b, d], preferred_element_type=F32))
            part = part.reshape(6, 32, 128)
            for i in range(6):
                row = 2 * i + a - 1
                if 0 <= row < 10:
                    upward[row, col, pl.ds(d, 32, stride=2), :] = part[i]


def put_lifted(target, upward, cols, y_ok):
    gx, nx = lax.axis_index("gx"), lax.axis_size("gx")

    def lifted(row, carry):
        ok = y_ok & inside(gx * 8 - 1 + row, nx * 8)
        for col in range(cols):
            put_taps(target, row, col * 384, jnp.where(ok, upward[row, col], 0.0))
        return carry

    lax.fori_loop(0, 10, lifted, 0)


def decode_skip_kernel(encoded, y_near, y_far, weight, total, stacked, near, far, wide):
    side_near, side_far, far_ok = sides()
    part = half_weights(weight, 1)
    own_columns(wide, part)

    def one_row(i, carry):
        for col in range(2):
            put_taps(stacked, i, col * 384, encoded[i, col].astype(F32))
        put_taps(near, i, 0, y_near[i].astype(F32))
        put_taps(far, i, 0, jnp.where(far_ok, y_far[i].astype(F32), 0.0))
        return carry

    lax.fori_loop(0, 8, one_row, 0)
    add_own(total, stacked, wide, start=True)
    add_side(total, near, part, side_near)
    add_side(total, far, part, side_far)


def decode_own_kernel(
    own, x_near, x_far, up, weight, before, total, stacked, edges, wide, upward
):
    total[...] = before[...]
    part = half_weights(weight, 0)
    own_columns(wide, part)
    lift(own[...].reshape(192, 256), up, 0, upward, 0)
    lift(own[...].reshape(192, 256), up, 1, upward, 1)
    put_lifted(stacked, upward, 2, True)
    add_own(total, stacked, wide)
    add_rows(total, x_near, x_far, edges, lambda off: weight[off, :, :, 128:])


def decode_near_kernel(y_near, up, weight, before, total, near, upward):
    side, _, _ = sides()
    total[...] = before[...]
    lift(y_near[...].reshape(192, 256), up, 1 - side, upward, 0)
    put_lifted(near, upward, 1, True)
    add_side(total, near, half_weights(weight, 0), side)


def decode_last_kernel(y_far, up, weight, before, decoded, far, upward, total):
    _, side, far_ok = sides()
    total[...] = before[...]
    lift(y_far[...].reshape(192, 256), up, 1 - side, upward, 0)
    put_lifted(far, upward, 1, far_ok)
    add_side(total, far, half_weights(weight, 0), side)
    for b in range(2):
        decoded[:, b] = leaky_unit(total[b]).astype(BF)


def call(kernel, outs, scratch, name, flops, *operands, remote=()):
    vmem = pl.BlockSpec(memory_space=pltpu.VMEM)
    anywhere = pl.BlockSpec(memory_space=pltpu.HBM)
    return pl.pallas_call(
        kernel,
        out_shape=[jax.ShapeDtypeStruct(shape, dtype) for shape, dtype in outs],
        in_specs=[anywhere if i in remote else vmem for i in range(len(operands))],
        out_specs=[vmem] * len(outs),
        scratch_shapes=[
            pltpu.SemaphoreType.DMA if shape is None else pltpu.VMEM(shape, dtype)
            for shape, dtype in scratch
        ],
        compiler_params=pltpu.CompilerParams(vmem_limit_bytes=LIMIT),
        cost_estimate=pl.CostEstimate(flops=flops, bytes_accessed=1 << 20, transcendentals=0),
        name=name,
    )(*operands)


def swap_y(near_cells, far_cells, far_first=True):
    nx, ny = lax.axis_size("gx"), lax.axis_size("gy")
    near = [(i, i ^ 1) for i in range(ny)]
    far = []
    for x in range(nx):
        for y in range(ny):
            to = (x ^ 1) * ny + y if y in (0, ny - 1) else x * ny + ((y + 1) ^ 1) - 1
            far.append((x * ny + y, to))
    far = far[ny // 2 - 1 :] + far[: ny // 2 - 1]
    got = lax.ppermute(near_cells, "gy", near)
    there = lax.ppermute(far_cells, ("gx", "gy"), far)
    if far_first:
        at = lax.axis_index("gy")
        there = jnp.where((at > 0) & (at < ny - 1), there, jnp.zeros_like(there))
        there = lax.optimization_barrier(there)
    return got, there


def swap_x(near_cells, far_cells):
    nx, ny = lax.axis_size("gx"), lax.axis_size("gy")
    near = [(i, i ^ 1) for i in range(nx)]
    far = []
    for x in range(nx):
        for y in range(ny):
            to = x * ny + (y ^ 1) if x in (0, nx - 1) else (((x + 1) ^ 1) - 1) * ny + y
            far.append((x * ny + y, to))
    got = lax.ppermute(near_cells, "gx", near)
    return got, lax.ppermute(far_cells, ("gx", "gy"), far)


def local(
    volume,
    weight_entry,
    weight_down,
    weight_deep_first,
    weight_deep_second,
    weight_upward,
    weight_decoder,
):
    odd_x = lax.rem(lax.axis_index("gx"), 2)
    odd_y = lax.rem(lax.axis_index("gy"), 2)

    def column(array, at):
        return lax.dynamic_index_in_dim(array, at, axis=1, keepdims=False)

    def rows(array, at, count):
        return lax.dynamic_slice_in_dim(array, at, count, axis=0)

    def four_columns(pair, y_near, y_far, at):
        near, far = rows(y_near, at, 1), rows(y_far, at, 1)
        low = jnp.where(odd_y == 1, near, far)
        high = jnp.where(odd_y == 1, far, near)
        return jnp.concatenate([low, pair, high], axis=0)

    at_near, at_far = 7 * (1 - odd_x), 7 * odd_x
    sums = ((2, 8, 64, 128), F32)
    line = ((8, 64, 128), BF)
    own, near, far, edge_near, edge_far = call(
        prep_kernel,
        [((8, 2, 64, 128), BF), line, line, ((2, 64, 128), BF), ((2, 64, 128), BF)],
        [(None, None)],
        "prep",
        1_000_000,
        volume,
        remote=(0,),
    )
    y1, y2 = swap_y(near, far)
    total, entry = call(
        entry_own_kernel,
        [sums, ((3, 3, 384, 128), BF)],
        [((8, 64, 768), BF), ((3, 768, 256), BF), (None, None)],
        "entry_own",
        2_000_000_000,
        own,
        weight_entry.reshape(3, 3, 384, 128),
        remote=(1,),
    )
    x1, x2 = swap_x(
        four_columns(edge_near, y1, y2, at_near), four_columns(edge_far, y1, y2, at_far)
    )
    (total,) = call(
        entry_side_kernel,
        [sums],
        [((8, 64, 384), BF), ((8, 64, 384), BF)],
        "entry_side",
        1_000_000_000,
        y1,
        y2,
        entry,
        total,
    )
    encoded, coarse = call(
        entry_last_kernel,
        [((8, 2, 64, 128), BF), ((4, 32, 256), BF)],
        [((2, 64, 1536), BF), ((8, 2, 64, 128), F32), sums],
        "entry_last",
        1_000_000_000,
        x1,
        x2,
        entry,
        weight_down,
        total,
    )

    g1, g2 = swap_y(column(encoded, 1 - odd_y), column(encoded, odd_y))
    c1, c2 = swap_y(coarse, coarse)
    c_low = jnp.where(odd_y == 1, c1, c2)
    c_high = jnp.where(odd_y == 1, c2, c1)

    def coarse_edge(at):
        return jnp.stack([rows(c_low, at, 3), rows(coarse, at, 3), rows(c_high, at, 3)], axis=1)

    d1, d2 = swap_x(coarse_edge(1 - odd_x), coarse_edge(odd_x))
    (deep_one,) = call(
        first_kernel,
        [((8, 32, 256), BF)],
        [((10, 32, 2304), BF)],
        "first",
        1_000_000_000,
        coarse,
        c1,
        c2,
        d1,
        d2,
        weight_deep_first.reshape(3, 2304, 256),
    )
    f1, f2 = swap_y(deep_one, deep_one)
    skip, _ = lax.optimization_barrier(((encoded, g1, g2), deep_one))
    (total,) = call(
        decode_skip_kernel,
        [sums],
        [((8, 64, 768), BF), ((8, 64, 384), BF), ((8, 64, 384), BF), ((3, 768, 256), BF)],
        "decode_skip",
        2_000_000_000,
        *skip,
        weight_decoder,
    )
    edges = (
        four_columns(rows(encoded, at_near, 1)[0], g1, g2, at_near),
        four_columns(rows(encoded, at_far, 1)[0], g1, g2, at_far),
    )
    edges, total = lax.optimization_barrier((edges, total))
    e1, e2 = swap_x(*edges)
    (deep_two,) = call(
        second_kernel,
        [((6, 32, 256), BF)],
        [((8, 32, 2304), BF)],
        "second",
        700_000_000,
        deep_one,
        f1,
        f2,
        weight_deep_second.reshape(3, 2304, 256),
    )
    h1, h2 = swap_y(deep_two, deep_two, far_first=False)
    (total,) = call(
        decode_own_kernel,
        [sums],
        [
            ((10, 64, 768), BF),
            ((2, 64, 1536), BF),
            ((3, 768, 256), BF),
            ((10, 2, 64, 128), F32),
        ],
        "decode_own",
        2_000_000_000,
        deep_two,
        e1,
        e2,
        weight_upward,
        weight_decoder,
        total,
    )
    (total,) = call(
        decode_near_kernel,
        [sums],
        [((10, 64, 384), BF), ((10, 1, 64, 128), F32)],
        "decode_near",
        1_000_000_000,
        h1,
        weight_upward,
        weight_decoder,
        total,
    )
    (decoded,) = call(
        decode_last_kernel,
        [((8, 2, 64, 128), BF)],
        [((10, 64, 384), BF), ((10, 1, 64, 128), F32), sums],
        "decode_last",
        1_000_000_000,
        h2,
        weight_upward,
        weight_decoder,
        total,
    )
    return decoded


def solution(mesh):
    return jax.shard_map(
        local,
        mesh=mesh,
        in_specs=(P("gx", "gy", None, None), P(), P(), P(), P(), P(), P()),
        out_specs=P("gx", "gy", None, None),
        check_vma=False,
    )
```

time: 50.4 us -> 48.3 us (0.958)
  waiting for transfers between devices: 19.2 us -> 14.7 us
  starting transfers between devices: 15.2 us -> 19.5 us
  local copies, waits for them, and re-layouts: 4.08 us -> 2.21 us
    ppermute x16, waiting for transfers between devices: 19.2 us -> 14.7 us  [the longest x5 11 us: swap_y(): there = lax.ppermute(far_cells, ('gx', 'gy'), far)]
    ppermute x16, starting transfers between devices: 15.2 us -> 19.5 us  [the longest x5 13.5 us: swap_y(): there = lax.ppermute(far_cells, ('gx', 'gy'), far)]
    squeeze x2 -> x1, local copies, waits for them, and re-layouts: 1.01 us -> 0.02 us  [column(): return lax.dynamic_index_in_dim(array, at, axis=1, keepdims=False)]
    squeeze x2 -> x1, local copies, waits for them, and re-layouts: 0.85 us -> 0.01 us  [local(): rows(encoded, at_far, 1)[0]]
    pallas_call x7 -> x10, Pallas kernels: 11.3 us -> 11.3 us  [call(): pl.pallas_call(kernel, out_shape=[jax.ShapeDtypeStruct(shape, dtype) for...]
    unnamed x16 -> x14, local copies, waits for them, and re-layouts: 2.15 us -> 2.15 us
  transfers between devices with their start and end apart: 16 -> 16, of which waited for: 9 -> 8; matrix products, arithmetic and copies ran while one was open for 2% -> 0% of each run, Pallas kernels for 17% -> 16%
where the time goes in v3:
time: 48.3 us; the launch traced here: 48.1 us
  starting transfers between devices  19.5 us (40%)
  waiting for transfers between devices  14.7 us (30%)
  Pallas kernels  11.3 us (23%)
  local copies, waits for them, and re-layouts  2.21 us (5%)
    ppermute x5, starting transfers between devices, swap_y(): there = lax.ppermute(far_cells, ('gx', 'gy'), far)  13.5 us
    pallas_call x10, Pallas kernels, call(): pl.pallas_call(kernel, out_shape=[jax.ShapeDtypeStruct(shape, dtype) for...  11.3 us
    ppermute x5, waiting for transfers between devices, swap_y(): there = lax.ppermute(far_cells, ('gx', 'gy'), far)  11 us
    ppermute x3, waiting for transfers between devices, swap_x(): return (got, lax.ppermute(far_cells, ('gx', 'gy'), far))  3.5 us
    ppermute x3, starting transfers between devices, swap_x(): got = lax.ppermute(near_cells, 'gx', near)  3.05 us
    ppermute x3, starting transfers between devices, swap_x(): return (got, lax.ppermute(far_cells, ('gx', 'gy'), far))  2.3 us
    unnamed x14, local copies, waits for them, and re-layouts  2.15 us
  transfers between devices with their start and end apart: 16, of which 8 were waited for; matrix products, arithmetic and copies ran while one was open for 0% of the time, Pallas kernels for 16%

profile of v3, /device:TPU:128, one launch (start us, length us, event | category | flops | bytes accessed | tf_op | source)
XLA Modules:
  0.0 48.1 jit_solution(8586501099702294360)
XLA Ops:
  0.0 0.9 %copy-done.2 = bf16[8,2,64,128]{3,2,1,0:T(8,128)(2,1)S(1)} copy-done((bf16[8,2,64,128]{3,2,1,0:T(8,128)(2,1)S(1)}, bf16[8,2,64,128]{3,2,1,0:T(8,128)(2,1)}, u32[]{:S(2)}) %copy-start.2) | copy-done | bytes 262168
  1.0 2.6 %collective-permute-start.1 = (bf16[8,64,128]{2,1,0:T(8,128)(2,1)S(1)}, bf16[8,64,128]{2,1,0:T(8,128)(2,1)S(1)}, u32[]{:S(2)}, u32[]{:S(2)}) collective-permute-start(bf16[8,64,128]{2,1,0:T(8,128)(2,1)S(1)} %get-tuple-element.21), channel_id=1, source_target_pairs={{15,16},{16,15},{17,18},{18,17},{19,20},{20,19},{21,22},{22,21},{2... | collective-permute-start | bytes 393224 | tf_op jit(solution)/shard_map/ppermute | solution.py:344
  3.7 0.6 %collective-permute-start = (bf16[8,64,128]{2,1,0:T(8,128)(2,1)S(1)}, bf16[8,64,128]{2,1,0:T(8,128)(2,1)S(1)}, u32[]{:S(2)}, u32[]{:S(2)}) collective-permute-start(bf16[8,64,128]{2,1,0:T(8,128)(2,1)S(1)} %get-tuple-element.20), channel_id=1, source_target_pairs={{0,1},{1,0},{2,3},{3,2},{4,5},{5,4},{6,7},{7,6},{8,9},{9,8},{10,11... | collective-permute-start | bytes 393224 | tf_op jit(solution)/shard_map/ppermute | solution.py:343
  4.3 1.2 %copy-done.4 = bf16[3,3,3,128,128]{4,3,2,1,0:T(8,128)(2,1)S(1)} copy-done((bf16[3,3,3,128,128]{4,3,2,1,0:T(8,128)(2,1)S(1)}, bf16[3,3,3,128,128]{4,3,2,1,0:T(8,128)(2,1)}, u32[]{:S(2)}) %copy-start.4) | copy-done | bytes 884760
  5.4 1.2 %entry_own.1 = (f32[2,8,64,128]{3,2,1,0:T(8,128)S(1)}, bf16[3,3,384,128]{3,2,1,0:T(8,128)(2,1)S(1)}) custom-call(bf16[8,2,64,128]{3,2,1,0:T(8,128)(2,1)S(1)} %get-tuple-element.24.own, bf16[3,3,384,128]{3,2,1,0:T(8,128)(2,1)S(1)} %bitcast.25), custom_call_target="tpu_custom_call" | custom-call | flops 2000000000 | bytes 1048576 | tf_op jit(solution)/shard_map/entry_own/pallas_call | solution.py:319
  6.6 3.0 %collective-permute-done.1 = bf16[8,64,128]{2,1,0:T(8,128)(2,1)S(1)} collective-permute-done((bf16[8,64,128]{2,1,0:T(8,128)(2,1)S(1)}, bf16[8,64,128]{2,1,0:T(8,128)(2,1)S(1)}, u32[]{:S(2)}, u32[]{:S(2)}) %collective-permute-start.1) | collective-permute-done | bytes 131104 | tf_op jit(solution)/shard_map/ppermute | solution.py:344
  9.7 0.1 collective-permute-start.3
  9.9 1.7 %collective-permute-start.2 = (bf16[4,64,128]{2,1,0:T(8,128)(2,1)S(1)}, bf16[4,64,128]{2,1,0:T(8,128)(2,1)S(1)}, u32[]{:S(2)}, u32[]{:S(2)}) collective-permute-start(bf16[4,64,128]{2,1,0:T(8,128)(2,1)S(1)} %pad_maximum_fusion.2), channel_id=1, source_target_pairs={{0,32},{32,0},{64,96},{96,64},{128,160},{160,128},{192,224},{224,1... | collective-permute-start | bytes 196616 | tf_op jit(solution)/shard_map/ppermute | solution.py:360
  11.5 0.9 %entry_side.1.before = f32[2,8,64,128]{3,2,1,0:T(8,128)S(1)} custom-call(bf16[8,64,128]{2,1,0:T(8,128)(2,1)S(1)} %collective-permute-done.y_near, bf16[8,64,128]{2,1,0:T(8,128)(2,1)S(1)} %broadcast_select_fusion.2.y_far, bf16[3,3,384,128]{3,2,1,0:T(8,128)(2,1)S(1)} %get-tuple-element.25.weight, f32[2,8,64,128]{3,2,1,0:T(8,128)S(1)} %get-tuple-element.26.before), custom_call_target="tpu_custom_call" | custom-call | flops 1000000000 | bytes 1048576 | tf_op jit(solution)/shard_map/entry_side/pallas_call | solution.py:319
  12.5 1.6 %collective-permute-done.3.x_far = bf16[4,64,128]{2,1,0:T(8,128)(2,1)S(1)} collective-permute-done((bf16[4,64,128]{2,1,0:T(8,128)(2,1)S(1)}, bf16[4,64,128]{2,1,0:T(8,128)(2,1)S(1)}, u32[]{:S(2)}, u32[]{:S(2)}) %collective-permute-start.3) | collective-permute-done | bytes 65568 | tf_op jit(solution)/shard_map/ppermute | solution.py:361
  14.1 0.7 %entry_last.1 = (bf16[8,2,64,128]{3,2,1,0:T(8,128)(2,1)S(1)}, bf16[4,32,256]{2,1,0:T(8,128)(2,1)S(1)}) custom-call(bf16[4,64,128]{2,1,0:T(8,128)(2,1)S(1)} %collective-permute-done.2.x_near, bf16[4,64,128]{2,1,0:T(8,128)(2,1)S(1)} %collective-permute-done.3.x_far, bf16[3,3,384,128]{3,2,1,0:T(8,128)(2,1)S(1)} %get-tuple-element.25.weight, ...), custom_call_target="tpu_custom_call" | custom-call | flops 1000000000 | bytes 1048576 | tf_op jit(solution)/shard_map/entry_last/pallas_call | solution.py:319
  14.8 2.6 %collective-permute-start.5 = (bf16[4,32,256]{2,1,0:T(8,128)(2,1)S(1)}, bf16[4,32,256]{2,1,0:T(8,128)(2,1)S(1)}, u32[]{:S(2)}, u32[]{:S(2)}) collective-permute-start(bf16[4,32,256]{2,1,0:T(8,128)(2,1)S(1)} %get-tuple-element.27.own), channel_id=1, source_target_pairs={{15,16},{16,15},{17,18},{18,17},{19,20},{20,19},{21,22},{22,21},{2... | collective-permute-start | bytes 196616 | tf_op jit(solution)/shard_map/ppermute | solution.py:344
  17.4 2.9 %collective-permute-start.13 = (bf16[8,64,128]{2,1,0:T(8,128)(2,1)S(1)}, bf16[8,64,128]{2,1,0:T(8,128)(2,1)S(1)}, u32[]{:S(2)}, u32[]{:S(2)}) collective-permute-start(bf16[8,64,128]{2,1,0:T(8,128)(2,1)S(1)} %get-tuple-element.42), channel_id=1, source_target_pairs={{15,16},{16,15},{17,18},{18,17},{19,20},{20,19},{21,22},{22,21},{2... | collective-permute-start | bytes 393224 | tf_op jit(solution)/shard_map/ppermute | solution.py:344
  20.4 2.1 %collective-permute-done.5 = bf16[4,32,256]{2,1,0:T(8,128)(2,1)S(1)} collective-permute-done((bf16[4,32,256]{2,1,0:T(8,128)(2,1)S(1)}, bf16[4,32,256]{2,1,0:T(8,128)(2,1)S(1)}, u32[]{:S(2)}, u32[]{:S(2)}) %collective-permute-start.5) | collective-permute-done | bytes 65568 | tf_op jit(solution)/shard_map/ppermute | solution.py:344
  22.6 0.1 collective-permute-start.7
  22.7 1.1 %collective-permute-start.6 = (bf16[3,3,32,256]{3,2,1,0:T(8,128)(2,1)S(1)}, bf16[3,3,32,256]{3,2,1,0:T(8,128)(2,1)S(1)}, u32[]{:S(2)}, u32[]{:S(2)}) collective-permute-start(bf16[3,3,32,256]{3,2,1,0:T(8,128)(2,1)S(1)} %pad_maximum_fusion), channel_id=1, source_target_pairs={{0,32},{32,0},{64,96},{96,64},{128,160},{160,128},{192,224},{224,1... | collective-permute-start | bytes 442376 | tf_op jit(solution)/shard_map/ppermute | solution.py:360
  23.8 2.0 %collective-permute-done.13 = bf16[8,64,128]{2,1,0:T(8,128)(2,1)S(1)} collective-permute-done((bf16[8,64,128]{2,1,0:T(8,128)(2,1)S(1)}, bf16[8,64,128]{2,1,0:T(8,128)(2,1)S(1)}, u32[]{:S(2)}, u32[]{:S(2)}) %collective-permute-start.13) | collective-permute-done | bytes 131104 | tf_op jit(solution)/shard_map/ppermute | solution.py:344
  25.9 1.9 %collective-permute-done.7.x2 = bf16[3,3,32,256]{3,2,1,0:T(8,128)(2,1)S(1)} collective-permute-done((bf16[3,3,32,256]{3,2,1,0:T(8,128)(2,1)S(1)}, bf16[3,3,32,256]{3,2,1,0:T(8,128)(2,1)S(1)}, u32[]{:S(2)}, u32[]{:S(2)}) %collective-permute-start.7) | collective-permute-done | bytes 147488 | tf_op jit(solution)/shard_map/ppermute | solution.py:361
  27.8 1.1 %first.1.own = bf16[8,32,256]{2,1,0:T(8,128)(2,1)S(1)} custom-call(bf16[4,32,256]{2,1,0:T(8,128)(2,1)S(1)} %get-tuple-element.27.own, bf16[4,32,256]{2,1,0:T(8,128)(2,1)S(1)} %collective-permute-done.4.y1, bf16[4,32,256]{2,1,0:T(8,128)(2,1)S(1)} %broadcast_select_fusion.5.y2, bf16[3,3,32,256]{3,2,1,0:T(8,128)(2,1)S(1)} %collective-permute-done.6.x1, ...), custom_call_target="tpu_custom_call" | custom-call | flops 1000000000 | bytes 1048576 | tf_op jit(solution)/shard_map/first/pallas_call | solution.py:319
  28.9 2.6 %collective-permute-start.9 = (bf16[8,32,256]{2,1,0:T(8,128)(2,1)S(1)}, bf16[8,32,256]{2,1,0:T(8,128)(2,1)S(1)}, u32[]{:S(2)}, u32[]{:S(2)}) collective-permute-start(bf16[8,32,256]{2,1,0:T(8,128)(2,1)S(1)} %first.1.own), channel_id=1, source_target_pairs={{15,16},{16,15},{17,18},{18,17},{19,20},{20,19},{21,22},{22,21},{2... | collective-permute-start | bytes 393224 | tf_op jit(solution)/shard_map/ppermute | solution.py:344
  31.6 2.0 %decode_skip.1.before = f32[2,8,64,128]{3,2,1,0:T(8,128)S(1)} custom-call(bf16[8,2,64,128]{3,2,1,0:T(8,128)(2,1)S(1)} %get-tuple-element.29.encoded, bf16[8,64,128]{2,1,0:T(8,128)(2,1)S(1)} %collective-permute-done.12.y_near, bf16[8,64,128]{2,1,0:T(8,128)(2,1)S(1)} %broadcast_select_fusion.1.y_far, bf16[3,3,3,256,128]{4,3,2,1,0:T(8,128)(2,1)S(1)} %copy-done.3), custom_call_target="tpu_custom_call" | custom-call | flops 2000000000 | bytes 1048576 | tf_op jit(solution)/shard_map/decode_skip/pallas_call | solution.py:319
  33.6 0.3 collective-permute-start.14
  33.9 2.1 %collective-permute-start.15 = (bf16[4,64,128]{2,1,0:T(8,128)(2,1)S(1)}, bf16[4,64,128]{2,1,0:T(8,128)(2,1)S(1)}, u32[]{:S(2)}, u32[]{:S(2)}) collective-permute-start(bf16[4,64,128]{2,1,0:T(8,128)(2,1)S(1)} %get-tuple-element.33), channel_id=1, source_target_pairs={{0,1},{1,0},{2,3},{3,2},{4,5},{5,4},{6,7},{7,6},{8,9},{9,8},{10,11... | collective-permute-start | bytes 196616 | tf_op jit(solution)/shard_map/ppermute | solution.py:361
  36.0 1.3 %collective-permute-done.9 = bf16[8,32,256]{2,1,0:T(8,128)(2,1)S(1)} collective-permute-done((bf16[8,32,256]{2,1,0:T(8,128)(2,1)S(1)}, bf16[8,32,256]{2,1,0:T(8,128)(2,1)S(1)}, u32[]{:S(2)}, u32[]{:S(2)}) %collective-permute-start.9) | collective-permute-done | bytes 131104 | tf_op jit(solution)/shard_map/ppermute | solution.py:344
  37.3 0.9 %second.1.own = bf16[6,32,256]{2,1,0:T(8,128)(2,1)S(1)} custom-call(bf16[8,32,256]{2,1,0:T(8,128)(2,1)S(1)} %first.1.own, bf16[8,32,256]{2,1,0:T(8,128)(2,1)S(1)} %collective-permute-done.8.y1, bf16[8,32,256]{2,1,0:T(8,128)(2,1)S(1)} %broadcast_select_fusion.y2, bf16[3,2304,256]{2,1,0:T(8,128)(2,1)S(1)} %bitcast.24), custom_call_target="tpu_custom_call" | custom-call | flops 700000000 | bytes 1048576 | tf_op jit(solution)/shard_map/second/pallas_call | solution.py:319
  38.3 0.1 collective-permute-start.11
  38.4 2.6 %collective-permute-start.10 = (bf16[6,32,256]{2,1,0:T(8,128)(2,1)S(1)}, bf16[6,32,256]{2,1,0:T(8,128)(2,1)S(1)}, u32[]{:S(2)}, u32[]{:S(2)}) collective-permute-start(bf16[6,32,256]{2,1,0:T(8,128)(2,1)S(1)} %second.1.own), channel_id=1, source_target_pairs={{15,16},{16,15},{17,18},{18,17},{19,20},{20,19},{21,22},{22,21},{2... | collective-permute-start | bytes 294920 | tf_op jit(solution)/shard_map/ppermute | solution.py:344
  41.0 1.8 %decode_own.1.before = f32[2,8,64,128]{3,2,1,0:T(8,128)S(1)} custom-call(bf16[6,32,256]{2,1,0:T(8,128)(2,1)S(1)} %second.1.own, bf16[4,64,128]{2,1,0:T(8,128)(2,1)S(1)} %collective-permute-done.14.x_near, bf16[4,64,128]{2,1,0:T(8,128)(2,1)S(1)} %collective-permute-done.15.x_far, bf16[2,2,2,256,128]{4,3,2,1,0:T(8,128)(2,1)S(1)} %copy-done.6, ...), custom_call_target="tpu_custom_call" | custom-call | flops 2000000000 | bytes 1048576 | tf_op jit(solution)/shard_map/decode_own/pallas_call | solution.py:319
  42.8 0.2 collective-permute-done.11.y_near
  43.0 0.9 %decode_near.1.before = f32[2,8,64,128]{3,2,1,0:T(8,128)S(1)} custom-call(bf16[6,32,256]{2,1,0:T(8,128)(2,1)S(1)} %collective-permute-done.11.y_near, bf16[2,2,2,256,128]{4,3,2,1,0:T(8,128)(2,1)S(1)} %copy-done.6, bf16[3,3,3,256,128]{4,3,2,1,0:T(8,128)(2,1)S(1)} %copy-done.3, f32[2,8,64,128]{3,2,1,0:T(8,128)S(1)} %decode_own.1.before), custom_call_target="tpu_custom_call" | custom-call | flops 1000000000 | bytes 1048576 | tf_op jit(solution)/shard_map/decode_near/pallas_call | solution.py:319
  43.9 2.5 %collective-permute-done.10.y_far = bf16[6,32,256]{2,1,0:T(8,128)(2,1)S(1)} collective-permute-done((bf16[6,32,256]{2,1,0:T(8,128)(2,1)S(1)}, bf16[6,32,256]{2,1,0:T(8,128)(2,1)S(1)}, u32[]{:S(2)}, u32[]{:S(2)}) %collective-permute-start.10) | collective-permute-done | bytes 98336 | tf_op jit(solution)/shard_map/ppermute | solution.py:344
  46.4 1.8 %decode_last.1 = bf16[8,2,64,128]{3,2,1,0:T(8,128)(2,1)} custom-call(bf16[6,32,256]{2,1,0:T(8,128)(2,1)S(1)} %collective-permute-done.10.y_far, bf16[2,2,2,256,128]{4,3,2,1,0:T(8,128)(2,1)S(1)} %copy-done.6, bf16[3,3,3,256,128]{4,3,2,1,0:T(8,128)(2,1)S(1)} %copy-done.3, f32[2,8,64,128]{3,2,1,0:T(8,128)S(1)} %decode_near.1.before), custom_call_target="tpu_custom_call" | custom-call | flops 1000000000 | bytes 1048576 | tf_op jit(solution)/shard_map/decode_last/pallas_call | solution.py:319
  (40 shorter events, 0.4 us)
Async XLA Ops:
  0.0 0.9 %copy-start.2 = (bf16[8,2,64,128]{3,2,1,0:T(8,128)(2,1)S(1)}, bf16[8,2,64,128]{3,2,1,0:T(8,128)(2,1)}, u32[]{:S(2)}) copy-start(bf16[8,2,64,128]{3,2,1,0:T(8,128)(2,1)} %volume.1) | copy-start | bytes 786436
  1.0 8.6 %collective-permute-start.1 = (bf16[8,64,128]{2,1,0:T(8,128)(2,1)S(1)}, bf16[8,64,128]{2,1,0:T(8,128)(2,1)S(1)}, u32[]{:S(2)}, u32[]{:S(2)}) collective-permute-start(bf16[8,64,128]{2,1,0:T(8,128)(2,1)S(1)} %get-tuple-element.21), channel_id=1, source_target_pairs={{15,16},{16,15},{17,18},{18,17},{19,20},{20,19},{21,22},{22,21},{2... | collective-permute-start | bytes 393224 | tf_op jit(solution)/shard_map/ppermute | solution.py:344
  3.7 6.0 %collective-permute-start = (bf16[8,64,128]{2,1,0:T(8,128)(2,1)S(1)}, bf16[8,64,128]{2,1,0:T(8,128)(2,1)S(1)}, u32[]{:S(2)}, u32[]{:S(2)}) collective-permute-start(bf16[8,64,128]{2,1,0:T(8,128)(2,1)S(1)} %get-tuple-element.20), channel_id=1, source_target_pairs={{0,1},{1,0},{2,3},{3,2},{4,5},{5,4},{6,7},{7,6},{8,9},{9,8},{10,11... | collective-permute-start | bytes 393224 | tf_op jit(solution)/shard_map/ppermute | solution.py:343
  4.3 1.2 %copy-start.4 = (bf16[3,3,3,128,128]{4,3,2,1,0:T(8,128)(2,1)S(1)}, bf16[3,3,3,128,128]{4,3,2,1,0:T(8,128)(2,1)}, u32[]{:S(2)}) copy-start(bf16[3,3,3,128,128]{4,3,2,1,0:T(8,128)(2,1)} %param.8) | copy-start | bytes 2654212
  6.6 7.5 %copy-start.5 = (bf16[2,2,2,128,256]{4,3,2,1,0:T(8,128)(2,1)S(1)}, bf16[2,2,2,128,256]{4,3,2,1,0:T(8,128)(2,1)}, u32[]{:S(2)}) copy-start(bf16[2,2,2,128,256]{4,3,2,1,0:T(8,128)(2,1)} %down.1) | copy-start | bytes 1572868
  9.7 4.4 %collective-permute-start.3 = (bf16[4,64,128]{2,1,0:T(8,128)(2,1)S(1)}, bf16[4,64,128]{2,1,0:T(8,128)(2,1)S(1)}, u32[]{:S(2)}, u32[]{:S(2)}) collective-permute-start(bf16[4,64,128]{2,1,0:T(8,128)(2,1)S(1)} %pad_maximum_fusion.3), channel_id=1, source_target_pairs={{0,1},{1,0},{2,3},{3,2},{4,5},{5,4},{6,7},{7,6},{8,9},{9,8},{10,11... | collective-permute-start | bytes 196616 | tf_op jit(solution)/shard_map/ppermute | solution.py:361
  9.9 4.2 %collective-permute-start.2 = (bf16[4,64,128]{2,1,0:T(8,128)(2,1)S(1)}, bf16[4,64,128]{2,1,0:T(8,128)(2,1)S(1)}, u32[]{:S(2)}, u32[]{:S(2)}) collective-permute-start(bf16[4,64,128]{2,1,0:T(8,128)(2,1)S(1)} %pad_maximum_fusion.2), channel_id=1, source_target_pairs={{0,32},{32,0},{64,96},{96,64},{128,160},{160,128},{192,224},{224,1... | collective-permute-start | bytes 196616 | tf_op jit(solution)/shard_map/ppermute | solution.py:360
  12.5 15.3 %copy-start = (bf16[3,3,3,256,256]{4,3,2,1,0:T(8,128)(2,1)S(1)}, bf16[3,3,3,256,256]{4,3,2,1,0:T(8,128)(2,1)}, u32[]{:S(2)}) copy-start(bf16[3,3,3,256,256]{4,3,2,1,0:T(8,128)(2,1)} %param.10) | copy-start | bytes 10616836
  14.8 7.7 %collective-permute-start.5 = (bf16[4,32,256]{2,1,0:T(8,128)(2,1)S(1)}, bf16[4,32,256]{2,1,0:T(8,128)(2,1)S(1)}, u32[]{:S(2)}, u32[]{:S(2)}) collective-permute-start(bf16[4,32,256]{2,1,0:T(8,128)(2,1)S(1)} %get-tuple-element.27.own), channel_id=1, source_target_pairs={{15,16},{16,15},{17,18},{18,17},{19,20},{20,19},{21,22},{22,21},{2... | collective-permute-start | bytes 196616 | tf_op jit(solution)/shard_map/ppermute | solution.py:344
  17.4 5.0 %collective-permute-start.4 = (bf16[4,32,256]{2,1,0:T(8,128)(2,1)S(1)}, bf16[4,32,256]{2,1,0:T(8,128)(2,1)S(1)}, u32[]{:S(2)}, u32[]{:S(2)}) collective-permute-start(bf16[4,32,256]{2,1,0:T(8,128)(2,1)S(1)} %get-tuple-element.27.own), channel_id=1, source_target_pairs={{0,1},{1,0},{2,3},{3,2},{4,5},{5,4},{6,7},{7,6},{8,9},{9,8},{10,11... | collective-permute-start | bytes 196616 | tf_op jit(solution)/shard_map/ppermute | solution.py:343
  17.4 14.2 %copy-start.3 = (bf16[3,3,3,256,128]{4,3,2,1,0:T(8,128)(2,1)S(1)}, bf16[3,3,3,256,128]{4,3,2,1,0:T(8,128)(2,1)}, u32[]{:S(2)}) copy-start(bf16[3,3,3,256,128]{4,3,2,1,0:T(8,128)(2,1)} %weight.7) | copy-start | bytes 5308420
  17.4 8.4 %collective-permute-start.13 = (bf16[8,64,128]{2,1,0:T(8,128)(2,1)S(1)}, bf16[8,64,128]{2,1,0:T(8,128)(2,1)S(1)}, u32[]{:S(2)}, u32[]{:S(2)}) collective-permute-start(bf16[8,64,128]{2,1,0:T(8,128)(2,1)S(1)} %get-tuple-element.42), channel_id=1, source_target_pairs={{15,16},{16,15},{17,18},{18,17},{19,20},{20,19},{21,22},{22,21},{2... | collective-permute-start | bytes 393224 | tf_op jit(solution)/shard_map/ppermute | solution.py:344
  20.3 5.5 %collective-permute-start.12 = (bf16[8,64,128]{2,1,0:T(8,128)(2,1)S(1)}, bf16[8,64,128]{2,1,0:T(8,128)(2,1)S(1)}, u32[]{:S(2)}, u32[]{:S(2)}) collective-permute-start(bf16[8,64,128]{2,1,0:T(8,128)(2,1)S(1)} %get-tuple-element.41), channel_id=1, source_target_pairs={{0,1},{1,0},{2,3},{3,2},{4,5},{5,4},{6,7},{7,6},{8,9},{9,8},{10,11... | collective-permute-start | bytes 393224 | tf_op jit(solution)/shard_map/ppermute | solution.py:343
  22.6 5.2 %collective-permute-start.7 = (bf16[3,3,32,256]{3,2,1,0:T(8,128)(2,1)S(1)}, bf16[3,3,32,256]{3,2,1,0:T(8,128)(2,1)S(1)}, u32[]{:S(2)}, u32[]{:S(2)}) collective-permute-start(bf16[3,3,32,256]{3,2,1,0:T(8,128)(2,1)S(1)} %pad_maximum_fusion.1), channel_id=1, source_target_pairs={{0,1},{1,0},{2,3},{3,2},{4,5},{5,4},{6,7},{7,6},{8,9},{9,8},{10,11... | collective-permute-start | bytes 442376 | tf_op jit(solution)/shard_map/ppermute | solution.py:361
  22.7 5.1 %collective-permute-start.6 = (bf16[3,3,32,256]{3,2,1,0:T(8,128)(2,1)S(1)}, bf16[3,3,32,256]{3,2,1,0:T(8,128)(2,1)S(1)}, u32[]{:S(2)}, u32[]{:S(2)}) collective-permute-start(bf16[3,3,32,256]{3,2,1,0:T(8,128)(2,1)S(1)} %pad_maximum_fusion), channel_id=1, source_target_pairs={{0,32},{32,0},{64,96},{96,64},{128,160},{160,128},{192,224},{224,1... | collective-permute-start | bytes 442376 | tf_op jit(solution)/shard_map/ppermute | solution.py:360
  28.9 8.4 %copy-start.1 = (bf16[3,3,3,256,256]{4,3,2,1,0:T(8,128)(2,1)S(1)}, bf16[3,3,3,256,256]{4,3,2,1,0:T(8,128)(2,1)}, u32[]{:S(2)}) copy-start(bf16[3,3,3,256,256]{4,3,2,1,0:T(8,128)(2,1)} %param.11) | copy-start | bytes 10616836
  28.9 8.4 %collective-permute-start.9 = (bf16[8,32,256]{2,1,0:T(8,128)(2,1)S(1)}, bf16[8,32,256]{2,1,0:T(8,128)(2,1)S(1)}, u32[]{:S(2)}, u32[]{:S(2)}) collective-permute-start(bf16[8,32,256]{2,1,0:T(8,128)(2,1)S(1)} %first.1.own), channel_id=1, source_target_pairs={{15,16},{16,15},{17,18},{18,17},{19,20},{20,19},{21,22},{22,21},{2... | collective-permute-start | bytes 393224 | tf_op jit(solution)/shard_map/ppermute | solution.py:344
  31.6 5.8 %collective-permute-start.8 = (bf16[8,32,256]{2,1,0:T(8,128)(2,1)S(1)}, bf16[8,32,256]{2,1,0:T(8,128)(2,1)S(1)}, u32[]{:S(2)}, u32[]{:S(2)}) collective-permute-start(bf16[8,32,256]{2,1,0:T(8,128)(2,1)S(1)} %first.1.own), channel_id=1, source_target_pairs={{0,1},{1,0},{2,3},{3,2},{4,5},{5,4},{6,7},{7,6},{8,9},{9,8},{10,11... | collective-permute-start | bytes 393224 | tf_op jit(solution)/shard_map/ppermute | solution.py:343
  33.6 7.4 %copy-start.6 = (bf16[2,2,2,256,128]{4,3,2,1,0:T(8,128)(2,1)S(1)}, bf16[2,2,2,256,128]{4,3,2,1,0:T(8,128)(2,1)}, u32[]{:S(2)}) copy-start(bf16[2,2,2,256,128]{4,3,2,1,0:T(8,128)(2,1)} %up.5) | copy-start | bytes 1572868
  33.6 7.4 %collective-permute-start.14 = (bf16[4,64,128]{2,1,0:T(8,128)(2,1)S(1)}, bf16[4,64,128]{2,1,0:T(8,128)(2,1)S(1)}, u32[]{:S(2)}, u32[]{:S(2)}) collective-permute-start(bf16[4,64,128]{2,1,0:T(8,128)(2,1)S(1)} %get-tuple-element.32), channel_id=1, source_target_pairs={{0,32},{32,0},{64,96},{96,64},{128,160},{160,128},{192,224},{224,1... | collective-permute-start | bytes 196616 | tf_op jit(solution)/shard_map/ppermute | solution.py:360
  33.9 7.2 %collective-permute-start.15 = (bf16[4,64,128]{2,1,0:T(8,128)(2,1)S(1)}, bf16[4,64,128]{2,1,0:T(8,128)(2,1)S(1)}, u32[]{:S(2)}, u32[]{:S(2)}) collective-permute-start(bf16[4,64,128]{2,1,0:T(8,128)(2,1)S(1)} %get-tuple-element.33), channel_id=1, source_target_pairs={{0,1},{1,0},{2,3},{3,2},{4,5},{5,4},{6,7},{7,6},{8,9},{9,8},{10,11... | collective-permute-start | bytes 196616 | tf_op jit(solution)/shard_map/ppermute | solution.py:361
  38.3 4.7 %collective-permute-start.11 = (bf16[6,32,256]{2,1,0:T(8,128)(2,1)S(1)}, bf16[6,32,256]{2,1,0:T(8,128)(2,1)S(1)}, u32[]{:S(2)}, u32[]{:S(2)}) collective-permute-start(bf16[6,32,256]{2,1,0:T(8,128)(2,1)S(1)} %second.1.own), channel_id=1, source_target_pairs={{0,1},{1,0},{2,3},{3,2},{4,5},{5,4},{6,7},{7,6},{8,9},{9,8},{10,11... | collective-permute-start | bytes 294920 | tf_op jit(solution)/shard_map/ppermute | solution.py:343
  38.4 8.0 %collective-permute-start.10 = (bf16[6,32,256]{2,1,0:T(8,128)(2,1)S(1)}, bf16[6,32,256]{2,1,0:T(8,128)(2,1)S(1)}, u32[]{:S(2)}, u32[]{:S(2)}) collective-permute-start(bf16[6,32,256]{2,1,0:T(8,128)(2,1)S(1)} %second.1.own), channel_id=1, source_target_pairs={{15,16},{16,15},{17,18},{18,17},{19,20},{20,19},{21,22},{22,21},{2... | collective-permute-start | bytes 294920 | tf_op jit(solution)/shard_map/ppermute | solution.py:344

commit v4 on v3

v4 whole, which is shorter than its diff:
```python
import jax
import jax.numpy as jnp
from jax import lax
from jax.experimental import pallas as pl
from jax.experimental.pallas import tpu as pltpu
from jax.sharding import PartitionSpec as P

BF = jnp.bfloat16
F32 = jnp.float32
LIMIT = 20 * 1024 * 1024


def leaky_unit(values):
    return jnp.where(values > 0, values, 0.1 * values)


def depth_sum(before, here, after, depth):
    at = lax.rem(lax.broadcasted_iota(jnp.int32, here.shape, 0), depth)
    count = here.shape[0]
    before = jnp.where(at == 0, 0.0, pltpu.roll(before, 1, axis=0))
    after = jnp.where(at == depth - 1, 0.0, pltpu.roll(after, count - 1, axis=0))
    return before + here + after


def three_rows(cells, first, rows):
    lanes = cells.shape[2]
    return jnp.concatenate(
        [
            cells[first + off : first + off + rows].reshape(rows * cells.shape[1], lanes)
            for off in range(3)
        ],
        axis=1,
    )


def own_sum(cells, part):
    left = three_rows(cells, 0, 8)
    products = []
    for d in range(3):
        blocks = []
        for off in range(3):
            blocks.append(jnp.concatenate([part(off, 1, d), part(off, 0, d)], axis=1))
            blocks.append(jnp.concatenate([part(off, 2, d), part(off, 1, d)], axis=1))
        products.append(
            jnp.dot(left, jnp.concatenate(blocks, axis=0), preferred_element_type=F32)
        )
    return depth_sum(*products, 64)


def taps_sum(left, blocks):
    right = jnp.concatenate([jnp.concatenate(parts, axis=0) for parts in blocks], axis=1)
    products = jnp.dot(left, right, preferred_element_type=F32)
    return depth_sum(*[products[:, d * 128 : d * 128 + 128] for d in range(3)], 64)


def side_sum(cells, part, side, first=0, rows=8):
    blocks = [[part(off, 2 * side, d) for off in range(3)] for d in range(3)]
    return taps_sum(three_rows(cells, first, rows), blocks).reshape(rows, 64, 128)


def add_rows(total, x_near, x_far, part):
    gx, nx = lax.axis_index("gx"), lax.axis_size("gx")
    odd_x = lax.rem(gx, 2)
    for cells, high, ok in ((x_near, 1 - odd_x, None), (x_far, odd_x, (gx > 0) & (gx < nx - 1))):
        for b in range(2):
            left = jnp.concatenate([cells[b + col] for col in range(3)], axis=1)
            blocks = [[part(2 * high, col, d) for col in range(3)] for d in range(3)]
            values = taps_sum(left, blocks)
            total[b, 7 * high] += values if ok is None else jnp.where(ok, values, 0.0)


def sides():
    odd = lax.rem(lax.axis_index("gy"), 2)
    return 1 - odd, odd


def clear_ends(cells):
    cells[0] = jnp.zeros_like(cells[0])
    cells[9] = jnp.zeros_like(cells[9])


def put_own(cells, own):
    clear_ends(cells)
    for b in range(2):
        cells[1:9, :, b * 128 : b * 128 + 128] = own[:, b]


def put_total(total, values):
    for b in range(2):
        total[b] = values[:, b * 128 : b * 128 + 128].reshape(8, 64, 128)


def prep_kernel(volume, own, near, far, edge_near, edge_far, sem):
    copy = pltpu.make_async_copy(volume, own, sem)
    copy.start()
    odd_x, odd_y = lax.rem(lax.axis_index("gx"), 2), lax.rem(lax.axis_index("gy"), 2)
    copy.wait()
    near[...] = own[:, 1 - odd_y]
    far[...] = own[:, odd_y]
    edge_near[...] = own[7 * (1 - odd_x)]
    edge_far[...] = own[7 * odd_x]


def entry_own_kernel(own, weight, total, cells):
    put_own(cells, own)
    put_total(total, own_sum(cells, lambda off, col, d: weight[off, col, d]))


def entry_side_kernel(y_near, y_far, weight, before, total, near, far):
    part = lambda off, col, d: weight[off, col, d]
    for cells, source, side in zip((near, far), (y_near, y_far), sides()):
        clear_ends(cells)
        cells[1:9] = source[...]
        total[side] = before[side] + side_sum(cells, part, side)


def entry_last_kernel(x_near, x_far, weight, down, before, encoded, coarse, fine, total):
    total[:, 0] = before[:, 0]
    total[:, 7] = before[:, 7]
    add_rows(total, x_near, x_far, lambda off, col, d: weight[off, col, d])

    def finish(row, source):
        for b in range(2):
            half = leaky_unit(source[b, row]).astype(BF)
            encoded[row, b] = half
            fine[row, b] = half.astype(F32)

    for row in range(1, 7):
        finish(row, before)
    finish(0, total)
    finish(7, total)
    small = jnp.zeros((128, 256), F32)
    for a in range(2):
        for d in range(2):
            cells = jnp.concatenate(
                [
                    jnp.concatenate(
                        [fine[2 * i + a, b, pl.ds(d, 32, stride=2), :] for b in range(2)], axis=1
                    )
                    for i in range(4)
                ],
                axis=0,
            ).astype(BF)
            small = small + jnp.dot(
                cells, down[a, :, d].reshape(256, 256), preferred_element_type=F32
            )
    coarse[...] = leaky_unit(small).astype(BF).reshape(4, 32, 256)


def deep_conv(rows, beyond, cells, weight, out):
    left = jnp.concatenate(
        [
            cells[plane, off : off + rows].reshape(rows * 32, 256)
            for off in range(3)
            for plane in range(3)
        ],
        axis=1,
    )
    products = [
        jnp.dot(left, weight[:, :, d].reshape(2304, 256), preferred_element_type=F32)
        for d in range(3)
    ]
    result = leaky_unit(depth_sum(*products, 32)).reshape(rows, 32, 256)
    gx, nx = lax.axis_index("gx"), lax.axis_size("gx")
    out[0:beyond] = jnp.where(gx > 0, result[0:beyond], 0.0).astype(BF)
    out[beyond : rows - beyond] = result[beyond : rows - beyond].astype(BF)
    out[rows - beyond :] = jnp.where(gx < nx - 1, result[rows - beyond :], 0.0).astype(BF)


def first_kernel(own, y_near, y_far, x_near, x_far, weight, out, cells):
    side_near, side_far = sides()
    gx, nx = lax.axis_index("gx"), lax.axis_size("gx")
    odd_x = lax.rem(gx, 2)
    cells[1, 3:7] = own[...]
    cells[2 * side_near, 3:7] = y_near[...]
    cells[2 * side_far, 3:7] = y_far[...]
    for plane in range(3):
        cells[plane, pl.ds(7 * (1 - odd_x), 3)] = x_near[:, plane]
        cells[plane, pl.ds(7 * odd_x, 3)] = jnp.where(
            (gx > 0) & (gx < nx - 1), x_far[:, plane].astype(F32), 0.0
        ).astype(BF)
    deep_conv(8, 2, cells, weight, out)


def deep_sum(planes, at, weight):
    left = jnp.concatenate([three_rows(p, 0, p.shape[0] - 2) for p in planes], axis=1)
    products = [
        jnp.dot(
            left,
            jnp.concatenate([weight[:, place, d].reshape(768, 256) for place in at], axis=0),
            preferred_element_type=F32,
        )
        for d in range(3)
    ]
    return depth_sum(*products, 32)


def second_own_kernel(own, y_near, weight, total):
    side, _ = sides()
    total[...] = deep_sum((own, y_near), (1, 2 * side), weight)


def second_far_kernel(y_far, weight, before, out):
    _, side = sides()
    gx, nx = lax.axis_index("gx"), lax.axis_size("gx")
    gy, ny = lax.axis_index("gy"), lax.axis_size("gy")
    far = jnp.where((gy > 0) & (gy < ny - 1), deep_sum((y_far,), (2 * side,), weight), 0.0)
    result = leaky_unit(before[...] + far).reshape(6, 32, 256)
    out[0] = jnp.where(gx > 0, result[0], 0.0).astype(BF)
    out[1:5] = result[1:5].astype(BF)
    out[5] = jnp.where(gx < nx - 1, result[5], 0.0).astype(BF)


def half_weights(weight, half):
    return lambda off, col, d: weight[off, col, d, half * 128 : half * 128 + 128]


def lift(cells, up, b, upward, col):
    for a in range(2):
        for d in range(2):
            part = leaky_unit(jnp.dot(cells, up[a, b, d], preferred_element_type=F32))
            part = part.reshape(6, 32, 128)
            for i in range(6):
                row = 2 * i + a - 1
                if 0 <= row < 10:
                    upward[row, col, pl.ds(d, 32, stride=2), :] = part[i]


def decode_skip_kernel(encoded, y_near, y_far, weight, total, own, near, far):
    part = half_weights(weight, 1)
    put_own(own, encoded)
    put_total(total, own_sum(own, part))
    for cells, source, side in zip((near, far), (y_near, y_far), sides()):
        clear_ends(cells)
        cells[1:9] = source[...]
        total[side] += side_sum(cells, part, side)


def decode_own_kernel(own, x_near, x_far, up, weight, before, total, cells, upward):
    lift(own[...].reshape(192, 256), up, 0, upward, 0)
    lift(own[...].reshape(192, 256), up, 1, upward, 1)
    for b in range(2):
        cells[:, :, b * 128 : b * 128 + 128] = upward[:, b].astype(BF)
    values = own_sum(cells, half_weights(weight, 0))
    for b in range(2):
        total[b] = before[b] + values[:, b * 128 : b * 128 + 128].reshape(8, 64, 128)
    add_rows(total, x_near, x_far, half_weights(weight, 1))


def decode_near_kernel(y_near, up, weight, before, decoded, cells, upward, column, sem):
    side, _ = sides()
    lift(y_near[...].reshape(192, 256), up, 1 - side, upward, 0)
    cells[...] = upward[:, 0].astype(BF)
    values = before[side] + side_sum(cells, half_weights(weight, 0), side)
    column[...] = leaky_unit(values).astype(BF)
    copy = pltpu.make_async_copy(column, decoded.at[:, side], sem)
    copy.start()
    copy.wait()


def decode_last_kernel(y_far, up, weight, before, _, decoded, cells, upward, column, sems):
    _, side = sides()
    gy, ny = lax.axis_index("gy"), lax.axis_size("gy")
    lift(y_far[...].reshape(192, 256), up, 1 - side, upward, 0)
    cells[...] = jnp.where((gy > 0) & (gy < ny - 1), upward[:, 0], 0.0).astype(BF)
    copies = []
    for half in range(2):
        rows = slice(4 * half, 4 * half + 4)
        values = before[side, rows] + side_sum(cells, half_weights(weight, 0), side, 4 * half, 4)
        column[rows] = leaky_unit(values).astype(BF)
        copies.append(
            pltpu.make_async_copy(column.at[rows], decoded.at[rows, side], sems.at[half])
        )
        copies[-1].start()
    for copy in copies:
        copy.wait()


def call(kernel, outs, scratch, name, flops, *operands, remote=(), hbm_out=False, aliases=()):
    vmem = pl.BlockSpec(memory_space=pltpu.VMEM)
    hbm = pl.BlockSpec(memory_space=pltpu.HBM)
    return pl.pallas_call(
        kernel,
        out_shape=[jax.ShapeDtypeStruct(shape, dtype) for shape, dtype in outs],
        in_specs=[hbm if i in remote else vmem for i in range(len(operands))],
        out_specs=[hbm if hbm_out else vmem] * len(outs),
        scratch_shapes=[
            pltpu.SemaphoreType.DMA(shape) if dtype is None else pltpu.VMEM(shape, dtype)
            for shape, dtype in scratch
        ],
        compiler_params=pltpu.CompilerParams(vmem_limit_bytes=LIMIT),
        cost_estimate=pl.CostEstimate(flops=flops, bytes_accessed=1 << 20, transcendentals=0),
        input_output_aliases=dict(aliases),
        name=name,
    )(*operands)


def swap_y(near_cells, far_cells, far_first=True):
    nx, ny = lax.axis_size("gx"), lax.axis_size("gy")
    near = [(i, i ^ 1) for i in range(ny)]
    far = []
    for x in range(nx):
        for y in range(ny):
            to = (x ^ 1) * ny + y if y in (0, ny - 1) else x * ny + ((y + 1) ^ 1) - 1
            far.append((x * ny + y, to))
    far = far[ny // 2 - 1 :] + far[: ny // 2 - 1]
    got = lax.ppermute(near_cells, "gy", near)
    there = lax.ppermute(far_cells, ("gx", "gy"), far)
    if far_first:
        at = lax.axis_index("gy")
        there = jnp.where((at > 0) & (at < ny - 1), there, jnp.zeros_like(there))
        there = lax.optimization_barrier(there)
    return got, there


def swap_x(near_cells, far_cells):
    nx, ny = lax.axis_size("gx"), lax.axis_size("gy")
    near = [(i, i ^ 1) for i in range(nx)]
    far = []
    for x in range(nx):
        for y in range(ny):
            idle = y ^ 4 if ny >= 8 else y ^ 1
            to = x * ny + idle if x in (0, nx - 1) else (((x + 1) ^ 1) - 1) * ny + y
            far.append((x * ny + y, to))
    got = lax.ppermute(near_cells, "gx", near)
    return got, lax.ppermute(far_cells, ("gx", "gy"), far)


def local(
    volume,
    weight_entry,
    weight_down,
    weight_deep_first,
    weight_deep_second,
    weight_upward,
    weight_decoder,
):
    odd_x = lax.rem(lax.axis_index("gx"), 2)
    odd_y = lax.rem(lax.axis_index("gy"), 2)

    def column(array, at):
        return lax.dynamic_index_in_dim(array, at, axis=1, keepdims=False)

    def rows(array, at, count):
        return lax.dynamic_slice_in_dim(array, at, count, axis=0)

    def four_columns(pair, y_near, y_far, at):
        near, far = rows(y_near, at, 1), rows(y_far, at, 1)
        low = jnp.where(odd_y == 1, near, far)
        high = jnp.where(odd_y == 1, far, near)
        return jnp.concatenate([low, pair, high], axis=0)

    at_near, at_far = 7 * (1 - odd_x), 7 * odd_x
    sums = ((2, 8, 64, 128), F32)
    line = ((8, 64, 128), BF)
    tall = ((10, 64, 128), BF)
    wide = ((10, 64, 256), BF)
    own, near, far, edge_near, edge_far = call(
        prep_kernel,
        [((8, 2, 64, 128), BF), line, line, ((2, 64, 128), BF), ((2, 64, 128), BF)],
        [((), None)],
        "prep",
        1_000_000,
        volume,
        remote=(0,),
    )
    y1, y2 = swap_y(near, far)
    (total,) = call(
        entry_own_kernel, [sums], [wide], "entry_own", 2_000_000_000, own, weight_entry
    )
    x1, x2 = swap_x(
        four_columns(edge_near, y1, y2, at_near), four_columns(edge_far, y1, y2, at_far)
    )
    (total,) = call(
        entry_side_kernel,
        [sums],
        [tall, tall],
        "entry_side",
        1_000_000_000,
        y1,
        y2,
        weight_entry,
        total,
    )
    encoded, coarse = call(
        entry_last_kernel,
        [((8, 2, 64, 128), BF), ((4, 32, 256), BF)],
        [((8, 2, 64, 128), F32), sums],
        "entry_last",
        1_000_000_000,
        x1,
        x2,
        weight_entry,
        weight_down,
        total,
    )

    g1, g2 = swap_y(column(encoded, 1 - odd_y), column(encoded, odd_y))
    c1, c2 = swap_y(coarse, coarse)
    c_low = jnp.where(odd_y == 1, c1, c2)
    c_high = jnp.where(odd_y == 1, c2, c1)

    def coarse_edge(at):
        return jnp.stack([rows(c_low, at, 3), rows(coarse, at, 3), rows(c_high, at, 3)], axis=1)

    d1, d2 = swap_x(coarse_edge(1 - odd_x), coarse_edge(odd_x))
    (deep_one,) = call(
        first_kernel,
        [((8, 32, 256), BF)],
        [((3, 10, 32, 256), BF)],
        "first",
        1_000_000_000,
        coarse,
        c1,
        c2,
        d1,
        d2,
        weight_deep_first,
    )
    f1, f2 = swap_y(deep_one, deep_one, far_first=False)
    skip, _ = lax.optimization_barrier(((encoded, g1, g2), deep_one))
    (total,) = call(
        decode_skip_kernel,
        [sums],
        [wide, tall, tall],
        "decode_skip",
        2_000_000_000,
        *skip,
        weight_decoder,
    )
    edges = (
        four_columns(rows(encoded, at_near, 1)[0], g1, g2, at_near),
        four_columns(rows(encoded, at_far, 1)[0], g1, g2, at_far),
    )
    edges, total = lax.optimization_barrier((edges, total))
    e1, e2 = swap_x(*edges)
    (part,) = call(
        second_own_kernel,
        [((192, 256), F32)],
        [],
        "second_own",
        700_000_000,
        deep_one,
        f1,
        weight_deep_second,
    )
    (deep_two,) = call(
        second_far_kernel,
        [((6, 32, 256), BF)],
        [],
        "second_far",
        500_000_000,
        f2,
        weight_deep_second,
        part,
    )
    h1, h2 = swap_y(deep_two, deep_two, far_first=False)
    upward = ((10, 1, 64, 128), F32)
    (total,) = call(
        decode_own_kernel,
        [sums],
        [wide, ((10, 2, 64, 128), F32)],
        "decode_own",
        2_000_000_000,
        deep_two,
        e1,
        e2,
        weight_upward,
        weight_decoder,
        total,
    )
    (decoded,) = call(
        decode_near_kernel,
        [((8, 2, 64, 128), BF)],
        [tall, upward, line, ((), None)],
        "decode_near",
        1_000_000_000,
        h1,
        weight_upward,
        weight_decoder,
        total,
        hbm_out=True,
    )
    (decoded,) = call(
        decode_last_kernel,
        [((8, 2, 64, 128), BF)],
        [tall, upward, line, ((2,), None)],
        "decode_last",
        1_000_000_000,
        h2,
        weight_upward,
        weight_decoder,
        total,
        decoded,
        remote=(4,),
        hbm_out=True,
        aliases=((4, 0),),
    )
    return decoded


def solution(mesh):
    return jax.shard_map(
        local,
        mesh=mesh,
        in_specs=(P("gx", "gy", None, None), P(), P(), P(), P(), P(), P()),
        out_specs=P("gx", "gy", None, None),
        check_vma=False,
    )
```

time: 48.3 us -> 47.6 us (0.986)
  waiting for transfers between devices: 14.7 us -> 17.4 us
  starting transfers between devices: 19.5 us -> 17.6 us
  Pallas kernels: 11.3 us -> 9.56 us
    pallas_call x10 -> x11, Pallas kernels: 11.3 us -> 9.56 us  [call(): pl.pallas_call(kernel, out_shape=[jax.ShapeDtypeStruct(shape, dtype) for...]
    ppermute x3, starting transfers between devices: 3.05 us -> 1.44 us  [swap_x(): got = lax.ppermute(near_cells, 'gx', near)]
    ppermute x5, waiting for transfers between devices: 11 us -> 12.4 us  [swap_y(): there = lax.ppermute(far_cells, ('gx', 'gy'), far)]
    ppermute x5, waiting for transfers between devices: 0.19 us -> 1.27 us  [swap_y(): got = lax.ppermute(near_cells, 'gy', near)]
    unnamed x14 -> x16, local copies, waits for them, and re-layouts: 2.15 us -> 2.15 us
  transfers between devices with their start and end apart: 16 -> 16, of which waited for: 8 -> 9; matrix products, arithmetic and copies ran while one was open for 0% -> 0% of each run, Pallas kernels for 16% -> 14%
where the time goes in v4:
time: 47.6 us; the launch traced here: 47.4 us
  starting transfers between devices  17.6 us (37%)
  waiting for transfers between devices  17.4 us (37%)
  Pallas kernels  9.56 us (20%)
  local copies, waits for them, and re-layouts  2.21 us (5%)
    ppermute x5, starting transfers between devices, swap_y(): there = lax.ppermute(far_cells, ('gx', 'gy'), far)  13.4 us
    ppermute x5, waiting for transfers between devices, swap_y(): there = lax.ppermute(far_cells, ('gx', 'gy'), far)  12.4 us
    pallas_call x11, Pallas kernels, call(): pl.pallas_call(kernel, out_shape=[jax.ShapeDtypeStruct(shape, dtype) for...  9.56 us
    ppermute x3, waiting for transfers between devices, swap_x(): return (got, lax.ppermute(far_cells, ('gx', 'gy'), far))  3.76 us
    unnamed x16, local copies, waits for them, and re-layouts  2.15 us
    ppermute x3, starting transfers between devices, swap_x(): return (got, lax.ppermute(far_cells, ('gx', 'gy'), far))  1.94 us
    ppermute x3, starting transfers between devices, swap_x(): got = lax.ppermute(near_cells, 'gx', near)  1.44 us
    ppermute x5, waiting for transfers between devices, swap_y(): got = lax.ppermute(near_cells, 'gy', near)  1.27 us
  transfers between devices with their start and end apart: 16, of which 9 were waited for; matrix products, arithmetic and copies ran while one was open for 0% of the time, Pallas kernels for 14%

profile of v4, /device:TPU:128, one launch (start us, length us, event | category | flops | bytes accessed | tf_op | source)
XLA Modules:
  0.0 47.4 jit_solution(9485568699037219558)
XLA Ops:
  0.0 0.9 %copy-done.2 = bf16[8,2,64,128]{3,2,1,0:T(8,128)(2,1)S(1)} copy-done((bf16[8,2,64,128]{3,2,1,0:T(8,128)(2,1)S(1)}, bf16[8,2,64,128]{3,2,1,0:T(8,128)(2,1)}, u32[]{:S(2)}) %copy-start.2) | copy-done | bytes 262168
  1.0 2.6 %collective-permute-start.1 = (bf16[8,64,128]{2,1,0:T(8,128)(2,1)S(1)}, bf16[8,64,128]{2,1,0:T(8,128)(2,1)S(1)}, u32[]{:S(2)}, u32[]{:S(2)}) collective-permute-start(bf16[8,64,128]{2,1,0:T(8,128)(2,1)S(1)} %get-tuple-element.19), channel_id=1, source_target_pairs={{15,16},{16,15},{17,18},{18,17},{19,20},{20,19},{21,22},{22,21},{2... | collective-permute-start | bytes 393224 | tf_op jit(solution)/shard_map/ppermute | solution.py:308
  3.7 0.6 %collective-permute-start = (bf16[8,64,128]{2,1,0:T(8,128)(2,1)S(1)}, bf16[8,64,128]{2,1,0:T(8,128)(2,1)S(1)}, u32[]{:S(2)}, u32[]{:S(2)}) collective-permute-start(bf16[8,64,128]{2,1,0:T(8,128)(2,1)S(1)} %get-tuple-element.18), channel_id=1, source_target_pairs={{0,1},{1,0},{2,3},{3,2},{4,5},{5,4},{6,7},{7,6},{8,9},{9,8},{10,11... | collective-permute-start | bytes 393224 | tf_op jit(solution)/shard_map/ppermute | solution.py:307
  4.3 1.2 %copy-done.4 = bf16[3,3,3,128,128]{4,3,2,1,0:T(8,128)(2,1)S(1)} copy-done((bf16[3,3,3,128,128]{4,3,2,1,0:T(8,128)(2,1)S(1)}, bf16[3,3,3,128,128]{4,3,2,1,0:T(8,128)(2,1)}, u32[]{:S(2)}) %copy-start.4) | copy-done | bytes 884760
  5.4 0.8 %entry_own.1.before = f32[2,8,64,128]{3,2,1,0:T(8,128)S(1)} custom-call(bf16[8,2,64,128]{3,2,1,0:T(8,128)(2,1)S(1)} %get-tuple-element.22.own, bf16[3,3,3,128,128]{4,3,2,1,0:T(8,128)(2,1)S(1)} %copy-done.4), custom_call_target="tpu_custom_call" | custom-call | flops 2000000000 | bytes 1048576 | tf_op jit(solution)/shard_map/entry_own/pallas_call | solution.py:282
  6.2 3.4 %collective-permute-done.1 = bf16[8,64,128]{2,1,0:T(8,128)(2,1)S(1)} collective-permute-done((bf16[8,64,128]{2,1,0:T(8,128)(2,1)S(1)}, bf16[8,64,128]{2,1,0:T(8,128)(2,1)S(1)}, u32[]{:S(2)}, u32[]{:S(2)}) %collective-permute-start.1) | collective-permute-done | bytes 131104 | tf_op jit(solution)/shard_map/ppermute | solution.py:308
  9.7 0.9 %collective-permute-start.3 = (bf16[4,64,128]{2,1,0:T(8,128)(2,1)S(1)}, bf16[4,64,128]{2,1,0:T(8,128)(2,1)S(1)}, u32[]{:S(2)}, u32[]{:S(2)}) collective-permute-start(bf16[4,64,128]{2,1,0:T(8,128)(2,1)S(1)} %pad_maximum_fusion.3), channel_id=1, source_target_pairs={{0,4},{1,5},{2,6},{3,7},{4,0},{5,1},{6,2},{7,3},{8,12},{9,13},{10,... | collective-permute-start | bytes 196616 | tf_op jit(solution)/shard_map/ppermute | solution.py:326
  10.7 0.8 %collective-permute-start.2 = (bf16[4,64,128]{2,1,0:T(8,128)(2,1)S(1)}, bf16[4,64,128]{2,1,0:T(8,128)(2,1)S(1)}, u32[]{:S(2)}, u32[]{:S(2)}) collective-permute-start(bf16[4,64,128]{2,1,0:T(8,128)(2,1)S(1)} %pad_maximum_fusion.2), channel_id=1, source_target_pairs={{0,32},{32,0},{64,96},{96,64},{128,160},{160,128},{192,224},{224,1... | collective-permute-start | bytes 196616 | tf_op jit(solution)/shard_map/ppermute | solution.py:325
  11.5 0.7 %entry_side.1.before = f32[2,8,64,128]{3,2,1,0:T(8,128)S(1)} custom-call(bf16[8,64,128]{2,1,0:T(8,128)(2,1)S(1)} %collective-permute-done.y_near, bf16[8,64,128]{2,1,0:T(8,128)(2,1)S(1)} %broadcast_select_fusion.1.y_far, bf16[3,3,3,128,128]{4,3,2,1,0:T(8,128)(2,1)S(1)} %copy-done.5, f32[2,8,64,128]{3,2,1,0:T(8,128)S(1)} %entry_own.1.before), custom_call_target="tpu_custom_call" | custom-call | flops 1000000000 | bytes 1048576 | tf_op jit(solution)/shard_map/entry_side/pallas_call | solution.py:282
  12.2 1.9 %collective-permute-done.3.x_far = bf16[4,64,128]{2,1,0:T(8,128)(2,1)S(1)} collective-permute-done((bf16[4,64,128]{2,1,0:T(8,128)(2,1)S(1)}, bf16[4,64,128]{2,1,0:T(8,128)(2,1)S(1)}, u32[]{:S(2)}, u32[]{:S(2)}) %collective-permute-start.3) | collective-permute-done | bytes 65568 | tf_op jit(solution)/shard_map/ppermute | solution.py:326
  14.1 0.7 %entry_last.1 = (bf16[8,2,64,128]{3,2,1,0:T(8,128)(2,1)S(1)}, bf16[4,32,256]{2,1,0:T(8,128)(2,1)S(1)}) custom-call(bf16[4,64,128]{2,1,0:T(8,128)(2,1)S(1)} %collective-permute-done.2.x_near, bf16[4,64,128]{2,1,0:T(8,128)(2,1)S(1)} %collective-permute-done.3.x_far, bf16[3,3,3,128,128]{4,3,2,1,0:T(8,128)(2,1)S(1)} %copy-done.5, ...), custom_call_target="tpu_custom_call" | custom-call | flops 1000000000 | bytes 1048576 | tf_op jit(solution)/shard_map/entry_last/pallas_call | solution.py:282
  14.8 2.6 %collective-permute-start.5 = (bf16[4,32,256]{2,1,0:T(8,128)(2,1)S(1)}, bf16[4,32,256]{2,1,0:T(8,128)(2,1)S(1)}, u32[]{:S(2)}, u32[]{:S(2)}) collective-permute-start(bf16[4,32,256]{2,1,0:T(8,128)(2,1)S(1)} %get-tuple-element.23.own), channel_id=1, source_target_pairs={{15,16},{16,15},{17,18},{18,17},{19,20},{20,19},{21,22},{22,21},{2... | collective-permute-start | bytes 196616 | tf_op jit(solution)/shard_map/ppermute | solution.py:308
  17.4 2.9 %collective-permute-start.12 = (bf16[8,64,128]{2,1,0:T(8,128)(2,1)S(1)}, bf16[8,64,128]{2,1,0:T(8,128)(2,1)S(1)}, u32[]{:S(2)}, u32[]{:S(2)}) collective-permute-start(bf16[8,64,128]{2,1,0:T(8,128)(2,1)S(1)} %get-tuple-element.38), channel_id=1, source_target_pairs={{15,16},{16,15},{17,18},{18,17},{19,20},{20,19},{21,22},{22,21},{2... | collective-permute-start | bytes 393224 | tf_op jit(solution)/shard_map/ppermute | solution.py:308
  20.4 2.1 %collective-permute-done.5 = bf16[4,32,256]{2,1,0:T(8,128)(2,1)S(1)} collective-permute-done((bf16[4,32,256]{2,1,0:T(8,128)(2,1)S(1)}, bf16[4,32,256]{2,1,0:T(8,128)(2,1)S(1)}, u32[]{:S(2)}, u32[]{:S(2)}) %collective-permute-start.5) | collective-permute-done | bytes 65568 | tf_op jit(solution)/shard_map/ppermute | solution.py:308
  22.6 0.7 %collective-permute-start.7 = (bf16[3,3,32,256]{3,2,1,0:T(8,128)(2,1)S(1)}, bf16[3,3,32,256]{3,2,1,0:T(8,128)(2,1)S(1)}, u32[]{:S(2)}, u32[]{:S(2)}) collective-permute-start(bf16[3,3,32,256]{3,2,1,0:T(8,128)(2,1)S(1)} %pad_maximum_fusion.1), channel_id=1, source_target_pairs={{0,4},{1,5},{2,6},{3,7},{4,0},{5,1},{6,2},{7,3},{8,12},{9,13},{10,... | collective-permute-start | bytes 442376 | tf_op jit(solution)/shard_map/ppermute | solution.py:326
  23.3 0.5 %collective-permute-start.6 = (bf16[3,3,32,256]{3,2,1,0:T(8,128)(2,1)S(1)}, bf16[3,3,32,256]{3,2,1,0:T(8,128)(2,1)S(1)}, u32[]{:S(2)}, u32[]{:S(2)}) collective-permute-start(bf16[3,3,32,256]{3,2,1,0:T(8,128)(2,1)S(1)} %pad_maximum_fusion), channel_id=1, source_target_pairs={{0,32},{32,0},{64,96},{96,64},{128,160},{160,128},{192,224},{224,1... | collective-permute-start | bytes 442376 | tf_op jit(solution)/shard_map/ppermute | solution.py:325
  23.8 2.0 %collective-permute-done.12 = bf16[8,64,128]{2,1,0:T(8,128)(2,1)S(1)} collective-permute-done((bf16[8,64,128]{2,1,0:T(8,128)(2,1)S(1)}, bf16[8,64,128]{2,1,0:T(8,128)(2,1)S(1)}, u32[]{:S(2)}, u32[]{:S(2)}) %collective-permute-start.12) | collective-permute-done | bytes 131104 | tf_op jit(solution)/shard_map/ppermute | solution.py:308
  25.9 1.9 %collective-permute-done.7.x_far = bf16[3,3,32,256]{3,2,1,0:T(8,128)(2,1)S(1)} collective-permute-done((bf16[3,3,32,256]{3,2,1,0:T(8,128)(2,1)S(1)}, bf16[3,3,32,256]{3,2,1,0:T(8,128)(2,1)S(1)}, u32[]{:S(2)}, u32[]{:S(2)}) %collective-permute-start.7) | collective-permute-done | bytes 147488 | tf_op jit(solution)/shard_map/ppermute | solution.py:326
  27.8 1.1 %first.1.own = bf16[8,32,256]{2,1,0:T(8,128)(2,1)S(1)} custom-call(bf16[4,32,256]{2,1,0:T(8,128)(2,1)S(1)} %get-tuple-element.23.own, bf16[4,32,256]{2,1,0:T(8,128)(2,1)S(1)} %collective-permute-done.4.y_near, bf16[4,32,256]{2,1,0:T(8,128)(2,1)S(1)} %broadcast_select_fusion.4.y_far, bf16[3,3,32,256]{3,2,1,0:T(8,128)(2,1)S(1)} %collective-permute-done.6.x_near, ...), custom_call_target="tpu_custom_call" | custom-call | flops 1000000000 | bytes 1048576 | tf_op jit(solution)/shard_map/first/pallas_call | solution.py:282
  29.0 2.6 %collective-permute-start.8 = (bf16[8,32,256]{2,1,0:T(8,128)(2,1)S(1)}, bf16[8,32,256]{2,1,0:T(8,128)(2,1)S(1)}, u32[]{:S(2)}, u32[]{:S(2)}) collective-permute-start(bf16[8,32,256]{2,1,0:T(8,128)(2,1)S(1)} %first.1.own), channel_id=1, source_target_pairs={{15,16},{16,15},{17,18},{18,17},{19,20},{20,19},{21,22},{22,21},{2... | collective-permute-start | bytes 393224 | tf_op jit(solution)/shard_map/ppermute | solution.py:308
  31.7 1.3 %decode_skip.1.before = f32[2,8,64,128]{3,2,1,0:T(8,128)S(1)} custom-call(bf16[8,2,64,128]{3,2,1,0:T(8,128)(2,1)S(1)} %get-tuple-element.25.encoded, bf16[8,64,128]{2,1,0:T(8,128)(2,1)S(1)} %collective-permute-done.11.y_near, bf16[8,64,128]{2,1,0:T(8,128)(2,1)S(1)} %broadcast_select_fusion.y_far, bf16[3,3,3,256,128]{4,3,2,1,0:T(8,128)(2,1)S(1)} %copy-done.3), custom_call_target="tpu_custom_call" | custom-call | flops 2000000000 | bytes 1048576 | tf_op jit(solution)/shard_map/decode_skip/pallas_call | solution.py:282
  33.1 0.3 collective-permute-start.14
  33.4 0.6 %collective-permute-done.9.y_near = bf16[8,32,256]{2,1,0:T(8,128)(2,1)S(1)} collective-permute-done((bf16[8,32,256]{2,1,0:T(8,128)(2,1)S(1)}, bf16[8,32,256]{2,1,0:T(8,128)(2,1)S(1)}, u32[]{:S(2)}, u32[]{:S(2)}) %collective-permute-start.9) | collective-permute-done | bytes 131104 | tf_op jit(solution)/shard_map/ppermute | solution.py:307
  34.0 0.6 %second_own.1.before = f32[192,256]{1,0:T(8,128)S(1)} custom-call(bf16[8,32,256]{2,1,0:T(8,128)(2,1)S(1)} %first.1.own, bf16[8,32,256]{2,1,0:T(8,128)(2,1)S(1)} %collective-permute-done.9.y_near, bf16[3,3,3,256,256]{4,3,2,1,0:T(8,128)(2,1)S(1)} %copy-done), custom_call_target="tpu_custom_call" | custom-call | flops 700000000 | bytes 1048576 | tf_op jit(solution)/shard_map/second_own/pallas_call | solution.py:282
  34.6 2.8 %collective-permute-done.8.y_far = bf16[8,32,256]{2,1,0:T(8,128)(2,1)S(1)} collective-permute-done((bf16[8,32,256]{2,1,0:T(8,128)(2,1)S(1)}, bf16[8,32,256]{2,1,0:T(8,128)(2,1)S(1)}, u32[]{:S(2)}, u32[]{:S(2)}) %collective-permute-start.8) | collective-permute-done | bytes 131104 | tf_op jit(solution)/shard_map/ppermute | solution.py:308
  37.4 0.4 second_far.1.own
  38.0 2.6 %collective-permute-start.10 = (bf16[6,32,256]{2,1,0:T(8,128)(2,1)S(1)}, bf16[6,32,256]{2,1,0:T(8,128)(2,1)S(1)}, u32[]{:S(2)}, u32[]{:S(2)}) collective-permute-start(bf16[6,32,256]{2,1,0:T(8,128)(2,1)S(1)} %second_far.1.own), channel_id=1, source_target_pairs={{15,16},{16,15},{17,18},{18,17},{19,20},{20,19},{21,22},{22,21},{2... | collective-permute-start | bytes 294920 | tf_op jit(solution)/shard_map/ppermute | solution.py:308
  40.6 1.3 %decode_own.1.before = f32[2,8,64,128]{3,2,1,0:T(8,128)S(1)} custom-call(bf16[6,32,256]{2,1,0:T(8,128)(2,1)S(1)} %second_far.1.own, bf16[4,64,128]{2,1,0:T(8,128)(2,1)S(1)} %collective-permute-done.13.x_near, bf16[4,64,128]{2,1,0:T(8,128)(2,1)S(1)} %collective-permute-done.14.x_far, bf16[2,2,2,256,128]{4,3,2,1,0:T(8,128)(2,1)S(1)} %copy-done.7, ...), custom_call_target="tpu_custom_call" | custom-call | flops 2000000000 | bytes 1048576 | tf_op jit(solution)/shard_map/decode_own/pallas_call | solution.py:282
  41.9 0.6 %collective-permute-done.15.y_near = bf16[6,32,256]{2,1,0:T(8,128)(2,1)S(1)} collective-permute-done((bf16[6,32,256]{2,1,0:T(8,128)(2,1)S(1)}, bf16[6,32,256]{2,1,0:T(8,128)(2,1)S(1)}, u32[]{:S(2)}, u32[]{:S(2)}) %collective-permute-start.15) | collective-permute-done | bytes 98336 | tf_op jit(solution)/shard_map/ppermute | solution.py:307
  42.6 1.4 %decode_near.1._ = bf16[8,2,64,128]{3,2,1,0:T(8,128)(2,1)} custom-call(bf16[6,32,256]{2,1,0:T(8,128)(2,1)S(1)} %collective-permute-done.15.y_near, bf16[2,2,2,256,128]{4,3,2,1,0:T(8,128)(2,1)S(1)} %copy-done.7, bf16[3,3,3,256,128]{4,3,2,1,0:T(8,128)(2,1)S(1)} %copy-done.3, f32[2,8,64,128]{3,2,1,0:T(8,128)S(1)} %decode_own.1.before), custom_call_target="tpu_custom_call" | custom-call | flops 1000000000 | bytes 1048576 | tf_op jit(solution)/shard_map/decode_near/pallas_call | solution.py:282
  43.9 2.1 %collective-permute-done.10.y_far = bf16[6,32,256]{2,1,0:T(8,128)(2,1)S(1)} collective-permute-done((bf16[6,32,256]{2,1,0:T(8,128)(2,1)S(1)}, bf16[6,32,256]{2,1,0:T(8,128)(2,1)S(1)}, u32[]{:S(2)}, u32[]{:S(2)}) %collective-permute-start.10) | collective-permute-done | bytes 98336 | tf_op jit(solution)/shard_map/ppermute | solution.py:308
  46.0 1.3 %decode_last.1 = bf16[8,2,64,128]{3,2,1,0:T(8,128)(2,1)} custom-call(bf16[6,32,256]{2,1,0:T(8,128)(2,1)S(1)} %collective-permute-done.10.y_far, bf16[2,2,2,256,128]{4,3,2,1,0:T(8,128)(2,1)S(1)} %copy-done.7, bf16[3,3,3,256,128]{4,3,2,1,0:T(8,128)(2,1)S(1)} %copy-done.3, f32[2,8,64,128]{3,2,1,0:T(8,128)S(1)} %decode_own.1.before, ...), custom_call_target="tpu_custom_call", output_to_operand_aliasing={{}: (4, {})} | custom-call | flops 1000000000 | bytes 1048576 | tf_op jit(solution)/shard_map/decode_last/pallas_call | solution.py:282
  (42 shorter events, 0.6 us)
Async XLA Ops:
  0.0 0.9 %copy-start.2 = (bf16[8,2,64,128]{3,2,1,0:T(8,128)(2,1)S(1)}, bf16[8,2,64,128]{3,2,1,0:T(8,128)(2,1)}, u32[]{:S(2)}) copy-start(bf16[8,2,64,128]{3,2,1,0:T(8,128)(2,1)} %volume.1) | copy-start | bytes 786436
  1.0 8.6 %collective-permute-start.1 = (bf16[8,64,128]{2,1,0:T(8,128)(2,1)S(1)}, bf16[8,64,128]{2,1,0:T(8,128)(2,1)S(1)}, u32[]{:S(2)}, u32[]{:S(2)}) collective-permute-start(bf16[8,64,128]{2,1,0:T(8,128)(2,1)S(1)} %get-tuple-element.19), channel_id=1, source_target_pairs={{15,16},{16,15},{17,18},{18,17},{19,20},{20,19},{21,22},{22,21},{2... | collective-permute-start | bytes 393224 | tf_op jit(solution)/shard_map/ppermute | solution.py:308
  3.7 6.0 %collective-permute-start = (bf16[8,64,128]{2,1,0:T(8,128)(2,1)S(1)}, bf16[8,64,128]{2,1,0:T(8,128)(2,1)S(1)}, u32[]{:S(2)}, u32[]{:S(2)}) collective-permute-start(bf16[8,64,128]{2,1,0:T(8,128)(2,1)S(1)} %get-tuple-element.18), channel_id=1, source_target_pairs={{0,1},{1,0},{2,3},{3,2},{4,5},{5,4},{6,7},{7,6},{8,9},{9,8},{10,11... | collective-permute-start | bytes 393224 | tf_op jit(solution)/shard_map/ppermute | solution.py:307
  4.3 1.2 %copy-start.4 = (bf16[3,3,3,128,128]{4,3,2,1,0:T(8,128)(2,1)S(1)}, bf16[3,3,3,128,128]{4,3,2,1,0:T(8,128)(2,1)}, u32[]{:S(2)}) copy-start(bf16[3,3,3,128,128]{4,3,2,1,0:T(8,128)(2,1)} %weight.12) | copy-start | bytes 2654212
  5.4 6.1 %copy-start.5 = (bf16[3,3,3,128,128]{4,3,2,1,0:T(8,128)(2,1)S(1)}, bf16[3,3,3,128,128]{4,3,2,1,0:T(8,128)(2,1)}, u32[]{:S(2)}) copy-start(bf16[3,3,3,128,128]{4,3,2,1,0:T(8,128)(2,1)} %weight.12) | copy-start | bytes 2654212
  6.2 7.9 %copy-start.6 = (bf16[2,2,2,128,256]{4,3,2,1,0:T(8,128)(2,1)S(1)}, bf16[2,2,2,128,256]{4,3,2,1,0:T(8,128)(2,1)}, u32[]{:S(2)}) copy-start(bf16[2,2,2,128,256]{4,3,2,1,0:T(8,128)(2,1)} %down.1) | copy-start | bytes 1572868
  9.7 4.4 %collective-permute-start.3 = (bf16[4,64,128]{2,1,0:T(8,128)(2,1)S(1)}, bf16[4,64,128]{2,1,0:T(8,128)(2,1)S(1)}, u32[]{:S(2)}, u32[]{:S(2)}) collective-permute-start(bf16[4,64,128]{2,1,0:T(8,128)(2,1)S(1)} %pad_maximum_fusion.3), channel_id=1, source_target_pairs={{0,4},{1,5},{2,6},{3,7},{4,0},{5,1},{6,2},{7,3},{8,12},{9,13},{10,... | collective-permute-start | bytes 196616 | tf_op jit(solution)/shard_map/ppermute | solution.py:326
  10.7 3.4 %collective-permute-start.2 = (bf16[4,64,128]{2,1,0:T(8,128)(2,1)S(1)}, bf16[4,64,128]{2,1,0:T(8,128)(2,1)S(1)}, u32[]{:S(2)}, u32[]{:S(2)}) collective-permute-start(bf16[4,64,128]{2,1,0:T(8,128)(2,1)S(1)} %pad_maximum_fusion.2), channel_id=1, source_target_pairs={{0,32},{32,0},{64,96},{96,64},{128,160},{160,128},{192,224},{224,1... | collective-permute-start | bytes 196616 | tf_op jit(solution)/shard_map/ppermute | solution.py:325
  12.2 15.6 %copy-start.1 = (bf16[3,3,3,256,256]{4,3,2,1,0:T(8,128)(2,1)S(1)}, bf16[3,3,3,256,256]{4,3,2,1,0:T(8,128)(2,1)}, u32[]{:S(2)}) copy-start(bf16[3,3,3,256,256]{4,3,2,1,0:T(8,128)(2,1)} %weight.13) | copy-start | bytes 10616836
  14.8 7.7 %collective-permute-start.5 = (bf16[4,32,256]{2,1,0:T(8,128)(2,1)S(1)}, bf16[4,32,256]{2,1,0:T(8,128)(2,1)S(1)}, u32[]{:S(2)}, u32[]{:S(2)}) collective-permute-start(bf16[4,32,256]{2,1,0:T(8,128)(2,1)S(1)} %get-tuple-element.23.own), channel_id=1, source_target_pairs={{15,16},{16,15},{17,18},{18,17},{19,20},{20,19},{21,22},{22,21},{2... | collective-permute-start | bytes 196616 | tf_op jit(solution)/shard_map/ppermute | solution.py:308
  17.4 5.0 %collective-permute-start.4 = (bf16[4,32,256]{2,1,0:T(8,128)(2,1)S(1)}, bf16[4,32,256]{2,1,0:T(8,128)(2,1)S(1)}, u32[]{:S(2)}, u32[]{:S(2)}) collective-permute-start(bf16[4,32,256]{2,1,0:T(8,128)(2,1)S(1)} %get-tuple-element.23.own), channel_id=1, source_target_pairs={{0,1},{1,0},{2,3},{3,2},{4,5},{5,4},{6,7},{7,6},{8,9},{9,8},{10,11... | collective-permute-start | bytes 196616 | tf_op jit(solution)/shard_map/ppermute | solution.py:307
  17.4 14.2 %copy-start.3 = (bf16[3,3,3,256,128]{4,3,2,1,0:T(8,128)(2,1)S(1)}, bf16[3,3,3,256,128]{4,3,2,1,0:T(8,128)(2,1)}, u32[]{:S(2)}) copy-start(bf16[3,3,3,256,128]{4,3,2,1,0:T(8,128)(2,1)} %weight.19) | copy-start | bytes 5308420
  17.4 8.4 %collective-permute-start.12 = (bf16[8,64,128]{2,1,0:T(8,128)(2,1)S(1)}, bf16[8,64,128]{2,1,0:T(8,128)(2,1)S(1)}, u32[]{:S(2)}, u32[]{:S(2)}) collective-permute-start(bf16[8,64,128]{2,1,0:T(8,128)(2,1)S(1)} %get-tuple-element.38), channel_id=1, source_target_pairs={{15,16},{16,15},{17,18},{18,17},{19,20},{20,19},{21,22},{22,21},{2... | collective-permute-start | bytes 393224 | tf_op jit(solution)/shard_map/ppermute | solution.py:308
  20.3 5.5 %collective-permute-start.11 = (bf16[8,64,128]{2,1,0:T(8,128)(2,1)S(1)}, bf16[8,64,128]{2,1,0:T(8,128)(2,1)S(1)}, u32[]{:S(2)}, u32[]{:S(2)}) collective-permute-start(bf16[8,64,128]{2,1,0:T(8,128)(2,1)S(1)} %get-tuple-element.37), channel_id=1, source_target_pairs={{0,1},{1,0},{2,3},{3,2},{4,5},{5,4},{6,7},{7,6},{8,9},{9,8},{10,11... | collective-permute-start | bytes 393224 | tf_op jit(solution)/shard_map/ppermute | solution.py:307
  22.6 5.2 %collective-permute-start.7 = (bf16[3,3,32,256]{3,2,1,0:T(8,128)(2,1)S(1)}, bf16[3,3,32,256]{3,2,1,0:T(8,128)(2,1)S(1)}, u32[]{:S(2)}, u32[]{:S(2)}) collective-permute-start(bf16[3,3,32,256]{3,2,1,0:T(8,128)(2,1)S(1)} %pad_maximum_fusion.1), channel_id=1, source_target_pairs={{0,4},{1,5},{2,6},{3,7},{4,0},{5,1},{6,2},{7,3},{8,12},{9,13},{10,... | collective-permute-start | bytes 442376 | tf_op jit(solution)/shard_map/ppermute | solution.py:326
  23.3 4.5 %collective-permute-start.6 = (bf16[3,3,32,256]{3,2,1,0:T(8,128)(2,1)S(1)}, bf16[3,3,32,256]{3,2,1,0:T(8,128)(2,1)S(1)}, u32[]{:S(2)}, u32[]{:S(2)}) collective-permute-start(bf16[3,3,32,256]{3,2,1,0:T(8,128)(2,1)S(1)} %pad_maximum_fusion), channel_id=1, source_target_pairs={{0,32},{32,0},{64,96},{96,64},{128,160},{160,128},{192,224},{224,1... | collective-permute-start | bytes 442376 | tf_op jit(solution)/shard_map/ppermute | solution.py:325
  28.9 5.1 %copy-start = (bf16[3,3,3,256,256]{4,3,2,1,0:T(8,128)(2,1)S(1)}, bf16[3,3,3,256,256]{4,3,2,1,0:T(8,128)(2,1)}, u32[]{:S(2)}) copy-start(bf16[3,3,3,256,256]{4,3,2,1,0:T(8,128)(2,1)} %weight.15) | copy-start | bytes 10616836
  28.9 5.1 %collective-permute-start.9 = (bf16[8,32,256]{2,1,0:T(8,128)(2,1)S(1)}, bf16[8,32,256]{2,1,0:T(8,128)(2,1)S(1)}, u32[]{:S(2)}, u32[]{:S(2)}) collective-permute-start(bf16[8,32,256]{2,1,0:T(8,128)(2,1)S(1)} %first.1.own), channel_id=1, source_target_pairs={{0,1},{1,0},{2,3},{3,2},{4,5},{5,4},{6,7},{7,6},{8,9},{9,8},{10,11... | collective-permute-start | bytes 393224 | tf_op jit(solution)/shard_map/ppermute | solution.py:307
  29.0 8.4 %collective-permute-start.8 = (bf16[8,32,256]{2,1,0:T(8,128)(2,1)S(1)}, bf16[8,32,256]{2,1,0:T(8,128)(2,1)S(1)}, u32[]{:S(2)}, u32[]{:S(2)}) collective-permute-start(bf16[8,32,256]{2,1,0:T(8,128)(2,1)S(1)} %first.1.own), channel_id=1, source_target_pairs={{15,16},{16,15},{17,18},{18,17},{19,20},{20,19},{21,22},{22,21},{2... | collective-permute-start | bytes 393224 | tf_op jit(solution)/shard_map/ppermute | solution.py:308
  32.9 7.7 %copy-start.7 = (bf16[2,2,2,256,128]{4,3,2,1,0:T(8,128)(2,1)S(1)}, bf16[2,2,2,256,128]{4,3,2,1,0:T(8,128)(2,1)}, u32[]{:S(2)}) copy-start(bf16[2,2,2,256,128]{4,3,2,1,0:T(8,128)(2,1)} %up.5) | copy-start | bytes 1572868
  33.0 7.6 %collective-permute-start.13 = (bf16[4,64,128]{2,1,0:T(8,128)(2,1)S(1)}, bf16[4,64,128]{2,1,0:T(8,128)(2,1)S(1)}, u32[]{:S(2)}, u32[]{:S(2)}) collective-permute-start(bf16[4,64,128]{2,1,0:T(8,128)(2,1)S(1)} %get-tuple-element.28), channel_id=1, source_target_pairs={{0,32},{32,0},{64,96},{96,64},{128,160},{160,128},{192,224},{224,1... | collective-permute-start | bytes 196616 | tf_op jit(solution)/shard_map/ppermute | solution.py:325
  33.1 7.5 %collective-permute-start.14 = (bf16[4,64,128]{2,1,0:T(8,128)(2,1)S(1)}, bf16[4,64,128]{2,1,0:T(8,128)(2,1)S(1)}, u32[]{:S(2)}, u32[]{:S(2)}) collective-permute-start(bf16[4,64,128]{2,1,0:T(8,128)(2,1)S(1)} %get-tuple-element.29), channel_id=1, source_target_pairs={{0,4},{1,5},{2,6},{3,7},{4,0},{5,1},{6,2},{7,3},{8,12},{9,13},{10,... | collective-permute-start | bytes 196616 | tf_op jit(solution)/shard_map/ppermute | solution.py:326
  37.9 4.7 %collective-permute-start.15 = (bf16[6,32,256]{2,1,0:T(8,128)(2,1)S(1)}, bf16[6,32,256]{2,1,0:T(8,128)(2,1)S(1)}, u32[]{:S(2)}, u32[]{:S(2)}) collective-permute-start(bf16[6,32,256]{2,1,0:T(8,128)(2,1)S(1)} %second_far.1.own), channel_id=1, source_target_pairs={{0,1},{1,0},{2,3},{3,2},{4,5},{5,4},{6,7},{7,6},{8,9},{9,8},{10,11... | collective-permute-start | bytes 294920 | tf_op jit(solution)/shard_map/ppermute | solution.py:307
  38.0 8.0 %collective-permute-start.10 = (bf16[6,32,256]{2,1,0:T(8,128)(2,1)S(1)}, bf16[6,32,256]{2,1,0:T(8,128)(2,1)S(1)}, u32[]{:S(2)}, u32[]{:S(2)}) collective-permute-start(bf16[6,32,256]{2,1,0:T(8,128)(2,1)S(1)} %second_far.1.own), channel_id=1, source_target_pairs={{15,16},{16,15},{17,18},{18,17},{19,20},{20,19},{21,22},{22,21},{2... | collective-permute-start | bytes 294920 | tf_op jit(solution)/shard_map/ppermute | solution.py:308

commit v5 on v4

--- a/solution.py
+++ b/solution.py
@@ -147,39 +147,47 @@
     coarse[...] = leaky_unit(small).astype(BF).reshape(4, 32, 256)
 
 
-def deep_conv(rows, beyond, cells, weight, out):
-    left = jnp.concatenate(
-        [
-            cells[plane, off : off + rows].reshape(rows * 32, 256)
-            for off in range(3)
-            for plane in range(3)
-        ],
-        axis=1,
-    )
-    products = [
-        jnp.dot(left, weight[:, :, d].reshape(2304, 256), preferred_element_type=F32)
-        for d in range(3)
-    ]
-    result = leaky_unit(depth_sum(*products, 32)).reshape(rows, 32, 256)
+def masked_rows(result, beyond, out):
+    rows = out.shape[0]
     gx, nx = lax.axis_index("gx"), lax.axis_size("gx")
     out[0:beyond] = jnp.where(gx > 0, result[0:beyond], 0.0).astype(BF)
     out[beyond : rows - beyond] = result[beyond : rows - beyond].astype(BF)
     out[rows - beyond :] = jnp.where(gx < nx - 1, result[rows - beyond :], 0.0).astype(BF)
 
 
-def first_kernel(own, y_near, y_far, x_near, x_far, weight, out, cells):
-    side_near, side_far = sides()
+def rows_sum(rows, weight, off):
+    left = jnp.concatenate([jnp.concatenate(planes, axis=1) for planes in rows], axis=0)
+    products = [
+        jnp.dot(left, weight[off, :, d].reshape(768, 256), preferred_element_type=F32)
+        for d in range(3)
+    ]
+    return depth_sum(*products, 32).reshape(len(rows), 32, 256)
+
+
+def first_own_kernel(own, y_near, y_far, weight, total, cells):
+    near, far = sides()
+    cells[1] = own[...]
+    cells[2 * near] = y_near[...]
+    cells[2 * far] = y_far[...]
+    rows = [[cells[plane, row] for plane in range(3)] for row in range(4)]
+    total[...] = jnp.zeros_like(total)
+    for off in range(3):
+        total[3 - off : 7 - off] += rows_sum(rows, weight, off)
+
+
+def first_last_kernel(x_near, x_far, weight, before, out, cells, total):
     gx, nx = lax.axis_index("gx"), lax.axis_size("gx")
     odd_x = lax.rem(gx, 2)
-    cells[1, 3:7] = own[...]
-    cells[2 * side_near, 3:7] = y_near[...]
-    cells[2 * side_far, 3:7] = y_far[...]
-    for plane in range(3):
-        cells[plane, pl.ds(7 * (1 - odd_x), 3)] = x_near[:, plane]
-        cells[plane, pl.ds(7 * odd_x, 3)] = jnp.where(
-            (gx > 0) & (gx < nx - 1), x_far[:, plane].astype(F32), 0.0
-        ).astype(BF)
-    deep_conv(8, 2, cells, weight, out)
+    cells[1 - odd_x] = x_near[...]
+    cells[odd_x] = jnp.where((gx > 0) & (gx < nx - 1), x_far[...].astype(F32), 0.0).astype(BF)
+    rows = [[cells[k // 3, k % 3, plane] for plane in range(3)] for k in range(6)]
+    total[...] = before[...]
+    for off in range(3):
+        part = rows_sum(rows[off : off + 4], weight, off)
+        below = 3 - off
+        total[0:below] += part[0:below]
+        total[7 - off : 8] += part[below:]
+    masked_rows(leaky_unit(total[...]), 2, out)
 
 
 def deep_sum(planes, at, weight):
@@ -202,13 +210,9 @@
 
 def second_far_kernel(y_far, weight, before, out):
     _, side = sides()
-    gx, nx = lax.axis_index("gx"), lax.axis_size("gx")
     gy, ny = lax.axis_index("gy"), lax.axis_size("gy")
     far = jnp.where((gy > 0) & (gy < ny - 1), deep_sum((y_far,), (2 * side,), weight), 0.0)
-    result = leaky_unit(before[...] + far).reshape(6, 32, 256)
-    out[0] = jnp.where(gx > 0, result[0], 0.0).astype(BF)
-    out[1:5] = result[1:5].astype(BF)
-    out[5] = jnp.where(gx < nx - 1, result[5], 0.0).astype(BF)
+    masked_rows(leaky_unit(before[...] + far).reshape(6, 32, 256), 1, out)
 
 
 def half_weights(weight, half):
@@ -404,18 +408,27 @@
         return jnp.stack([rows(c_low, at, 3), rows(coarse, at, 3), rows(c_high, at, 3)], axis=1)
 
     d1, d2 = swap_x(coarse_edge(1 - odd_x), coarse_edge(odd_x))
-    (deep_one,) = call(
-        first_kernel,
-        [((8, 32, 256), BF)],
-        [((3, 10, 32, 256), BF)],
-        "first",
-        1_000_000_000,
+    (part,) = call(
+        first_own_kernel,
+        [((8, 32, 256), F32)],
+        [((3, 4, 32, 256), BF)],
+        "first_own",
+        700_000_000,
         coarse,
         c1,
         c2,
+        weight_deep_first,
+    )
+    (deep_one,) = call(
+        first_last_kernel,
+        [((8, 32, 256), BF)],
+        [((2, 3, 3, 32, 256), BF), ((8, 32, 256), F32)],
+        "first_last",
+        1_000_000_000,
         d1,
         d2,
         weight_deep_first,
+        part,
     )
     f1, f2 = swap_y(deep_one, deep_one, far_first=False)
     skip, _ = lax.optimization_barrier(((encoded, g1, g2), deep_one))

time: 47.6 us -> 47.1 us (0.989)
  waiting for transfers between devices: 17.4 us -> 16.8 us
    ppermute x5, waiting for transfers between devices: 12.4 us -> 11.7 us  [swap_y(): there = lax.ppermute(far_cells, ('gx', 'gy'), far)]
    pallas_call x11 -> x12, Pallas kernels: 9.56 us -> 9.77 us  [call(): pl.pallas_call(kernel, out_shape=[jax.ShapeDtypeStruct(shape, dtype) for...]
  transfers between devices with their start and end apart: 16 -> 16, of which waited for: 9 -> 9; matrix products, arithmetic and copies ran while one was open for 0% -> 0% of each run, Pallas kernels for 14% -> 15%
where the time goes in v5:
time: 47.1 us; the launch traced here: 47 us
  starting transfers between devices  17.6 us (37%)
  waiting for transfers between devices  16.8 us (36%)
  Pallas kernels  9.77 us (21%)
  local copies, waits for them, and re-layouts  2.21 us (5%)
    ppermute x5, starting transfers between devices, swap_y(): there = lax.ppermute(far_cells, ('gx', 'gy'), far)  13.4 us
    ppermute x5, waiting for transfers between devices, swap_y(): there = lax.ppermute(far_cells, ('gx', 'gy'), far)  11.7 us
    pallas_call x12, Pallas kernels, call(): pl.pallas_call(kernel, out_shape=[jax.ShapeDtypeStruct(shape, dtype) for...  9.77 us
    ppermute x3, waiting for transfers between devices, swap_x(): return (got, lax.ppermute(far_cells, ('gx', 'gy'), far))  3.76 us
    unnamed x16, local copies, waits for them, and re-layouts  2.15 us
    ppermute x3, starting transfers between devices, swap_x(): return (got, lax.ppermute(far_cells, ('gx', 'gy'), far))  1.94 us
    ppermute x3, starting transfers between devices, swap_x(): got = lax.ppermute(near_cells, 'gx', near)  1.44 us
    ppermute x5, waiting for transfers between devices, swap_y(): got = lax.ppermute(near_cells, 'gy', near)  1.27 us
  transfers between devices with their start and end apart: 16, of which 9 were waited for; matrix products, arithmetic and copies ran while one was open for 0% of the time, Pallas kernels for 15%

profile of v5, /device:TPU:128, one launch (start us, length us, event | category | flops | bytes accessed | tf_op | source)
XLA Modules:
  0.0 47.0 jit_solution(10083448910943088496)
XLA Ops:
  0.0 0.9 %copy-done.2 = bf16[8,2,64,128]{3,2,1,0:T(8,128)(2,1)S(1)} copy-done((bf16[8,2,64,128]{3,2,1,0:T(8,128)(2,1)S(1)}, bf16[8,2,64,128]{3,2,1,0:T(8,128)(2,1)}, u32[]{:S(2)}) %copy-start.2) | copy-done | bytes 262168
  1.0 2.6 %collective-permute-start.1 = (bf16[8,64,128]{2,1,0:T(8,128)(2,1)S(1)}, bf16[8,64,128]{2,1,0:T(8,128)(2,1)S(1)}, u32[]{:S(2)}, u32[]{:S(2)}) collective-permute-start(bf16[8,64,128]{2,1,0:T(8,128)(2,1)S(1)} %get-tuple-element.19), channel_id=1, source_target_pairs={{15,16},{16,15},{17,18},{18,17},{19,20},{20,19},{21,22},{22,21},{2... | collective-permute-start | bytes 393224 | tf_op jit(solution)/shard_map/ppermute | solution.py:312
  3.7 0.6 %collective-permute-start = (bf16[8,64,128]{2,1,0:T(8,128)(2,1)S(1)}, bf16[8,64,128]{2,1,0:T(8,128)(2,1)S(1)}, u32[]{:S(2)}, u32[]{:S(2)}) collective-permute-start(bf16[8,64,128]{2,1,0:T(8,128)(2,1)S(1)} %get-tuple-element.18), channel_id=1, source_target_pairs={{0,1},{1,0},{2,3},{3,2},{4,5},{5,4},{6,7},{7,6},{8,9},{9,8},{10,11... | collective-permute-start | bytes 393224 | tf_op jit(solution)/shard_map/ppermute | solution.py:311
  4.3 1.2 %copy-done.4 = bf16[3,3,3,128,128]{4,3,2,1,0:T(8,128)(2,1)S(1)} copy-done((bf16[3,3,3,128,128]{4,3,2,1,0:T(8,128)(2,1)S(1)}, bf16[3,3,3,128,128]{4,3,2,1,0:T(8,128)(2,1)}, u32[]{:S(2)}) %copy-start.4) | copy-done | bytes 884760
  5.4 0.8 %entry_own.1.before = f32[2,8,64,128]{3,2,1,0:T(8,128)S(1)} custom-call(bf16[8,2,64,128]{3,2,1,0:T(8,128)(2,1)S(1)} %get-tuple-element.22.own, bf16[3,3,3,128,128]{4,3,2,1,0:T(8,128)(2,1)S(1)} %copy-done.4), custom_call_target="tpu_custom_call" | custom-call | flops 2000000000 | bytes 1048576 | tf_op jit(solution)/shard_map/entry_own/pallas_call | solution.py:286
  6.2 3.4 %collective-permute-done.1 = bf16[8,64,128]{2,1,0:T(8,128)(2,1)S(1)} collective-permute-done((bf16[8,64,128]{2,1,0:T(8,128)(2,1)S(1)}, bf16[8,64,128]{2,1,0:T(8,128)(2,1)S(1)}, u32[]{:S(2)}, u32[]{:S(2)}) %collective-permute-start.1) | collective-permute-done | bytes 131104 | tf_op jit(solution)/shard_map/ppermute | solution.py:312
  9.7 0.9 %collective-permute-start.3 = (bf16[4,64,128]{2,1,0:T(8,128)(2,1)S(1)}, bf16[4,64,128]{2,1,0:T(8,128)(2,1)S(1)}, u32[]{:S(2)}, u32[]{:S(2)}) collective-permute-start(bf16[4,64,128]{2,1,0:T(8,128)(2,1)S(1)} %pad_maximum_fusion.3), channel_id=1, source_target_pairs={{0,4},{1,5},{2,6},{3,7},{4,0},{5,1},{6,2},{7,3},{8,12},{9,13},{10,... | collective-permute-start | bytes 196616 | tf_op jit(solution)/shard_map/ppermute | solution.py:330
  10.7 0.8 %collective-permute-start.2 = (bf16[4,64,128]{2,1,0:T(8,128)(2,1)S(1)}, bf16[4,64,128]{2,1,0:T(8,128)(2,1)S(1)}, u32[]{:S(2)}, u32[]{:S(2)}) collective-permute-start(bf16[4,64,128]{2,1,0:T(8,128)(2,1)S(1)} %pad_maximum_fusion.2), channel_id=1, source_target_pairs={{0,32},{32,0},{64,96},{96,64},{128,160},{160,128},{192,224},{224,1... | collective-permute-start | bytes 196616 | tf_op jit(solution)/shard_map/ppermute | solution.py:329
  11.5 0.7 %entry_side.1.before = f32[2,8,64,128]{3,2,1,0:T(8,128)S(1)} custom-call(bf16[8,64,128]{2,1,0:T(8,128)(2,1)S(1)} %collective-permute-done.y_near, bf16[8,64,128]{2,1,0:T(8,128)(2,1)S(1)} %broadcast_select_fusion.1.y_far, bf16[3,3,3,128,128]{4,3,2,1,0:T(8,128)(2,1)S(1)} %copy-done.5, f32[2,8,64,128]{3,2,1,0:T(8,128)S(1)} %entry_own.1.before), custom_call_target="tpu_custom_call" | custom-call | flops 1000000000 | bytes 1048576 | tf_op jit(solution)/shard_map/entry_side/pallas_call | solution.py:286
  12.2 1.9 %collective-permute-done.3.x_far = bf16[4,64,128]{2,1,0:T(8,128)(2,1)S(1)} collective-permute-done((bf16[4,64,128]{2,1,0:T(8,128)(2,1)S(1)}, bf16[4,64,128]{2,1,0:T(8,128)(2,1)S(1)}, u32[]{:S(2)}, u32[]{:S(2)}) %collective-permute-start.3) | collective-permute-done | bytes 65568 | tf_op jit(solution)/shard_map/ppermute | solution.py:330
  14.1 0.7 %entry_last.1 = (bf16[8,2,64,128]{3,2,1,0:T(8,128)(2,1)S(1)}, bf16[4,32,256]{2,1,0:T(8,128)(2,1)S(1)}) custom-call(bf16[4,64,128]{2,1,0:T(8,128)(2,1)S(1)} %collective-permute-done.2.x_near, bf16[4,64,128]{2,1,0:T(8,128)(2,1)S(1)} %collective-permute-done.3.x_far, bf16[3,3,3,128,128]{4,3,2,1,0:T(8,128)(2,1)S(1)} %copy-done.5, ...), custom_call_target="tpu_custom_call" | custom-call | flops 1000000000 | bytes 1048576 | tf_op jit(solution)/shard_map/entry_last/pallas_call | solution.py:286
  14.8 2.6 %collective-permute-start.5 = (bf16[4,32,256]{2,1,0:T(8,128)(2,1)S(1)}, bf16[4,32,256]{2,1,0:T(8,128)(2,1)S(1)}, u32[]{:S(2)}, u32[]{:S(2)}) collective-permute-start(bf16[4,32,256]{2,1,0:T(8,128)(2,1)S(1)} %get-tuple-element.23.own), channel_id=1, source_target_pairs={{15,16},{16,15},{17,18},{18,17},{19,20},{20,19},{21,22},{22,21},{2... | collective-permute-start | bytes 196616 | tf_op jit(solution)/shard_map/ppermute | solution.py:312
  17.4 2.9 %collective-permute-start.12 = (bf16[8,64,128]{2,1,0:T(8,128)(2,1)S(1)}, bf16[8,64,128]{2,1,0:T(8,128)(2,1)S(1)}, u32[]{:S(2)}, u32[]{:S(2)}) collective-permute-start(bf16[8,64,128]{2,1,0:T(8,128)(2,1)S(1)} %get-tuple-element.38), channel_id=1, source_target_pairs={{15,16},{16,15},{17,18},{18,17},{19,20},{20,19},{21,22},{22,21},{2... | collective-permute-start | bytes 393224 | tf_op jit(solution)/shard_map/ppermute | solution.py:312
  20.4 2.1 %collective-permute-done.5 = bf16[4,32,256]{2,1,0:T(8,128)(2,1)S(1)} collective-permute-done((bf16[4,32,256]{2,1,0:T(8,128)(2,1)S(1)}, bf16[4,32,256]{2,1,0:T(8,128)(2,1)S(1)}, u32[]{:S(2)}, u32[]{:S(2)}) %collective-permute-start.5) | collective-permute-done | bytes 65568 | tf_op jit(solution)/shard_map/ppermute | solution.py:312
  22.6 0.7 %collective-permute-start.7 = (bf16[3,3,32,256]{3,2,1,0:T(8,128)(2,1)S(1)}, bf16[3,3,32,256]{3,2,1,0:T(8,128)(2,1)S(1)}, u32[]{:S(2)}, u32[]{:S(2)}) collective-permute-start(bf16[3,3,32,256]{3,2,1,0:T(8,128)(2,1)S(1)} %pad_maximum_fusion.1), channel_id=1, source_target_pairs={{0,4},{1,5},{2,6},{3,7},{4,0},{5,1},{6,2},{7,3},{8,12},{9,13},{10,... | collective-permute-start | bytes 442376 | tf_op jit(solution)/shard_map/ppermute | solution.py:330
  23.3 0.5 %collective-permute-start.6 = (bf16[3,3,32,256]{3,2,1,0:T(8,128)(2,1)S(1)}, bf16[3,3,32,256]{3,2,1,0:T(8,128)(2,1)S(1)}, u32[]{:S(2)}, u32[]{:S(2)}) collective-permute-start(bf16[3,3,32,256]{3,2,1,0:T(8,128)(2,1)S(1)} %pad_maximum_fusion), channel_id=1, source_target_pairs={{0,32},{32,0},{64,96},{96,64},{128,160},{160,128},{192,224},{224,1... | collective-permute-start | bytes 442376 | tf_op jit(solution)/shard_map/ppermute | solution.py:329
  23.8 0.6 %first_own.1.before = f32[8,32,256]{2,1,0:T(8,128)S(1)} custom-call(bf16[4,32,256]{2,1,0:T(8,128)(2,1)S(1)} %get-tuple-element.23.own, bf16[4,32,256]{2,1,0:T(8,128)(2,1)S(1)} %collective-permute-done.4.y_near, bf16[4,32,256]{2,1,0:T(8,128)(2,1)S(1)} %broadcast_select_fusion.2.y_far, bf16[3,3,3,256,256]{4,3,2,1,0:T(8,128)(2,1)S(1)} %copy-done), custom_call_target="tpu_custom_call" | custom-call | flops 700000000 | bytes 1048576 | tf_op jit(solution)/shard_map/first_own/pallas_call | solution.py:286
  24.5 1.4 %collective-permute-done.12 = bf16[8,64,128]{2,1,0:T(8,128)(2,1)S(1)} collective-permute-done((bf16[8,64,128]{2,1,0:T(8,128)(2,1)S(1)}, bf16[8,64,128]{2,1,0:T(8,128)(2,1)S(1)}, u32[]{:S(2)}, u32[]{:S(2)}) %collective-permute-start.12) | collective-permute-done | bytes 131104 | tf_op jit(solution)/shard_map/ppermute | solution.py:312
  25.9 1.9 %collective-permute-done.7.x_far = bf16[3,3,32,256]{3,2,1,0:T(8,128)(2,1)S(1)} collective-permute-done((bf16[3,3,32,256]{3,2,1,0:T(8,128)(2,1)S(1)}, bf16[3,3,32,256]{3,2,1,0:T(8,128)(2,1)S(1)}, u32[]{:S(2)}, u32[]{:S(2)}) %collective-permute-start.7) | collective-permute-done | bytes 147488 | tf_op jit(solution)/shard_map/ppermute | solution.py:330
  27.8 0.7 %first_last.1.own = bf16[8,32,256]{2,1,0:T(8,128)(2,1)S(1)} custom-call(bf16[3,3,32,256]{3,2,1,0:T(8,128)(2,1)S(1)} %collective-permute-done.6.x_near, bf16[3,3,32,256]{3,2,1,0:T(8,128)(2,1)S(1)} %collective-permute-done.7.x_far, bf16[3,3,3,256,256]{4,3,2,1,0:T(8,128)(2,1)S(1)} %copy-done, f32[8,32,256]{2,1,0:T(8,128)S(1)} %first_own.1.before), custom_call_target="tpu_custom_call" | custom-call | flops 1000000000 | bytes 1048576 | tf_op jit(solution)/shard_map/first_last/pallas_call | solution.py:286
  28.6 2.6 %collective-permute-start.8 = (bf16[8,32,256]{2,1,0:T(8,128)(2,1)S(1)}, bf16[8,32,256]{2,1,0:T(8,128)(2,1)S(1)}, u32[]{:S(2)}, u32[]{:S(2)}) collective-permute-start(bf16[8,32,256]{2,1,0:T(8,128)(2,1)S(1)} %first_last.1.own), channel_id=1, source_target_pairs={{15,16},{16,15},{17,18},{18,17},{19,20},{20,19},{21,22},{22,21},{2... | collective-permute-start | bytes 393224 | tf_op jit(solution)/shard_map/ppermute | solution.py:312
  31.2 1.3 %decode_skip.1.before = f32[2,8,64,128]{3,2,1,0:T(8,128)S(1)} custom-call(bf16[8,2,64,128]{3,2,1,0:T(8,128)(2,1)S(1)} %get-tuple-element.25.encoded, bf16[8,64,128]{2,1,0:T(8,128)(2,1)S(1)} %collective-permute-done.11.y_near, bf16[8,64,128]{2,1,0:T(8,128)(2,1)S(1)} %broadcast_select_fusion.y_far, bf16[3,3,3,256,128]{4,3,2,1,0:T(8,128)(2,1)S(1)} %copy-done.3), custom_call_target="tpu_custom_call" | custom-call | flops 2000000000 | bytes 1048576 | tf_op jit(solution)/shard_map/decode_skip/pallas_call | solution.py:286
  32.9 0.6 %collective-permute-done.9.y_near = bf16[8,32,256]{2,1,0:T(8,128)(2,1)S(1)} collective-permute-done((bf16[8,32,256]{2,1,0:T(8,128)(2,1)S(1)}, bf16[8,32,256]{2,1,0:T(8,128)(2,1)S(1)}, u32[]{:S(2)}, u32[]{:S(2)}) %collective-permute-start.9) | collective-permute-done | bytes 131104 | tf_op jit(solution)/shard_map/ppermute | solution.py:311
  33.5 0.6 %second_own.1.before = f32[192,256]{1,0:T(8,128)S(1)} custom-call(bf16[8,32,256]{2,1,0:T(8,128)(2,1)S(1)} %first_last.1.own, bf16[8,32,256]{2,1,0:T(8,128)(2,1)S(1)} %collective-permute-done.9.y_near, bf16[3,3,3,256,256]{4,3,2,1,0:T(8,128)(2,1)S(1)} %copy-done.1), custom_call_target="tpu_custom_call" | custom-call | flops 700000000 | bytes 1048576 | tf_op jit(solution)/shard_map/second_own/pallas_call | solution.py:286
  34.2 2.8 %collective-permute-done.8.y_far = bf16[8,32,256]{2,1,0:T(8,128)(2,1)S(1)} collective-permute-done((bf16[8,32,256]{2,1,0:T(8,128)(2,1)S(1)}, bf16[8,32,256]{2,1,0:T(8,128)(2,1)S(1)}, u32[]{:S(2)}, u32[]{:S(2)}) %collective-permute-start.8) | collective-permute-done | bytes 131104 | tf_op jit(solution)/shard_map/ppermute | solution.py:312
  37.0 0.4 second_far.1.own
  37.5 2.6 %collective-permute-start.10 = (bf16[6,32,256]{2,1,0:T(8,128)(2,1)S(1)}, bf16[6,32,256]{2,1,0:T(8,128)(2,1)S(1)}, u32[]{:S(2)}, u32[]{:S(2)}) collective-permute-start(bf16[6,32,256]{2,1,0:T(8,128)(2,1)S(1)} %second_far.1.own), channel_id=1, source_target_pairs={{15,16},{16,15},{17,18},{18,17},{19,20},{20,19},{21,22},{22,21},{2... | collective-permute-start | bytes 294920 | tf_op jit(solution)/shard_map/ppermute | solution.py:312
  40.2 1.3 %decode_own.1.before = f32[2,8,64,128]{3,2,1,0:T(8,128)S(1)} custom-call(bf16[6,32,256]{2,1,0:T(8,128)(2,1)S(1)} %second_far.1.own, bf16[4,64,128]{2,1,0:T(8,128)(2,1)S(1)} %collective-permute-done.13.x_near, bf16[4,64,128]{2,1,0:T(8,128)(2,1)S(1)} %collective-permute-done.14.x_far, bf16[2,2,2,256,128]{4,3,2,1,0:T(8,128)(2,1)S(1)} %copy-done.7, ...), custom_call_target="tpu_custom_call" | custom-call | flops 2000000000 | bytes 1048576 | tf_op jit(solution)/shard_map/decode_own/pallas_call | solution.py:286
  41.5 0.6 %collective-permute-done.15.y_near = bf16[6,32,256]{2,1,0:T(8,128)(2,1)S(1)} collective-permute-done((bf16[6,32,256]{2,1,0:T(8,128)(2,1)S(1)}, bf16[6,32,256]{2,1,0:T(8,128)(2,1)S(1)}, u32[]{:S(2)}, u32[]{:S(2)}) %collective-permute-start.15) | collective-permute-done | bytes 98336 | tf_op jit(solution)/shard_map/ppermute | solution.py:311
  42.1 1.4 %decode_near.1._ = bf16[8,2,64,128]{3,2,1,0:T(8,128)(2,1)} custom-call(bf16[6,32,256]{2,1,0:T(8,128)(2,1)S(1)} %collective-permute-done.15.y_near, bf16[2,2,2,256,128]{4,3,2,1,0:T(8,128)(2,1)S(1)} %copy-done.7, bf16[3,3,3,256,128]{4,3,2,1,0:T(8,128)(2,1)S(1)} %copy-done.3, f32[2,8,64,128]{3,2,1,0:T(8,128)S(1)} %decode_own.1.before), custom_call_target="tpu_custom_call" | custom-call | flops 1000000000 | bytes 1048576 | tf_op jit(solution)/shard_map/decode_near/pallas_call | solution.py:286
  43.5 2.1 %collective-permute-done.10.y_far = bf16[6,32,256]{2,1,0:T(8,128)(2,1)S(1)} collective-permute-done((bf16[6,32,256]{2,1,0:T(8,128)(2,1)S(1)}, bf16[6,32,256]{2,1,0:T(8,128)(2,1)S(1)}, u32[]{:S(2)}, u32[]{:S(2)}) %collective-permute-start.10) | collective-permute-done | bytes 98336 | tf_op jit(solution)/shard_map/ppermute | solution.py:312
  45.5 1.3 %decode_last.1 = bf16[8,2,64,128]{3,2,1,0:T(8,128)(2,1)} custom-call(bf16[6,32,256]{2,1,0:T(8,128)(2,1)S(1)} %collective-permute-done.10.y_far, bf16[2,2,2,256,128]{4,3,2,1,0:T(8,128)(2,1)S(1)} %copy-done.7, bf16[3,3,3,256,128]{4,3,2,1,0:T(8,128)(2,1)S(1)} %copy-done.3, f32[2,8,64,128]{3,2,1,0:T(8,128)S(1)} %decode_own.1.before, ...), custom_call_target="tpu_custom_call", output_to_operand_aliasing={{}: (4, {})} | custom-call | flops 1000000000 | bytes 1048576 | tf_op jit(solution)/shard_map/decode_last/pallas_call | solution.py:286
  (43 shorter events, 0.9 us)
Async XLA Ops:
  0.0 0.9 %copy-start.2 = (bf16[8,2,64,128]{3,2,1,0:T(8,128)(2,1)S(1)}, bf16[8,2,64,128]{3,2,1,0:T(8,128)(2,1)}, u32[]{:S(2)}) copy-start(bf16[8,2,64,128]{3,2,1,0:T(8,128)(2,1)} %volume.1) | copy-start | bytes 786436
  1.0 8.6 %collective-permute-start.1 = (bf16[8,64,128]{2,1,0:T(8,128)(2,1)S(1)}, bf16[8,64,128]{2,1,0:T(8,128)(2,1)S(1)}, u32[]{:S(2)}, u32[]{:S(2)}) collective-permute-start(bf16[8,64,128]{2,1,0:T(8,128)(2,1)S(1)} %get-tuple-element.19), channel_id=1, source_target_pairs={{15,16},{16,15},{17,18},{18,17},{19,20},{20,19},{21,22},{22,21},{2... | collective-permute-start | bytes 393224 | tf_op jit(solution)/shard_map/ppermute | solution.py:312
  3.7 6.0 %collective-permute-start = (bf16[8,64,128]{2,1,0:T(8,128)(2,1)S(1)}, bf16[8,64,128]{2,1,0:T(8,128)(2,1)S(1)}, u32[]{:S(2)}, u32[]{:S(2)}) collective-permute-start(bf16[8,64,128]{2,1,0:T(8,128)(2,1)S(1)} %get-tuple-element.18), channel_id=1, source_target_pairs={{0,1},{1,0},{2,3},{3,2},{4,5},{5,4},{6,7},{7,6},{8,9},{9,8},{10,11... | collective-permute-start | bytes 393224 | tf_op jit(solution)/shard_map/ppermute | solution.py:311
  4.3 1.2 %copy-start.4 = (bf16[3,3,3,128,128]{4,3,2,1,0:T(8,128)(2,1)S(1)}, bf16[3,3,3,128,128]{4,3,2,1,0:T(8,128)(2,1)}, u32[]{:S(2)}) copy-start(bf16[3,3,3,128,128]{4,3,2,1,0:T(8,128)(2,1)} %weight.13) | copy-start | bytes 2654212
  5.4 6.1 %copy-start.5 = (bf16[3,3,3,128,128]{4,3,2,1,0:T(8,128)(2,1)S(1)}, bf16[3,3,3,128,128]{4,3,2,1,0:T(8,128)(2,1)}, u32[]{:S(2)}) copy-start(bf16[3,3,3,128,128]{4,3,2,1,0:T(8,128)(2,1)} %weight.13) | copy-start | bytes 2654212
  6.2 7.9 %copy-start.6 = (bf16[2,2,2,128,256]{4,3,2,1,0:T(8,128)(2,1)S(1)}, bf16[2,2,2,128,256]{4,3,2,1,0:T(8,128)(2,1)}, u32[]{:S(2)}) copy-start(bf16[2,2,2,128,256]{4,3,2,1,0:T(8,128)(2,1)} %down.1) | copy-start | bytes 1572868
  9.7 4.4 %collective-permute-start.3 = (bf16[4,64,128]{2,1,0:T(8,128)(2,1)S(1)}, bf16[4,64,128]{2,1,0:T(8,128)(2,1)S(1)}, u32[]{:S(2)}, u32[]{:S(2)}) collective-permute-start(bf16[4,64,128]{2,1,0:T(8,128)(2,1)S(1)} %pad_maximum_fusion.3), channel_id=1, source_target_pairs={{0,4},{1,5},{2,6},{3,7},{4,0},{5,1},{6,2},{7,3},{8,12},{9,13},{10,... | collective-permute-start | bytes 196616 | tf_op jit(solution)/shard_map/ppermute | solution.py:330
  10.7 3.4 %collective-permute-start.2 = (bf16[4,64,128]{2,1,0:T(8,128)(2,1)S(1)}, bf16[4,64,128]{2,1,0:T(8,128)(2,1)S(1)}, u32[]{:S(2)}, u32[]{:S(2)}) collective-permute-start(bf16[4,64,128]{2,1,0:T(8,128)(2,1)S(1)} %pad_maximum_fusion.2), channel_id=1, source_target_pairs={{0,32},{32,0},{64,96},{96,64},{128,160},{160,128},{192,224},{224,1... | collective-permute-start | bytes 196616 | tf_op jit(solution)/shard_map/ppermute | solution.py:329
  12.2 11.6 %copy-start = (bf16[3,3,3,256,256]{4,3,2,1,0:T(8,128)(2,1)S(1)}, bf16[3,3,3,256,256]{4,3,2,1,0:T(8,128)(2,1)}, u32[]{:S(2)}) copy-start(bf16[3,3,3,256,256]{4,3,2,1,0:T(8,128)(2,1)} %weight.15) | copy-start | bytes 10616836
  14.8 7.7 %collective-permute-start.5 = (bf16[4,32,256]{2,1,0:T(8,128)(2,1)S(1)}, bf16[4,32,256]{2,1,0:T(8,128)(2,1)S(1)}, u32[]{:S(2)}, u32[]{:S(2)}) collective-permute-start(bf16[4,32,256]{2,1,0:T(8,128)(2,1)S(1)} %get-tuple-element.23.own), channel_id=1, source_target_pairs={{15,16},{16,15},{17,18},{18,17},{19,20},{20,19},{21,22},{22,21},{2... | collective-permute-start | bytes 196616 | tf_op jit(solution)/shard_map/ppermute | solution.py:312
  17.4 5.0 %collective-permute-start.4 = (bf16[4,32,256]{2,1,0:T(8,128)(2,1)S(1)}, bf16[4,32,256]{2,1,0:T(8,128)(2,1)S(1)}, u32[]{:S(2)}, u32[]{:S(2)}) collective-permute-start(bf16[4,32,256]{2,1,0:T(8,128)(2,1)S(1)} %get-tuple-element.23.own), channel_id=1, source_target_pairs={{0,1},{1,0},{2,3},{3,2},{4,5},{5,4},{6,7},{7,6},{8,9},{9,8},{10,11... | collective-permute-start | bytes 196616 | tf_op jit(solution)/shard_map/ppermute | solution.py:311
  17.4 8.4 %collective-permute-start.12 = (bf16[8,64,128]{2,1,0:T(8,128)(2,1)S(1)}, bf16[8,64,128]{2,1,0:T(8,128)(2,1)S(1)}, u32[]{:S(2)}, u32[]{:S(2)}) collective-permute-start(bf16[8,64,128]{2,1,0:T(8,128)(2,1)S(1)} %get-tuple-element.38), channel_id=1, source_target_pairs={{15,16},{16,15},{17,18},{18,17},{19,20},{20,19},{21,22},{22,21},{2... | collective-permute-start | bytes 393224 | tf_op jit(solution)/shard_map/ppermute | solution.py:312
  20.3 5.5 %collective-permute-start.11 = (bf16[8,64,128]{2,1,0:T(8,128)(2,1)S(1)}, bf16[8,64,128]{2,1,0:T(8,128)(2,1)S(1)}, u32[]{:S(2)}, u32[]{:S(2)}) collective-permute-start(bf16[8,64,128]{2,1,0:T(8,128)(2,1)S(1)} %get-tuple-element.37), channel_id=1, source_target_pairs={{0,1},{1,0},{2,3},{3,2},{4,5},{5,4},{6,7},{7,6},{8,9},{9,8},{10,11... | collective-permute-start | bytes 393224 | tf_op jit(solution)/shard_map/ppermute | solution.py:311
  22.6 5.2 %collective-permute-start.7 = (bf16[3,3,32,256]{3,2,1,0:T(8,128)(2,1)S(1)}, bf16[3,3,32,256]{3,2,1,0:T(8,128)(2,1)S(1)}, u32[]{:S(2)}, u32[]{:S(2)}) collective-permute-start(bf16[3,3,32,256]{3,2,1,0:T(8,128)(2,1)S(1)} %pad_maximum_fusion.1), channel_id=1, source_target_pairs={{0,4},{1,5},{2,6},{3,7},{4,0},{5,1},{6,2},{7,3},{8,12},{9,13},{10,... | collective-permute-start | bytes 442376 | tf_op jit(solution)/shard_map/ppermute | solution.py:330
  23.3 7.9 %copy-start.3 = (bf16[3,3,3,256,128]{4,3,2,1,0:T(8,128)(2,1)S(1)}, bf16[3,3,3,256,128]{4,3,2,1,0:T(8,128)(2,1)}, u32[]{:S(2)}) copy-start(bf16[3,3,3,256,128]{4,3,2,1,0:T(8,128)(2,1)} %weight.21) | copy-start | bytes 5308420
  23.3 4.5 %collective-permute-start.6 = (bf16[3,3,32,256]{3,2,1,0:T(8,128)(2,1)S(1)}, bf16[3,3,32,256]{3,2,1,0:T(8,128)(2,1)S(1)}, u32[]{:S(2)}, u32[]{:S(2)}) collective-permute-start(bf16[3,3,32,256]{3,2,1,0:T(8,128)(2,1)S(1)} %pad_maximum_fusion), channel_id=1, source_target_pairs={{0,32},{32,0},{64,96},{96,64},{128,160},{160,128},{192,224},{224,1... | collective-permute-start | bytes 442376 | tf_op jit(solution)/shard_map/ppermute | solution.py:329
  28.5 5.1 %copy-start.1 = (bf16[3,3,3,256,256]{4,3,2,1,0:T(8,128)(2,1)S(1)}, bf16[3,3,3,256,256]{4,3,2,1,0:T(8,128)(2,1)}, u32[]{:S(2)}) copy-start(bf16[3,3,3,256,256]{4,3,2,1,0:T(8,128)(2,1)} %weight.17) | copy-start | bytes 10616836
  28.5 5.1 %collective-permute-start.9 = (bf16[8,32,256]{2,1,0:T(8,128)(2,1)S(1)}, bf16[8,32,256]{2,1,0:T(8,128)(2,1)S(1)}, u32[]{:S(2)}, u32[]{:S(2)}) collective-permute-start(bf16[8,32,256]{2,1,0:T(8,128)(2,1)S(1)} %first_last.1.own), channel_id=1, source_target_pairs={{0,1},{1,0},{2,3},{3,2},{4,5},{5,4},{6,7},{7,6},{8,9},{9,8},{10,11... | collective-permute-start | bytes 393224 | tf_op jit(solution)/shard_map/ppermute | solution.py:311
  28.6 8.4 %collective-permute-start.8 = (bf16[8,32,256]{2,1,0:T(8,128)(2,1)S(1)}, bf16[8,32,256]{2,1,0:T(8,128)(2,1)S(1)}, u32[]{:S(2)}, u32[]{:S(2)}) collective-permute-start(bf16[8,32,256]{2,1,0:T(8,128)(2,1)S(1)} %first_last.1.own), channel_id=1, source_target_pairs={{15,16},{16,15},{17,18},{18,17},{19,20},{20,19},{21,22},{22,21},{2... | collective-permute-start | bytes 393224 | tf_op jit(solution)/shard_map/ppermute | solution.py:312
  32.5 7.7 %copy-start.7 = (bf16[2,2,2,256,128]{4,3,2,1,0:T(8,128)(2,1)S(1)}, bf16[2,2,2,256,128]{4,3,2,1,0:T(8,128)(2,1)}, u32[]{:S(2)}) copy-start(bf16[2,2,2,256,128]{4,3,2,1,0:T(8,128)(2,1)} %up.5) | copy-start | bytes 1572868
  32.5 7.7 %collective-permute-start.13 = (bf16[4,64,128]{2,1,0:T(8,128)(2,1)S(1)}, bf16[4,64,128]{2,1,0:T(8,128)(2,1)S(1)}, u32[]{:S(2)}, u32[]{:S(2)}) collective-permute-start(bf16[4,64,128]{2,1,0:T(8,128)(2,1)S(1)} %get-tuple-element.28), channel_id=1, source_target_pairs={{0,32},{32,0},{64,96},{96,64},{128,160},{160,128},{192,224},{224,1... | collective-permute-start | bytes 196616 | tf_op jit(solution)/shard_map/ppermute | solution.py:329
  32.6 7.6 %collective-permute-start.14 = (bf16[4,64,128]{2,1,0:T(8,128)(2,1)S(1)}, bf16[4,64,128]{2,1,0:T(8,128)(2,1)S(1)}, u32[]{:S(2)}, u32[]{:S(2)}) collective-permute-start(bf16[4,64,128]{2,1,0:T(8,128)(2,1)S(1)} %get-tuple-element.29), channel_id=1, source_target_pairs={{0,4},{1,5},{2,6},{3,7},{4,0},{5,1},{6,2},{7,3},{8,12},{9,13},{10,... | collective-permute-start | bytes 196616 | tf_op jit(solution)/shard_map/ppermute | solution.py:330
  37.4 4.7 %collective-permute-start.15 = (bf16[6,32,256]{2,1,0:T(8,128)(2,1)S(1)}, bf16[6,32,256]{2,1,0:T(8,128)(2,1)S(1)}, u32[]{:S(2)}, u32[]{:S(2)}) collective-permute-start(bf16[6,32,256]{2,1,0:T(8,128)(2,1)S(1)} %second_far.1.own), channel_id=1, source_target_pairs={{0,1},{1,0},{2,3},{3,2},{4,5},{5,4},{6,7},{7,6},{8,9},{9,8},{10,11... | collective-permute-start | bytes 294920 | tf_op jit(solution)/shard_map/ppermute | solution.py:311
  37.5 8.0 %collective-permute-start.10 = (bf16[6,32,256]{2,1,0:T(8,128)(2,1)S(1)}, bf16[6,32,256]{2,1,0:T(8,128)(2,1)S(1)}, u32[]{:S(2)}, u32[]{:S(2)}) collective-permute-start(bf16[6,32,256]{2,1,0:T(8,128)(2,1)S(1)} %second_far.1.own), channel_id=1, source_target_pairs={{15,16},{16,15},{17,18},{18,17},{19,20},{20,19},{21,22},{22,21},{2... | collective-permute-start | bytes 294920 | tf_op jit(solution)/shard_map/ppermute | solution.py:312

commit v6 on v5

--- a/solution.py
+++ b/solution.py
@@ -62,11 +62,16 @@
     gx, nx = lax.axis_index("gx"), lax.axis_size("gx")
     odd_x = lax.rem(gx, 2)
     for cells, high, ok in ((x_near, 1 - odd_x, None), (x_far, odd_x, (gx > 0) & (gx < nx - 1))):
+        left = jnp.concatenate(
+            [jnp.concatenate([cells[b + col] for col in range(3)], axis=1) for b in range(2)],
+            axis=0,
+        )
+        blocks = [[part(2 * high, col, d) for col in range(3)] for d in range(3)]
+        values = taps_sum(left, blocks)
+        if ok is not None:
+            values = jnp.where(ok, values, 0.0)
         for b in range(2):
-            left = jnp.concatenate([cells[b + col] for col in range(3)], axis=1)
-            blocks = [[part(2 * high, col, d) for col in range(3)] for d in range(3)]
-            values = taps_sum(left, blocks)
-            total[b, 7 * high] += values if ok is None else jnp.where(ok, values, 0.0)
+            total[b, 7 * high] += values[b * 64 : b * 64 + 64]
 
 
 def sides():
@@ -157,10 +162,9 @@
 
 def rows_sum(rows, weight, off):
     left = jnp.concatenate([jnp.concatenate(planes, axis=1) for planes in rows], axis=0)
-    products = [
-        jnp.dot(left, weight[off, :, d].reshape(768, 256), preferred_element_type=F32)
-        for d in range(3)
-    ]
+    right = jnp.concatenate([weight[off, :, d].reshape(768, 256) for d in range(3)], axis=1)
+    products = jnp.dot(left, right, preferred_element_type=F32)
+    products = [products[:, d * 256 : d * 256 + 256] for d in range(3)]
     return depth_sum(*products, 32).reshape(len(rows), 32, 256)
 
 
@@ -192,14 +196,15 @@
 
 def deep_sum(planes, at, weight):
     left = jnp.concatenate([three_rows(p, 0, p.shape[0] - 2) for p in planes], axis=1)
-    products = [
-        jnp.dot(
-            left,
-            jnp.concatenate([weight[:, place, d].reshape(768, 256) for place in at], axis=0),
-            preferred_element_type=F32,
-        )
-        for d in range(3)
-    ]
+    right = jnp.concatenate(
+        [
+            jnp.concatenate([weight[:, place, d].reshape(768, 256) for place in at], axis=0)
+            for d in range(3)
+        ],
+        axis=1,
+    )
+    products = jnp.dot(left, right, preferred_element_type=F32)
+    products = [products[:, d * 256 : d * 256 + 256] for d in range(3)]
     return depth_sum(*products, 32)
 
 
@@ -215,15 +220,28 @@
     masked_rows(leaky_unit(before[...] + far).reshape(6, 32, 256), 1, out)
 
 
+def beside_own_kernel(own, y_far, weight, total):
+    _, side = sides()
+    total[...] = deep_sum((own, y_far), (2 - 2 * side, 1), weight)
+
+
+def beside_far_kernel(beyond, weight, before, out):
+    _, side = sides()
+    values = before[...] + deep_sum((beyond,), (2 * side,), weight)
+    masked_rows(leaky_unit(values).reshape(6, 32, 256), 1, out)
+
+
 def half_weights(weight, half):
     return lambda off, col, d: weight[off, col, d, half * 128 : half * 128 + 128]
 
 
 def lift(cells, up, b, upward, col):
+    parts = jnp.concatenate([up[a, b, d] for a in range(2) for d in range(2)], axis=1)
+    lifted = leaky_unit(jnp.dot(cells, parts, preferred_element_type=F32))
     for a in range(2):
         for d in range(2):
-            part = leaky_unit(jnp.dot(cells, up[a, b, d], preferred_element_type=F32))
-            part = part.reshape(6, 32, 128)
+            lane = (2 * a + d) * 128
+            part = lifted[:, lane : lane + 128].reshape(6, 32, 128)
             for i in range(6):
                 row = 2 * i + a - 1
                 if 0 <= row < 10:
@@ -251,10 +269,11 @@
     add_rows(total, x_near, x_far, half_weights(weight, 1))
 
 
-def decode_near_kernel(y_near, up, weight, before, decoded, cells, upward, column, sem):
-    side, _ = sides()
-    lift(y_near[...].reshape(192, 256), up, 1 - side, upward, 0)
-    cells[...] = upward[:, 0].astype(BF)
+def decode_far_kernel(y_far, up, weight, before, decoded, cells, upward, column, sem):
+    _, side = sides()
+    gy, ny = lax.axis_index("gy"), lax.axis_size("gy")
+    lift(y_far[...].reshape(192, 256), up, 1 - side, upward, 0)
+    cells[...] = jnp.where((gy > 0) & (gy < ny - 1), upward[:, 0], 0.0).astype(BF)
     values = before[side] + side_sum(cells, half_weights(weight, 0), side)
     column[...] = leaky_unit(values).astype(BF)
     copy = pltpu.make_async_copy(column, decoded.at[:, side], sem)
@@ -262,11 +281,10 @@
     copy.wait()
 
 
-def decode_last_kernel(y_far, up, weight, before, _, decoded, cells, upward, column, sems):
-    _, side = sides()
-    gy, ny = lax.axis_index("gy"), lax.axis_size("gy")
-    lift(y_far[...].reshape(192, 256), up, 1 - side, upward, 0)
-    cells[...] = jnp.where((gy > 0) & (gy < ny - 1), upward[:, 0], 0.0).astype(BF)
+def decode_near_kernel(y_near, up, weight, before, _, decoded, cells, upward, column, sems):
+    side, _ = sides()
+    lift(y_near[...].reshape(192, 256), up, 1 - side, upward, 0)
+    cells[...] = upward[:, 0].astype(BF)
     copies = []
     for half in range(2):
         rows = slice(4 * half, 4 * half + 4)
@@ -299,22 +317,26 @@
     )(*operands)
 
 
-def swap_y(near_cells, far_cells, far_first=True):
+def swap_near(cells):
+    return lax.ppermute(cells, "gy", [(i, i ^ 1) for i in range(lax.axis_size("gy"))])
+
+
+def swap_far(cells):
     nx, ny = lax.axis_size("gx"), lax.axis_size("gy")
-    near = [(i, i ^ 1) for i in range(ny)]
     far = []
     for x in range(nx):
         for y in range(ny):
             to = (x ^ 1) * ny + y if y in (0, ny - 1) else x * ny + ((y + 1) ^ 1) - 1
             far.append((x * ny + y, to))
     far = far[ny // 2 - 1 :] + far[: ny // 2 - 1]
-    got = lax.ppermute(near_cells, "gy", near)
-    there = lax.ppermute(far_cells, ("gx", "gy"), far)
-    if far_first:
-        at = lax.axis_index("gy")
-        there = jnp.where((at > 0) & (at < ny - 1), there, jnp.zeros_like(there))
-        there = lax.optimization_barrier(there)
-    return got, there
+    return lax.ppermute(cells, ("gx", "gy"), far)
+
+
+def swap_y(near_cells, far_cells):
+    near, far = swap_near(near_cells), swap_far(far_cells)
+    at, ny = lax.axis_index("gy"), lax.axis_size("gy")
+    far = jnp.where((at > 0) & (at < ny - 1), far, jnp.zeros_like(far))
+    return lax.optimization_barrier((near, far))
 
 
 def swap_x(near_cells, far_cells):
@@ -370,7 +392,7 @@
     )
     y1, y2 = swap_y(near, far)
     (total,) = call(
-        entry_own_kernel, [sums], [wide], "entry_own", 2_000_000_000, own, weight_entry
+        entry_own_kernel, [sums], [wide], "entry_own", 600_000_000, own, weight_entry
     )
     x1, x2 = swap_x(
         four_columns(edge_near, y1, y2, at_near), four_columns(edge_far, y1, y2, at_far)
@@ -430,7 +452,8 @@
         weight_deep_first,
         part,
     )
-    f1, f2 = swap_y(deep_one, deep_one, far_first=False)
+    f1, f2 = swap_near(deep_one), swap_far(deep_one)
+    f3 = swap_far(f1)
     skip, _ = lax.optimization_barrier(((encoded, g1, g2), deep_one))
     (total,) = call(
         decode_skip_kernel,
@@ -445,36 +468,29 @@
         four_columns(rows(encoded, at_near, 1)[0], g1, g2, at_near),
         four_columns(rows(encoded, at_far, 1)[0], g1, g2, at_far),
     )
-    edges, total = lax.optimization_barrier((edges, total))
+    edges, _ = lax.optimization_barrier((edges, deep_one))
     e1, e2 = swap_x(*edges)
+    sum_two, two = ((192, 256), F32), ((6, 32, 256), BF)
     (part,) = call(
-        second_own_kernel,
-        [((192, 256), F32)],
-        [],
-        "second_own",
-        700_000_000,
-        deep_one,
-        f1,
-        weight_deep_second,
+        second_own_kernel, [sum_two], [], "second_own", 1000, deep_one, f1, weight_deep_second
     )
     (deep_two,) = call(
-        second_far_kernel,
-        [((6, 32, 256), BF)],
-        [],
-        "second_far",
-        500_000_000,
-        f2,
-        weight_deep_second,
-        part,
-    )
-    h1, h2 = swap_y(deep_two, deep_two, far_first=False)
+        second_far_kernel, [two], [], "second_far", 1000, f2, weight_deep_second, part
+    )
+    h1 = swap_near(deep_two)
+    (part,) = call(
+        beside_own_kernel, [sum_two], [], "beside_own", 1000, deep_one, f2, weight_deep_second
+    )
+    (beside,) = call(
+        beside_far_kernel, [two], [], "beside_far", 1000000000, f3, weight_deep_second, part
+    )
     upward = ((10, 1, 64, 128), F32)
     (total,) = call(
         decode_own_kernel,
         [sums],
         [wide, ((10, 2, 64, 128), F32)],
         "decode_own",
-        2_000_000_000,
+        1000,
         deep_two,
         e1,
         e2,
@@ -483,24 +499,24 @@
         total,
     )
     (decoded,) = call(
-        decode_near_kernel,
+        decode_far_kernel,
         [((8, 2, 64, 128), BF)],
         [tall, upward, line, ((), None)],
-        "decode_near",
-        1_000_000_000,
-        h1,
+        "decode_far",
+        2000000000,
+        beside,
         weight_upward,
         weight_decoder,
         total,
         hbm_out=True,
     )
     (decoded,) = call(
-        decode_last_kernel,
+        decode_near_kernel,
         [((8, 2, 64, 128), BF)],
         [tall, upward, line, ((2,), None)],
-        "decode_last",
-        1_000_000_000,
-        h2,
+        "decode_near",
+        1000,
+        h1,
         weight_upward,
         weight_decoder,
         total,

time: 47.1 us -> 46 us (0.977)
  starting transfers between devices: 17.6 us -> 15.6 us
  waiting for transfers between devices: 16.8 us -> 15.5 us
  local copies, waits for them, and re-layouts: 2.21 us -> 3.37 us
  Pallas kernels: 9.77 us -> 10.6 us
    ppermute x3, starting transfers between devices: 1.44 us -> 0.19 us  [swap_x(): got = lax.ppermute(near_cells, 'gx', near)]
    unnamed x16, local copies, waits for them, and re-layouts: 2.15 us -> 3.31 us
    ppermute x10, waiting for transfers between devices: 13 us -> 12.1 us  [the longest x5 9.29 us: swap_far(): return lax.ppermute(cells, ('gx', 'gy'), far)]
    pallas_call x12 -> x14, Pallas kernels: 9.77 us -> 10.6 us  [call(): pl.pallas_call(kernel, out_shape=[jax.ShapeDtypeStruct(shape, dtype) for...]
    ppermute x3, starting transfers between devices: 1.94 us -> 1.31 us  [swap_x(): return (got, lax.ppermute(far_cells, ('gx', 'gy'), far))]
  transfers between devices with their start and end apart: 16 -> 16, of which waited for: 9 -> 7; matrix products, arithmetic and copies ran while one was open for 0% -> 0% of each run, Pallas kernels for 15% -> 17%
where the time goes in v6:
time: 46 us; the launch traced here: 45.7 us
  starting transfers between devices  15.6 us (34%)
  waiting for transfers between devices  15.5 us (34%)
  Pallas kernels  10.6 us (23%)
  local copies, waits for them, and re-layouts  3.37 us (7%)
  between operations  0.52 us (1%)
    ppermute x5, starting transfers between devices, swap_far(): return lax.ppermute(cells, ('gx', 'gy'), far)  13.4 us
    pallas_call x14, Pallas kernels, call(): pl.pallas_call(kernel, out_shape=[jax.ShapeDtypeStruct(shape, dtype) for...  10.6 us
    ppermute x5, waiting for transfers between devices, swap_far(): return lax.ppermute(cells, ('gx', 'gy'), far)  9.29 us
    ppermute x3, waiting for transfers between devices, swap_x(): return (got, lax.ppermute(far_cells, ('gx', 'gy'), far))  3.36 us
    unnamed x16, local copies, waits for them, and re-layouts  3.31 us
    ppermute x5, waiting for transfers between devices, swap_near(): lax.ppermute(cells, 'gy', [(i, i ^ 1) for i in range(lax.axis_size('gy'))])  2.81 us
    ppermute x3, starting transfers between devices, swap_x(): return (got, lax.ppermute(far_cells, ('gx', 'gy'), far))  1.31 us
  transfers between devices with their start and end apart: 16, of which 7 were waited for; matrix products, arithmetic and copies ran while one was open for 0% of the time, Pallas kernels for 17%

profile of v6, /device:TPU:128, one launch (start us, length us, event | category | flops | bytes accessed | tf_op | source)
XLA Modules:
  0.0 45.7 jit_solution(14406245061779497753)
XLA Ops:
  0.0 0.9 %copy-done.4 = bf16[8,2,64,128]{3,2,1,0:T(8,128)(2,1)S(1)} copy-done((bf16[8,2,64,128]{3,2,1,0:T(8,128)(2,1)S(1)}, bf16[8,2,64,128]{3,2,1,0:T(8,128)(2,1)}, u32[]{:S(2)}) %copy-start.4) | copy-done | bytes 262168
  1.0 2.6 %collective-permute-start.1 = (bf16[8,64,128]{2,1,0:T(8,128)(2,1)S(1)}, bf16[8,64,128]{2,1,0:T(8,128)(2,1)S(1)}, u32[]{:S(2)}, u32[]{:S(2)}) collective-permute-start(bf16[8,64,128]{2,1,0:T(8,128)(2,1)S(1)} %get-tuple-element.24), channel_id=1, source_target_pairs={{15,16},{16,15},{17,18},{18,17},{19,20},{20,19},{21,22},{22,21},{2... | collective-permute-start | bytes 393224 | tf_op jit(solution)/shard_map/ppermute | solution.py:332
  3.7 0.6 %collective-permute-start = (bf16[8,64,128]{2,1,0:T(8,128)(2,1)S(1)}, bf16[8,64,128]{2,1,0:T(8,128)(2,1)S(1)}, u32[]{:S(2)}, u32[]{:S(2)}) collective-permute-start(bf16[8,64,128]{2,1,0:T(8,128)(2,1)S(1)} %get-tuple-element.23), channel_id=1, source_target_pairs={{0,1},{1,0},{2,3},{3,2},{4,5},{5,4},{6,7},{7,6},{8,9},{9,8},{10,11... | collective-permute-start | bytes 393224 | tf_op jit(solution)/shard_map/ppermute | solution.py:321
  4.3 1.2 %copy-done.5 = bf16[3,3,3,128,128]{4,3,2,1,0:T(8,128)(2,1)S(1)} copy-done((bf16[3,3,3,128,128]{4,3,2,1,0:T(8,128)(2,1)S(1)}, bf16[3,3,3,128,128]{4,3,2,1,0:T(8,128)(2,1)}, u32[]{:S(2)}) %copy-start.5) | copy-done | bytes 884760
  5.4 0.8 %entry_own.1.before = f32[2,8,64,128]{3,2,1,0:T(8,128)S(1)} custom-call(bf16[8,2,64,128]{3,2,1,0:T(8,128)(2,1)S(1)} %get-tuple-element.29.own, bf16[3,3,3,128,128]{4,3,2,1,0:T(8,128)(2,1)S(1)} %copy-done.5), custom_call_target="tpu_custom_call" | custom-call | flops 600000000 | bytes 1048576 | tf_op jit(solution)/shard_map/entry_own/pallas_call | solution.py:304
  6.2 3.4 %collective-permute-done.1 = bf16[8,64,128]{2,1,0:T(8,128)(2,1)S(1)} collective-permute-done((bf16[8,64,128]{2,1,0:T(8,128)(2,1)S(1)}, bf16[8,64,128]{2,1,0:T(8,128)(2,1)S(1)}, u32[]{:S(2)}, u32[]{:S(2)}) %collective-permute-start.1) | collective-permute-done | bytes 131104 | tf_op jit(solution)/shard_map/ppermute | solution.py:332
  9.7 0.1 collective-permute-start.2
  9.9 0.9 %collective-permute-start.3 = (bf16[4,64,128]{2,1,0:T(8,128)(2,1)S(1)}, bf16[4,64,128]{2,1,0:T(8,128)(2,1)S(1)}, u32[]{:S(2)}, u32[]{:S(2)}) collective-permute-start(bf16[4,64,128]{2,1,0:T(8,128)(2,1)S(1)} %pad_maximum_fusion.3), channel_id=1, source_target_pairs={{0,4},{1,5},{2,6},{3,7},{4,0},{5,1},{6,2},{7,3},{8,12},{9,13},{10,... | collective-permute-start | bytes 196616 | tf_op jit(solution)/shard_map/ppermute | solution.py:352
  10.8 1.2 %copy-done.6 = bf16[3,3,3,128,128]{4,3,2,1,0:T(8,128)(2,1)S(1)} copy-done((bf16[3,3,3,128,128]{4,3,2,1,0:T(8,128)(2,1)S(1)}, bf16[3,3,3,128,128]{4,3,2,1,0:T(8,128)(2,1)}, u32[]{:S(2)}) %copy-start.6) | copy-done | bytes 884760
  12.0 0.7 %entry_side.1.before = f32[2,8,64,128]{3,2,1,0:T(8,128)S(1)} custom-call(bf16[8,64,128]{2,1,0:T(8,128)(2,1)S(1)} %collective-permute-done.y_near, bf16[8,64,128]{2,1,0:T(8,128)(2,1)S(1)} %broadcast_select_fusion.1.y_far, bf16[3,3,3,128,128]{4,3,2,1,0:T(8,128)(2,1)S(1)} %copy-done.6, f32[2,8,64,128]{3,2,1,0:T(8,128)S(1)} %entry_own.1.before), custom_call_target="tpu_custom_call" | custom-call | flops 1000000000 | bytes 1048576 | tf_op jit(solution)/shard_map/entry_side/pallas_call | solution.py:304
  12.6 1.6 %collective-permute-done.3.x_far = bf16[4,64,128]{2,1,0:T(8,128)(2,1)S(1)} collective-permute-done((bf16[4,64,128]{2,1,0:T(8,128)(2,1)S(1)}, bf16[4,64,128]{2,1,0:T(8,128)(2,1)S(1)}, u32[]{:S(2)}, u32[]{:S(2)}) %collective-permute-start.3) | collective-permute-done | bytes 65568 | tf_op jit(solution)/shard_map/ppermute | solution.py:352
  14.2 0.6 %entry_last.1 = (bf16[8,2,64,128]{3,2,1,0:T(8,128)(2,1)S(1)}, bf16[4,32,256]{2,1,0:T(8,128)(2,1)S(1)}) custom-call(bf16[4,64,128]{2,1,0:T(8,128)(2,1)S(1)} %collective-permute-done.2.x_near, bf16[4,64,128]{2,1,0:T(8,128)(2,1)S(1)} %collective-permute-done.3.x_far, bf16[3,3,3,128,128]{4,3,2,1,0:T(8,128)(2,1)S(1)} %copy-done.6, ...), custom_call_target="tpu_custom_call" | custom-call | flops 1000000000 | bytes 1048576 | tf_op jit(solution)/shard_map/entry_last/pallas_call | solution.py:304
  14.9 2.6 %collective-permute-start.5 = (bf16[4,32,256]{2,1,0:T(8,128)(2,1)S(1)}, bf16[4,32,256]{2,1,0:T(8,128)(2,1)S(1)}, u32[]{:S(2)}, u32[]{:S(2)}) collective-permute-start(bf16[4,32,256]{2,1,0:T(8,128)(2,1)S(1)} %get-tuple-element.30.own), channel_id=1, source_target_pairs={{15,16},{16,15},{17,18},{18,17},{19,20},{20,19},{21,22},{22,21},{2... | collective-permute-start | bytes 196616 | tf_op jit(solution)/shard_map/ppermute | solution.py:332
  17.5 2.9 %collective-permute-start.12 = (bf16[8,64,128]{2,1,0:T(8,128)(2,1)S(1)}, bf16[8,64,128]{2,1,0:T(8,128)(2,1)S(1)}, u32[]{:S(2)}, u32[]{:S(2)}) collective-permute-start(bf16[8,64,128]{2,1,0:T(8,128)(2,1)S(1)} %get-tuple-element.47), channel_id=1, source_target_pairs={{15,16},{16,15},{17,18},{18,17},{19,20},{20,19},{21,22},{22,21},{2... | collective-permute-start | bytes 393224 | tf_op jit(solution)/shard_map/ppermute | solution.py:332
  20.4 2.1 %collective-permute-done.5 = bf16[4,32,256]{2,1,0:T(8,128)(2,1)S(1)} collective-permute-done((bf16[4,32,256]{2,1,0:T(8,128)(2,1)S(1)}, bf16[4,32,256]{2,1,0:T(8,128)(2,1)S(1)}, u32[]{:S(2)}, u32[]{:S(2)}) %collective-permute-start.5) | collective-permute-done | bytes 65568 | tf_op jit(solution)/shard_map/ppermute | solution.py:332
  22.8 0.4 collective-permute-start.7
  23.2 0.6 %first_own.1.before = f32[8,32,256]{2,1,0:T(8,128)S(1)} custom-call(bf16[4,32,256]{2,1,0:T(8,128)(2,1)S(1)} %get-tuple-element.30.own, bf16[4,32,256]{2,1,0:T(8,128)(2,1)S(1)} %collective-permute-done.4.y_near, bf16[4,32,256]{2,1,0:T(8,128)(2,1)S(1)} %broadcast_select_fusion.2.y_far, bf16[3,3,3,256,256]{4,3,2,1,0:T(8,128)(2,1)S(1)} %copy-done.1), custom_call_target="tpu_custom_call" | custom-call | flops 700000000 | bytes 1048576 | tf_op jit(solution)/shard_map/first_own/pallas_call | solution.py:304
  23.8 2.4 %collective-permute-done.12 = bf16[8,64,128]{2,1,0:T(8,128)(2,1)S(1)} collective-permute-done((bf16[8,64,128]{2,1,0:T(8,128)(2,1)S(1)}, bf16[8,64,128]{2,1,0:T(8,128)(2,1)S(1)}, u32[]{:S(2)}, u32[]{:S(2)}) %collective-permute-start.12) | collective-permute-done | bytes 131104 | tf_op jit(solution)/shard_map/ppermute | solution.py:332
  26.2 1.8 %collective-permute-done.7.x_far = bf16[3,3,32,256]{3,2,1,0:T(8,128)(2,1)S(1)} collective-permute-done((bf16[3,3,32,256]{3,2,1,0:T(8,128)(2,1)S(1)}, bf16[3,3,32,256]{3,2,1,0:T(8,128)(2,1)S(1)}, u32[]{:S(2)}, u32[]{:S(2)}) %collective-permute-start.7) | collective-permute-done | bytes 147488 | tf_op jit(solution)/shard_map/ppermute | solution.py:352
  28.0 0.7 %first_last.1.own = bf16[8,32,256]{2,1,0:T(8,128)(2,1)S(1)} custom-call(bf16[3,3,32,256]{3,2,1,0:T(8,128)(2,1)S(1)} %collective-permute-done.6.x_near, bf16[3,3,32,256]{3,2,1,0:T(8,128)(2,1)S(1)} %collective-permute-done.7.x_far, bf16[3,3,3,256,256]{4,3,2,1,0:T(8,128)(2,1)S(1)} %copy-done.1, f32[8,32,256]{2,1,0:T(8,128)S(1)} %first_own.1.before), custom_call_target="tpu_custom_call" | custom-call | flops 1000000000 | bytes 1048576 | tf_op jit(solution)/shard_map/first_last/pallas_call | solution.py:304
  28.8 2.6 %collective-permute-start.8 = (bf16[8,32,256]{2,1,0:T(8,128)(2,1)S(1)}, bf16[8,32,256]{2,1,0:T(8,128)(2,1)S(1)}, u32[]{:S(2)}, u32[]{:S(2)}) collective-permute-start(bf16[8,32,256]{2,1,0:T(8,128)(2,1)S(1)} %first_last.1.own), channel_id=1, source_target_pairs={{15,16},{16,15},{17,18},{18,17},{19,20},{20,19},{21,22},{22,21},{2... | collective-permute-start | bytes 393224 | tf_op jit(solution)/shard_map/ppermute | solution.py:332
  31.5 2.8 %collective-permute-done.9.y_near = bf16[8,32,256]{2,1,0:T(8,128)(2,1)S(1)} collective-permute-done((bf16[8,32,256]{2,1,0:T(8,128)(2,1)S(1)}, bf16[8,32,256]{2,1,0:T(8,128)(2,1)S(1)}, u32[]{:S(2)}, u32[]{:S(2)}) %collective-permute-start.9) | collective-permute-done | bytes 131104 | tf_op jit(solution)/shard_map/ppermute | solution.py:321
  34.3 2.6 %collective-permute-start.15 = (bf16[8,32,256]{2,1,0:T(8,128)(2,1)S(1)}, bf16[8,32,256]{2,1,0:T(8,128)(2,1)S(1)}, u32[]{:S(2)}, u32[]{:S(2)}) collective-permute-start(bf16[8,32,256]{2,1,0:T(8,128)(2,1)S(1)} %collective-permute-done.9.y_near), channel_id=1, source_target_pairs={{15,16},{16,15},{17,18},{18,17},{19,20},{20,19},{21,22},{22,21},{2... | collective-permute-start | bytes 393224 | tf_op jit(solution)/shard_map/ppermute | solution.py:332
  36.8 1.3 %decode_skip.1.before = f32[2,8,64,128]{3,2,1,0:T(8,128)S(1)} custom-call(bf16[8,2,64,128]{3,2,1,0:T(8,128)(2,1)S(1)} %get-tuple-element.38.encoded, bf16[8,64,128]{2,1,0:T(8,128)(2,1)S(1)} %collective-permute-done.11.y_near, bf16[8,64,128]{2,1,0:T(8,128)(2,1)S(1)} %broadcast_select_fusion.y_far, bf16[3,3,3,256,128]{4,3,2,1,0:T(8,128)(2,1)S(1)} %copy-done.2), custom_call_target="tpu_custom_call" | custom-call | flops 2000000000 | bytes 1048576 | tf_op jit(solution)/shard_map/decode_skip/pallas_call | solution.py:304
  38.1 0.6 %second_own.1.before = f32[192,256]{1,0:T(8,128)S(1)} custom-call(bf16[8,32,256]{2,1,0:T(8,128)(2,1)S(1)} %first_last.1.own, bf16[8,32,256]{2,1,0:T(8,128)(2,1)S(1)} %collective-permute-done.9.y_near, bf16[3,3,3,256,256]{4,3,2,1,0:T(8,128)(2,1)S(1)} %copy-done), custom_call_target="tpu_custom_call" | custom-call | flops 1000 | bytes 1048576 | tf_op jit(solution)/shard_map/second_own/pallas_call | solution.py:304
  38.8 0.5 %second_far.1.own = bf16[6,32,256]{2,1,0:T(8,128)(2,1)S(1)} custom-call(bf16[8,32,256]{2,1,0:T(8,128)(2,1)S(1)} %collective-permute-done.8.y_far, bf16[3,3,3,256,256]{4,3,2,1,0:T(8,128)(2,1)S(1)} %copy-done, f32[192,256]{1,0:T(8,128)S(1)} %second_own.1.before), custom_call_target="tpu_custom_call" | custom-call | flops 1000 | bytes 1048576 | tf_op jit(solution)/shard_map/second_far/pallas_call | solution.py:304
  39.3 0.6 %beside_own.1.before = f32[192,256]{1,0:T(8,128)S(1)} custom-call(bf16[8,32,256]{2,1,0:T(8,128)(2,1)S(1)} %first_last.1.own, bf16[8,32,256]{2,1,0:T(8,128)(2,1)S(1)} %collective-permute-done.8.y_far, bf16[3,3,3,256,256]{4,3,2,1,0:T(8,128)(2,1)S(1)} %copy-done), custom_call_target="tpu_custom_call" | custom-call | flops 1000 | bytes 1048576 | tf_op jit(solution)/shard_map/beside_own/pallas_call | solution.py:304
  40.0 1.2 %decode_own.1.before = f32[2,8,64,128]{3,2,1,0:T(8,128)S(1)} custom-call(bf16[6,32,256]{2,1,0:T(8,128)(2,1)S(1)} %second_far.1.own, bf16[4,64,128]{2,1,0:T(8,128)(2,1)S(1)} %collective-permute-done.13.x_near, bf16[4,64,128]{2,1,0:T(8,128)(2,1)S(1)} %collective-permute-done.14.x_far, bf16[2,2,2,256,128]{4,3,2,1,0:T(8,128)(2,1)S(1)} %copy-done.3, ...), custom_call_target="tpu_custom_call" | custom-call | flops 1000 | bytes 1048576 | tf_op jit(solution)/shard_map/decode_own/pallas_call | solution.py:304
  41.2 1.4 %collective-permute-done.15.beyond = bf16[8,32,256]{2,1,0:T(8,128)(2,1)S(1)} collective-permute-done((bf16[8,32,256]{2,1,0:T(8,128)(2,1)S(1)}, bf16[8,32,256]{2,1,0:T(8,128)(2,1)S(1)}, u32[]{:S(2)}, u32[]{:S(2)}) %collective-permute-start.15) | collective-permute-done | bytes 131104 | tf_op jit(solution)/shard_map/ppermute | solution.py:332
  42.6 0.4 beside_far.1.y_far
  43.0 1.3 %decode_far.1._ = bf16[8,2,64,128]{3,2,1,0:T(8,128)(2,1)} custom-call(bf16[6,32,256]{2,1,0:T(8,128)(2,1)S(1)} %beside_far.1.y_far, bf16[2,2,2,256,128]{4,3,2,1,0:T(8,128)(2,1)S(1)} %copy-done.3, bf16[3,3,3,256,128]{4,3,2,1,0:T(8,128)(2,1)S(1)} %copy-done.2, f32[2,8,64,128]{3,2,1,0:T(8,128)S(1)} %decode_own.1.before), custom_call_target="tpu_custom_call" | custom-call | flops 2000000000 | bytes 1048576 | tf_op jit(solution)/shard_map/decode_far/pallas_call | solution.py:304
  44.3 1.2 %decode_near.1 = bf16[8,2,64,128]{3,2,1,0:T(8,128)(2,1)} custom-call(bf16[6,32,256]{2,1,0:T(8,128)(2,1)S(1)} %collective-permute-done.10.y_near, bf16[2,2,2,256,128]{4,3,2,1,0:T(8,128)(2,1)S(1)} %copy-done.3, bf16[3,3,3,256,128]{4,3,2,1,0:T(8,128)(2,1)S(1)} %copy-done.2, f32[2,8,64,128]{3,2,1,0:T(8,128)S(1)} %decode_own.1.before, ...), custom_call_target="tpu_custom_call", output_to_operand_aliasing={{}: (4, {})} | custom-call | flops 1000 | bytes 1048576 | tf_op jit(solution)/shard_map/decode_near/pallas_call | solution.py:304
  (45 shorter events, 0.6 us)
Async XLA Ops:
  0.0 0.9 %copy-start.4 = (bf16[8,2,64,128]{3,2,1,0:T(8,128)(2,1)S(1)}, bf16[8,2,64,128]{3,2,1,0:T(8,128)(2,1)}, u32[]{:S(2)}) copy-start(bf16[8,2,64,128]{3,2,1,0:T(8,128)(2,1)} %volume.1) | copy-start | bytes 786436
  1.0 8.6 %collective-permute-start.1 = (bf16[8,64,128]{2,1,0:T(8,128)(2,1)S(1)}, bf16[8,64,128]{2,1,0:T(8,128)(2,1)S(1)}, u32[]{:S(2)}, u32[]{:S(2)}) collective-permute-start(bf16[8,64,128]{2,1,0:T(8,128)(2,1)S(1)} %get-tuple-element.24), channel_id=1, source_target_pairs={{15,16},{16,15},{17,18},{18,17},{19,20},{20,19},{21,22},{22,21},{2... | collective-permute-start | bytes 393224 | tf_op jit(solution)/shard_map/ppermute | solution.py:332
  3.7 6.0 %collective-permute-start = (bf16[8,64,128]{2,1,0:T(8,128)(2,1)S(1)}, bf16[8,64,128]{2,1,0:T(8,128)(2,1)S(1)}, u32[]{:S(2)}, u32[]{:S(2)}) collective-permute-start(bf16[8,64,128]{2,1,0:T(8,128)(2,1)S(1)} %get-tuple-element.23), channel_id=1, source_target_pairs={{0,1},{1,0},{2,3},{3,2},{4,5},{5,4},{6,7},{7,6},{8,9},{9,8},{10,11... | collective-permute-start | bytes 393224 | tf_op jit(solution)/shard_map/ppermute | solution.py:321
  4.3 1.2 %copy-start.5 = (bf16[3,3,3,128,128]{4,3,2,1,0:T(8,128)(2,1)S(1)}, bf16[3,3,3,128,128]{4,3,2,1,0:T(8,128)(2,1)}, u32[]{:S(2)}) copy-start(bf16[3,3,3,128,128]{4,3,2,1,0:T(8,128)(2,1)} %weight.15) | copy-start | bytes 2654212
  5.4 8.8 %copy-start.7 = (bf16[2,2,2,128,256]{4,3,2,1,0:T(8,128)(2,1)S(1)}, bf16[2,2,2,128,256]{4,3,2,1,0:T(8,128)(2,1)}, u32[]{:S(2)}) copy-start(bf16[2,2,2,128,256]{4,3,2,1,0:T(8,128)(2,1)} %down.1) | copy-start | bytes 1572868
  9.7 2.9 %collective-permute-start.2 = (bf16[4,64,128]{2,1,0:T(8,128)(2,1)S(1)}, bf16[4,64,128]{2,1,0:T(8,128)(2,1)S(1)}, u32[]{:S(2)}, u32[]{:S(2)}) collective-permute-start(bf16[4,64,128]{2,1,0:T(8,128)(2,1)S(1)} %pad_maximum_fusion.2), channel_id=1, source_target_pairs={{0,32},{32,0},{64,96},{96,64},{128,160},{160,128},{192,224},{224,1... | collective-permute-start | bytes 196616 | tf_op jit(solution)/shard_map/ppermute | solution.py:351
  9.9 4.4 %collective-permute-start.3 = (bf16[4,64,128]{2,1,0:T(8,128)(2,1)S(1)}, bf16[4,64,128]{2,1,0:T(8,128)(2,1)S(1)}, u32[]{:S(2)}, u32[]{:S(2)}) collective-permute-start(bf16[4,64,128]{2,1,0:T(8,128)(2,1)S(1)} %pad_maximum_fusion.3), channel_id=1, source_target_pairs={{0,4},{1,5},{2,6},{3,7},{4,0},{5,1},{6,2},{7,3},{8,12},{9,13},{10,... | collective-permute-start | bytes 196616 | tf_op jit(solution)/shard_map/ppermute | solution.py:352
  10.8 1.2 %copy-start.6 = (bf16[3,3,3,128,128]{4,3,2,1,0:T(8,128)(2,1)S(1)}, bf16[3,3,3,128,128]{4,3,2,1,0:T(8,128)(2,1)}, u32[]{:S(2)}) copy-start(bf16[3,3,3,128,128]{4,3,2,1,0:T(8,128)(2,1)} %weight.15) | copy-start | bytes 2654212
  12.6 10.5 %copy-start.1 = (bf16[3,3,3,256,256]{4,3,2,1,0:T(8,128)(2,1)S(1)}, bf16[3,3,3,256,256]{4,3,2,1,0:T(8,128)(2,1)}, u32[]{:S(2)}) copy-start(bf16[3,3,3,256,256]{4,3,2,1,0:T(8,128)(2,1)} %weight.17) | copy-start | bytes 10616836
  14.9 7.7 %collective-permute-start.5 = (bf16[4,32,256]{2,1,0:T(8,128)(2,1)S(1)}, bf16[4,32,256]{2,1,0:T(8,128)(2,1)S(1)}, u32[]{:S(2)}, u32[]{:S(2)}) collective-permute-start(bf16[4,32,256]{2,1,0:T(8,128)(2,1)S(1)} %get-tuple-element.30.own), channel_id=1, source_target_pairs={{15,16},{16,15},{17,18},{18,17},{19,20},{20,19},{21,22},{22,21},{2... | collective-permute-start | bytes 196616 | tf_op jit(solution)/shard_map/ppermute | solution.py:332
  17.5 5.0 %collective-permute-start.4 = (bf16[4,32,256]{2,1,0:T(8,128)(2,1)S(1)}, bf16[4,32,256]{2,1,0:T(8,128)(2,1)S(1)}, u32[]{:S(2)}, u32[]{:S(2)}) collective-permute-start(bf16[4,32,256]{2,1,0:T(8,128)(2,1)S(1)} %get-tuple-element.30.own), channel_id=1, source_target_pairs={{0,1},{1,0},{2,3},{3,2},{4,5},{5,4},{6,7},{7,6},{8,9},{9,8},{10,11... | collective-permute-start | bytes 196616 | tf_op jit(solution)/shard_map/ppermute | solution.py:321
  17.5 8.6 %collective-permute-start.12 = (bf16[8,64,128]{2,1,0:T(8,128)(2,1)S(1)}, bf16[8,64,128]{2,1,0:T(8,128)(2,1)S(1)}, u32[]{:S(2)}, u32[]{:S(2)}) collective-permute-start(bf16[8,64,128]{2,1,0:T(8,128)(2,1)S(1)} %get-tuple-element.47), channel_id=1, source_target_pairs={{15,16},{16,15},{17,18},{18,17},{19,20},{20,19},{21,22},{22,21},{2... | collective-permute-start | bytes 393224 | tf_op jit(solution)/shard_map/ppermute | solution.py:332
  20.4 5.8 %collective-permute-start.11 = (bf16[8,64,128]{2,1,0:T(8,128)(2,1)S(1)}, bf16[8,64,128]{2,1,0:T(8,128)(2,1)S(1)}, u32[]{:S(2)}, u32[]{:S(2)}) collective-permute-start(bf16[8,64,128]{2,1,0:T(8,128)(2,1)S(1)} %get-tuple-element.48), channel_id=1, source_target_pairs={{0,1},{1,0},{2,3},{3,2},{4,5},{5,4},{6,7},{7,6},{8,9},{9,8},{10,11... | collective-permute-start | bytes 393224 | tf_op jit(solution)/shard_map/ppermute | solution.py:321
  22.6 3.6 %collective-permute-start.6 = (bf16[3,3,32,256]{3,2,1,0:T(8,128)(2,1)S(1)}, bf16[3,3,32,256]{3,2,1,0:T(8,128)(2,1)S(1)}, u32[]{:S(2)}, u32[]{:S(2)}) collective-permute-start(bf16[3,3,32,256]{3,2,1,0:T(8,128)(2,1)S(1)} %pad_maximum_fusion), channel_id=1, source_target_pairs={{0,32},{32,0},{64,96},{96,64},{128,160},{160,128},{192,224},{224,1... | collective-permute-start | bytes 442376 | tf_op jit(solution)/shard_map/ppermute | solution.py:351
  22.8 14.1 %copy-start.2 = (bf16[3,3,3,256,128]{4,3,2,1,0:T(8,128)(2,1)S(1)}, bf16[3,3,3,256,128]{4,3,2,1,0:T(8,128)(2,1)}, u32[]{:S(2)}) copy-start(bf16[3,3,3,256,128]{4,3,2,1,0:T(8,128)(2,1)} %weight.25) | copy-start | bytes 5308420
  22.8 5.2 %collective-permute-start.7 = (bf16[3,3,32,256]{3,2,1,0:T(8,128)(2,1)S(1)}, bf16[3,3,32,256]{3,2,1,0:T(8,128)(2,1)S(1)}, u32[]{:S(2)}, u32[]{:S(2)}) collective-permute-start(bf16[3,3,32,256]{3,2,1,0:T(8,128)(2,1)S(1)} %pad_maximum_fusion.1), channel_id=1, source_target_pairs={{0,4},{1,5},{2,6},{3,7},{4,0},{5,1},{6,2},{7,3},{8,12},{9,13},{10,... | collective-permute-start | bytes 442376 | tf_op jit(solution)/shard_map/ppermute | solution.py:352
  28.7 5.6 %collective-permute-start.9 = (bf16[8,32,256]{2,1,0:T(8,128)(2,1)S(1)}, bf16[8,32,256]{2,1,0:T(8,128)(2,1)S(1)}, u32[]{:S(2)}, u32[]{:S(2)}) collective-permute-start(bf16[8,32,256]{2,1,0:T(8,128)(2,1)S(1)} %first_last.1.own), channel_id=1, source_target_pairs={{0,1},{1,0},{2,3},{3,2},{4,5},{5,4},{6,7},{7,6},{8,9},{9,8},{10,11... | collective-permute-start | bytes 393224 | tf_op jit(solution)/shard_map/ppermute | solution.py:321
  28.8 9.9 %collective-permute-start.8 = (bf16[8,32,256]{2,1,0:T(8,128)(2,1)S(1)}, bf16[8,32,256]{2,1,0:T(8,128)(2,1)S(1)}, u32[]{:S(2)}, u32[]{:S(2)}) collective-permute-start(bf16[8,32,256]{2,1,0:T(8,128)(2,1)S(1)} %first_last.1.own), channel_id=1, source_target_pairs={{15,16},{16,15},{17,18},{18,17},{19,20},{20,19},{21,22},{22,21},{2... | collective-permute-start | bytes 393224 | tf_op jit(solution)/shard_map/ppermute | solution.py:332
  31.5 6.6 %copy-start = (bf16[3,3,3,256,256]{4,3,2,1,0:T(8,128)(2,1)S(1)}, bf16[3,3,3,256,256]{4,3,2,1,0:T(8,128)(2,1)}, u32[]{:S(2)}) copy-start(bf16[3,3,3,256,256]{4,3,2,1,0:T(8,128)(2,1)} %weight.23) | copy-start | bytes 10616836
  31.5 8.5 %collective-permute-start.13 = (bf16[4,64,128]{2,1,0:T(8,128)(2,1)S(1)}, bf16[4,64,128]{2,1,0:T(8,128)(2,1)S(1)}, u32[]{:S(2)}, u32[]{:S(2)}) collective-permute-start(bf16[4,64,128]{2,1,0:T(8,128)(2,1)S(1)} %get-tuple-element.36), channel_id=1, source_target_pairs={{0,32},{32,0},{64,96},{96,64},{128,160},{160,128},{192,224},{224,1... | collective-permute-start | bytes 196616 | tf_op jit(solution)/shard_map/ppermute | solution.py:351
  31.5 8.5 %collective-permute-start.14 = (bf16[4,64,128]{2,1,0:T(8,128)(2,1)S(1)}, bf16[4,64,128]{2,1,0:T(8,128)(2,1)S(1)}, u32[]{:S(2)}, u32[]{:S(2)}) collective-permute-start(bf16[4,64,128]{2,1,0:T(8,128)(2,1)S(1)} %get-tuple-element.37), channel_id=1, source_target_pairs={{0,4},{1,5},{2,6},{3,7},{4,0},{5,1},{6,2},{7,3},{8,12},{9,13},{10,... | collective-permute-start | bytes 196616 | tf_op jit(solution)/shard_map/ppermute | solution.py:352
  34.3 8.3 %collective-permute-start.15 = (bf16[8,32,256]{2,1,0:T(8,128)(2,1)S(1)}, bf16[8,32,256]{2,1,0:T(8,128)(2,1)S(1)}, u32[]{:S(2)}, u32[]{:S(2)}) collective-permute-start(bf16[8,32,256]{2,1,0:T(8,128)(2,1)S(1)} %collective-permute-done.9.y_near), channel_id=1, source_target_pairs={{15,16},{16,15},{17,18},{18,17},{19,20},{20,19},{21,22},{22,21},{2... | collective-permute-start | bytes 393224 | tf_op jit(solution)/shard_map/ppermute | solution.py:332
  38.8 1.3 %copy-start.3 = (bf16[2,2,2,256,128]{4,3,2,1,0:T(8,128)(2,1)S(1)}, bf16[2,2,2,256,128]{4,3,2,1,0:T(8,128)(2,1)}, u32[]{:S(2)}) copy-start(bf16[2,2,2,256,128]{4,3,2,1,0:T(8,128)(2,1)} %up.5) | copy-start | bytes 1572868
  39.2 5.1 %collective-permute-start.10 = (bf16[6,32,256]{2,1,0:T(8,128)(2,1)S(1)}, bf16[6,32,256]{2,1,0:T(8,128)(2,1)S(1)}, u32[]{:S(2)}, u32[]{:S(2)}) collective-permute-start(bf16[6,32,256]{2,1,0:T(8,128)(2,1)S(1)} %second_far.1.own), channel_id=1, source_target_pairs={{0,1},{1,0},{2,3},{3,2},{4,5},{5,4},{6,7},{7,6},{8,9},{9,8},{10,11... | collective-permute-start | bytes 294920 | tf_op jit(solution)/shard_map/ppermute | solution.py:321

commit v7 on v6

--- a/solution.py
+++ b/solution.py
@@ -269,23 +269,23 @@
     add_rows(total, x_near, x_far, half_weights(weight, 1))
 
 
-def decode_far_kernel(y_far, up, weight, before, decoded, cells, upward, column, sem):
+def decode_far_kernel(y_far, up, weight, before, column, cells, upward):
     _, side = sides()
     gy, ny = lax.axis_index("gy"), lax.axis_size("gy")
     lift(y_far[...].reshape(192, 256), up, 1 - side, upward, 0)
     cells[...] = jnp.where((gy > 0) & (gy < ny - 1), upward[:, 0], 0.0).astype(BF)
     values = before[side] + side_sum(cells, half_weights(weight, 0), side)
     column[...] = leaky_unit(values).astype(BF)
-    copy = pltpu.make_async_copy(column, decoded.at[:, side], sem)
-    copy.start()
-    copy.wait()
-
-
-def decode_near_kernel(y_near, up, weight, before, _, decoded, cells, upward, column, sems):
-    side, _ = sides()
+
+
+def decode_near_kernel(
+    y_near, up, weight, before, far_column, decoded, cells, upward, column, sems
+):
+    side, side_far = sides()
+    copies = [pltpu.make_async_copy(far_column, decoded.at[:, side_far], sems.at[2])]
+    copies[0].start()
     lift(y_near[...].reshape(192, 256), up, 1 - side, upward, 0)
     cells[...] = upward[:, 0].astype(BF)
-    copies = []
     for half in range(2):
         rows = slice(4 * half, 4 * half + 4)
         values = before[side, rows] + side_sum(cells, half_weights(weight, 0), side, 4 * half, 4)
@@ -498,32 +498,29 @@
         weight_decoder,
         total,
     )
-    (decoded,) = call(
+    (far_column,) = call(
         decode_far_kernel,
-        [((8, 2, 64, 128), BF)],
-        [tall, upward, line, ((), None)],
+        [line],
+        [tall, upward],
         "decode_far",
         2000000000,
         beside,
         weight_upward,
         weight_decoder,
         total,
-        hbm_out=True,
     )
     (decoded,) = call(
         decode_near_kernel,
         [((8, 2, 64, 128), BF)],
-        [tall, upward, line, ((2,), None)],
+        [tall, upward, line, ((3,), None)],
         "decode_near",
         1000,
         h1,
         weight_upward,
         weight_decoder,
         total,
-        decoded,
-        remote=(4,),
+        far_column,
         hbm_out=True,
-        aliases=((4, 0),),
     )
     return decoded
 

time: 46 us -> 45.8 us (level)
  Pallas kernels: 10.6 us -> 9.89 us
    pallas_call x14, Pallas kernels: 10.6 us -> 9.89 us  [call(): pl.pallas_call(kernel, out_shape=[jax.ShapeDtypeStruct(shape, dtype) for...]
  transfers between devices with their start and end apart: 16 -> 16, of which waited for: 7 -> 8; matrix products, arithmetic and copies ran while one was open for 0% -> 0% of each run, Pallas kernels for 17% -> 16%
where the time goes in v7:
time: 45.8 us; the launch traced here: 45.4 us
  waiting for transfers between devices  15.8 us (34%)
  starting transfers between devices  15.6 us (34%)
  Pallas kernels  9.89 us (22%)
  local copies, waits for them, and re-layouts  3.37 us (7%)
  between operations  0.51 us (1%)
    ppermute x5, starting transfers between devices, swap_far(): return lax.ppermute(cells, ('gx', 'gy'), far)  13.4 us
    pallas_call x14, Pallas kernels, call(): pl.pallas_call(kernel, out_shape=[jax.ShapeDtypeStruct(shape, dtype) for...  9.89 us
    ppermute x5, waiting for transfers between devices, swap_far(): return lax.ppermute(cells, ('gx', 'gy'), far)  9.29 us
    ppermute x3, waiting for transfers between devices, swap_x(): return (got, lax.ppermute(far_cells, ('gx', 'gy'), far))  3.36 us
    unnamed x16, local copies, waits for them, and re-layouts  3.31 us
    ppermute x5, waiting for transfers between devices, swap_near(): lax.ppermute(cells, 'gy', [(i, i ^ 1) for i in range(lax.axis_size('gy'))])  3.11 us
    ppermute x3, starting transfers between devices, swap_x(): return (got, lax.ppermute(far_cells, ('gx', 'gy'), far))  1.31 us
  transfers between devices with their start and end apart: 16, of which 8 were waited for; matrix products, arithmetic and copies ran while one was open for 0% of the time, Pallas kernels for 16%

profile of v7, /device:TPU:128, one launch (start us, length us, event | category | flops | bytes accessed | tf_op | source)
XLA Modules:
  0.0 45.4 jit_solution(3456952048302603546)
XLA Ops:
  0.0 0.9 %copy-done.4 = bf16[8,2,64,128]{3,2,1,0:T(8,128)(2,1)S(1)} copy-done((bf16[8,2,64,128]{3,2,1,0:T(8,128)(2,1)S(1)}, bf16[8,2,64,128]{3,2,1,0:T(8,128)(2,1)}, u32[]{:S(2)}) %copy-start.4) | copy-done | bytes 262168
  1.0 2.6 %collective-permute-start.1 = (bf16[8,64,128]{2,1,0:T(8,128)(2,1)S(1)}, bf16[8,64,128]{2,1,0:T(8,128)(2,1)S(1)}, u32[]{:S(2)}, u32[]{:S(2)}) collective-permute-start(bf16[8,64,128]{2,1,0:T(8,128)(2,1)S(1)} %get-tuple-element.24), channel_id=1, source_target_pairs={{15,16},{16,15},{17,18},{18,17},{19,20},{20,19},{21,22},{22,21},{2... | collective-permute-start | bytes 393224 | tf_op jit(solution)/shard_map/ppermute | solution.py:332
  3.7 0.6 %collective-permute-start = (bf16[8,64,128]{2,1,0:T(8,128)(2,1)S(1)}, bf16[8,64,128]{2,1,0:T(8,128)(2,1)S(1)}, u32[]{:S(2)}, u32[]{:S(2)}) collective-permute-start(bf16[8,64,128]{2,1,0:T(8,128)(2,1)S(1)} %get-tuple-element.23), channel_id=1, source_target_pairs={{0,1},{1,0},{2,3},{3,2},{4,5},{5,4},{6,7},{7,6},{8,9},{9,8},{10,11... | collective-permute-start | bytes 393224 | tf_op jit(solution)/shard_map/ppermute | solution.py:321
  4.3 1.2 %copy-done.5 = bf16[3,3,3,128,128]{4,3,2,1,0:T(8,128)(2,1)S(1)} copy-done((bf16[3,3,3,128,128]{4,3,2,1,0:T(8,128)(2,1)S(1)}, bf16[3,3,3,128,128]{4,3,2,1,0:T(8,128)(2,1)}, u32[]{:S(2)}) %copy-start.5) | copy-done | bytes 884760
  5.4 0.8 %entry_own.1.before = f32[2,8,64,128]{3,2,1,0:T(8,128)S(1)} custom-call(bf16[8,2,64,128]{3,2,1,0:T(8,128)(2,1)S(1)} %get-tuple-element.29.own, bf16[3,3,3,128,128]{4,3,2,1,0:T(8,128)(2,1)S(1)} %copy-done.5), custom_call_target="tpu_custom_call" | custom-call | flops 600000000 | bytes 1048576 | tf_op jit(solution)/shard_map/entry_own/pallas_call | solution.py:304
  6.2 3.4 %collective-permute-done.1 = bf16[8,64,128]{2,1,0:T(8,128)(2,1)S(1)} collective-permute-done((bf16[8,64,128]{2,1,0:T(8,128)(2,1)S(1)}, bf16[8,64,128]{2,1,0:T(8,128)(2,1)S(1)}, u32[]{:S(2)}, u32[]{:S(2)}) %collective-permute-start.1) | collective-permute-done | bytes 131104 | tf_op jit(solution)/shard_map/ppermute | solution.py:332
  9.9 0.9 %collective-permute-start.3 = (bf16[4,64,128]{2,1,0:T(8,128)(2,1)S(1)}, bf16[4,64,128]{2,1,0:T(8,128)(2,1)S(1)}, u32[]{:S(2)}, u32[]{:S(2)}) collective-permute-start(bf16[4,64,128]{2,1,0:T(8,128)(2,1)S(1)} %pad_maximum_fusion.3), channel_id=1, source_target_pairs={{0,4},{1,5},{2,6},{3,7},{4,0},{5,1},{6,2},{7,3},{8,12},{9,13},{10,... | collective-permute-start | bytes 196616 | tf_op jit(solution)/shard_map/ppermute | solution.py:352
  10.8 1.2 %copy-done.6 = bf16[3,3,3,128,128]{4,3,2,1,0:T(8,128)(2,1)S(1)} copy-done((bf16[3,3,3,128,128]{4,3,2,1,0:T(8,128)(2,1)S(1)}, bf16[3,3,3,128,128]{4,3,2,1,0:T(8,128)(2,1)}, u32[]{:S(2)}) %copy-start.6) | copy-done | bytes 884760
  12.0 0.7 %entry_side.1.before = f32[2,8,64,128]{3,2,1,0:T(8,128)S(1)} custom-call(bf16[8,64,128]{2,1,0:T(8,128)(2,1)S(1)} %collective-permute-done.y_near, bf16[8,64,128]{2,1,0:T(8,128)(2,1)S(1)} %broadcast_select_fusion.1.y_far, bf16[3,3,3,128,128]{4,3,2,1,0:T(8,128)(2,1)S(1)} %copy-done.6, f32[2,8,64,128]{3,2,1,0:T(8,128)S(1)} %entry_own.1.before), custom_call_target="tpu_custom_call" | custom-call | flops 1000000000 | bytes 1048576 | tf_op jit(solution)/shard_map/entry_side/pallas_call | solution.py:304
  12.6 1.6 %collective-permute-done.3.x_far = bf16[4,64,128]{2,1,0:T(8,128)(2,1)S(1)} collective-permute-done((bf16[4,64,128]{2,1,0:T(8,128)(2,1)S(1)}, bf16[4,64,128]{2,1,0:T(8,128)(2,1)S(1)}, u32[]{:S(2)}, u32[]{:S(2)}) %collective-permute-start.3) | collective-permute-done | bytes 65568 | tf_op jit(solution)/shard_map/ppermute | solution.py:352
  14.2 0.6 %entry_last.1 = (bf16[8,2,64,128]{3,2,1,0:T(8,128)(2,1)S(1)}, bf16[4,32,256]{2,1,0:T(8,128)(2,1)S(1)}) custom-call(bf16[4,64,128]{2,1,0:T(8,128)(2,1)S(1)} %collective-permute-done.2.x_near, bf16[4,64,128]{2,1,0:T(8,128)(2,1)S(1)} %collective-permute-done.3.x_far, bf16[3,3,3,128,128]{4,3,2,1,0:T(8,128)(2,1)S(1)} %copy-done.6, ...), custom_call_target="tpu_custom_call" | custom-call | flops 1000000000 | bytes 1048576 | tf_op jit(solution)/shard_map/entry_last/pallas_call | solution.py:304
  14.9 2.6 %collective-permute-start.5 = (bf16[4,32,256]{2,1,0:T(8,128)(2,1)S(1)}, bf16[4,32,256]{2,1,0:T(8,128)(2,1)S(1)}, u32[]{:S(2)}, u32[]{:S(2)}) collective-permute-start(bf16[4,32,256]{2,1,0:T(8,128)(2,1)S(1)} %get-tuple-element.30.own), channel_id=1, source_target_pairs={{15,16},{16,15},{17,18},{18,17},{19,20},{20,19},{21,22},{22,21},{2... | collective-permute-start | bytes 196616 | tf_op jit(solution)/shard_map/ppermute | solution.py:332
  17.5 2.9 %collective-permute-start.12 = (bf16[8,64,128]{2,1,0:T(8,128)(2,1)S(1)}, bf16[8,64,128]{2,1,0:T(8,128)(2,1)S(1)}, u32[]{:S(2)}, u32[]{:S(2)}) collective-permute-start(bf16[8,64,128]{2,1,0:T(8,128)(2,1)S(1)} %get-tuple-element.47), channel_id=1, source_target_pairs={{15,16},{16,15},{17,18},{18,17},{19,20},{20,19},{21,22},{22,21},{2... | collective-permute-start | bytes 393224 | tf_op jit(solution)/shard_map/ppermute | solution.py:332
  20.4 2.1 %collective-permute-done.5 = bf16[4,32,256]{2,1,0:T(8,128)(2,1)S(1)} collective-permute-done((bf16[4,32,256]{2,1,0:T(8,128)(2,1)S(1)}, bf16[4,32,256]{2,1,0:T(8,128)(2,1)S(1)}, u32[]{:S(2)}, u32[]{:S(2)}) %collective-permute-start.5) | collective-permute-done | bytes 65568 | tf_op jit(solution)/shard_map/ppermute | solution.py:332
  22.8 0.4 collective-permute-start.7
  23.2 0.6 %first_own.1.before = f32[8,32,256]{2,1,0:T(8,128)S(1)} custom-call(bf16[4,32,256]{2,1,0:T(8,128)(2,1)S(1)} %get-tuple-element.30.own, bf16[4,32,256]{2,1,0:T(8,128)(2,1)S(1)} %collective-permute-done.4.y_near, bf16[4,32,256]{2,1,0:T(8,128)(2,1)S(1)} %broadcast_select_fusion.2.y_far, bf16[3,3,3,256,256]{4,3,2,1,0:T(8,128)(2,1)S(1)} %copy-done.1), custom_call_target="tpu_custom_call" | custom-call | flops 700000000 | bytes 1048576 | tf_op jit(solution)/shard_map/first_own/pallas_call | solution.py:304
  23.8 2.4 %collective-permute-done.12 = bf16[8,64,128]{2,1,0:T(8,128)(2,1)S(1)} collective-permute-done((bf16[8,64,128]{2,1,0:T(8,128)(2,1)S(1)}, bf16[8,64,128]{2,1,0:T(8,128)(2,1)S(1)}, u32[]{:S(2)}, u32[]{:S(2)}) %collective-permute-start.12) | collective-permute-done | bytes 131104 | tf_op jit(solution)/shard_map/ppermute | solution.py:332
  26.2 1.8 %collective-permute-done.7.x_far = bf16[3,3,32,256]{3,2,1,0:T(8,128)(2,1)S(1)} collective-permute-done((bf16[3,3,32,256]{3,2,1,0:T(8,128)(2,1)S(1)}, bf16[3,3,32,256]{3,2,1,0:T(8,128)(2,1)S(1)}, u32[]{:S(2)}, u32[]{:S(2)}) %collective-permute-start.7) | collective-permute-done | bytes 147488 | tf_op jit(solution)/shard_map/ppermute | solution.py:352
  28.0 0.7 %first_last.1.own = bf16[8,32,256]{2,1,0:T(8,128)(2,1)S(1)} custom-call(bf16[3,3,32,256]{3,2,1,0:T(8,128)(2,1)S(1)} %collective-permute-done.6.x_near, bf16[3,3,32,256]{3,2,1,0:T(8,128)(2,1)S(1)} %collective-permute-done.7.x_far, bf16[3,3,3,256,256]{4,3,2,1,0:T(8,128)(2,1)S(1)} %copy-done.1, f32[8,32,256]{2,1,0:T(8,128)S(1)} %first_own.1.before), custom_call_target="tpu_custom_call" | custom-call | flops 1000000000 | bytes 1048576 | tf_op jit(solution)/shard_map/first_last/pallas_call | solution.py:304
  28.8 2.6 %collective-permute-start.8 = (bf16[8,32,256]{2,1,0:T(8,128)(2,1)S(1)}, bf16[8,32,256]{2,1,0:T(8,128)(2,1)S(1)}, u32[]{:S(2)}, u32[]{:S(2)}) collective-permute-start(bf16[8,32,256]{2,1,0:T(8,128)(2,1)S(1)} %first_last.1.own), channel_id=1, source_target_pairs={{15,16},{16,15},{17,18},{18,17},{19,20},{20,19},{21,22},{22,21},{2... | collective-permute-start | bytes 393224 | tf_op jit(solution)/shard_map/ppermute | solution.py:332
  31.5 2.8 %collective-permute-done.9.y_near = bf16[8,32,256]{2,1,0:T(8,128)(2,1)S(1)} collective-permute-done((bf16[8,32,256]{2,1,0:T(8,128)(2,1)S(1)}, bf16[8,32,256]{2,1,0:T(8,128)(2,1)S(1)}, u32[]{:S(2)}, u32[]{:S(2)}) %collective-permute-start.9) | collective-permute-done | bytes 131104 | tf_op jit(solution)/shard_map/ppermute | solution.py:321
  34.3 2.6 %collective-permute-start.15 = (bf16[8,32,256]{2,1,0:T(8,128)(2,1)S(1)}, bf16[8,32,256]{2,1,0:T(8,128)(2,1)S(1)}, u32[]{:S(2)}, u32[]{:S(2)}) collective-permute-start(bf16[8,32,256]{2,1,0:T(8,128)(2,1)S(1)} %collective-permute-done.9.y_near), channel_id=1, source_target_pairs={{15,16},{16,15},{17,18},{18,17},{19,20},{20,19},{21,22},{22,21},{2... | collective-permute-start | bytes 393224 | tf_op jit(solution)/shard_map/ppermute | solution.py:332
  36.8 1.3 %decode_skip.1.before = f32[2,8,64,128]{3,2,1,0:T(8,128)S(1)} custom-call(bf16[8,2,64,128]{3,2,1,0:T(8,128)(2,1)S(1)} %get-tuple-element.38.encoded, bf16[8,64,128]{2,1,0:T(8,128)(2,1)S(1)} %collective-permute-done.11.y_near, bf16[8,64,128]{2,1,0:T(8,128)(2,1)S(1)} %broadcast_select_fusion.y_far, bf16[3,3,3,256,128]{4,3,2,1,0:T(8,128)(2,1)S(1)} %copy-done.2), custom_call_target="tpu_custom_call" | custom-call | flops 2000000000 | bytes 1048576 | tf_op jit(solution)/shard_map/decode_skip/pallas_call | solution.py:304
  38.1 0.6 %second_own.1.before = f32[192,256]{1,0:T(8,128)S(1)} custom-call(bf16[8,32,256]{2,1,0:T(8,128)(2,1)S(1)} %first_last.1.own, bf16[8,32,256]{2,1,0:T(8,128)(2,1)S(1)} %collective-permute-done.9.y_near, bf16[3,3,3,256,256]{4,3,2,1,0:T(8,128)(2,1)S(1)} %copy-done), custom_call_target="tpu_custom_call" | custom-call | flops 1000 | bytes 1048576 | tf_op jit(solution)/shard_map/second_own/pallas_call | solution.py:304
  38.8 0.5 %second_far.1.own = bf16[6,32,256]{2,1,0:T(8,128)(2,1)S(1)} custom-call(bf16[8,32,256]{2,1,0:T(8,128)(2,1)S(1)} %collective-permute-done.8.y_far, bf16[3,3,3,256,256]{4,3,2,1,0:T(8,128)(2,1)S(1)} %copy-done, f32[192,256]{1,0:T(8,128)S(1)} %second_own.1.before), custom_call_target="tpu_custom_call" | custom-call | flops 1000 | bytes 1048576 | tf_op jit(solution)/shard_map/second_far/pallas_call | solution.py:304
  39.3 0.6 %beside_own.1.before = f32[192,256]{1,0:T(8,128)S(1)} custom-call(bf16[8,32,256]{2,1,0:T(8,128)(2,1)S(1)} %first_last.1.own, bf16[8,32,256]{2,1,0:T(8,128)(2,1)S(1)} %collective-permute-done.8.y_far, bf16[3,3,3,256,256]{4,3,2,1,0:T(8,128)(2,1)S(1)} %copy-done), custom_call_target="tpu_custom_call" | custom-call | flops 1000 | bytes 1048576 | tf_op jit(solution)/shard_map/beside_own/pallas_call | solution.py:304
  40.0 1.2 %decode_own.1.before = f32[2,8,64,128]{3,2,1,0:T(8,128)S(1)} custom-call(bf16[6,32,256]{2,1,0:T(8,128)(2,1)S(1)} %second_far.1.own, bf16[4,64,128]{2,1,0:T(8,128)(2,1)S(1)} %collective-permute-done.13.x_near, bf16[4,64,128]{2,1,0:T(8,128)(2,1)S(1)} %collective-permute-done.14.x_far, bf16[2,2,2,256,128]{4,3,2,1,0:T(8,128)(2,1)S(1)} %copy-done.3, ...), custom_call_target="tpu_custom_call" | custom-call | flops 1000 | bytes 1048576 | tf_op jit(solution)/shard_map/decode_own/pallas_call | solution.py:304
  41.2 1.4 %collective-permute-done.15.beyond = bf16[8,32,256]{2,1,0:T(8,128)(2,1)S(1)} collective-permute-done((bf16[8,32,256]{2,1,0:T(8,128)(2,1)S(1)}, bf16[8,32,256]{2,1,0:T(8,128)(2,1)S(1)}, u32[]{:S(2)}, u32[]{:S(2)}) %collective-permute-start.15) | collective-permute-done | bytes 131104 | tf_op jit(solution)/shard_map/ppermute | solution.py:332
  42.6 0.4 beside_far.1.y_far
  43.0 0.6 %decode_far.1.far_column = bf16[8,64,128]{2,1,0:T(8,128)(2,1)S(1)} custom-call(bf16[6,32,256]{2,1,0:T(8,128)(2,1)S(1)} %beside_far.1.y_far, bf16[2,2,2,256,128]{4,3,2,1,0:T(8,128)(2,1)S(1)} %copy-done.3, bf16[3,3,3,256,128]{4,3,2,1,0:T(8,128)(2,1)S(1)} %copy-done.2, f32[2,8,64,128]{3,2,1,0:T(8,128)S(1)} %decode_own.1.before), custom_call_target="tpu_custom_call" | custom-call | flops 2000000000 | bytes 1048576 | tf_op jit(solution)/shard_map/decode_far/pallas_call | solution.py:304
  43.6 0.3 collective-permute-done.10.y_near
  44.0 1.2 %decode_near.1 = bf16[8,2,64,128]{3,2,1,0:T(8,128)(2,1)} custom-call(bf16[6,32,256]{2,1,0:T(8,128)(2,1)S(1)} %collective-permute-done.10.y_near, bf16[2,2,2,256,128]{4,3,2,1,0:T(8,128)(2,1)S(1)} %copy-done.3, bf16[3,3,3,256,128]{4,3,2,1,0:T(8,128)(2,1)S(1)} %copy-done.2, f32[2,8,64,128]{3,2,1,0:T(8,128)S(1)} %decode_own.1.before, ...), custom_call_target="tpu_custom_call" | custom-call | flops 1000 | bytes 1048576 | tf_op jit(solution)/shard_map/decode_near/pallas_call | solution.py:304
  (45 shorter events, 0.7 us)
Async XLA Ops:
  0.0 0.9 %copy-start.4 = (bf16[8,2,64,128]{3,2,1,0:T(8,128)(2,1)S(1)}, bf16[8,2,64,128]{3,2,1,0:T(8,128)(2,1)}, u32[]{:S(2)}) copy-start(bf16[8,2,64,128]{3,2,1,0:T(8,128)(2,1)} %volume.1) | copy-start | bytes 786436
  1.0 8.6 %collective-permute-start.1 = (bf16[8,64,128]{2,1,0:T(8,128)(2,1)S(1)}, bf16[8,64,128]{2,1,0:T(8,128)(2,1)S(1)}, u32[]{:S(2)}, u32[]{:S(2)}) collective-permute-start(bf16[8,64,128]{2,1,0:T(8,128)(2,1)S(1)} %get-tuple-element.24), channel_id=1, source_target_pairs={{15,16},{16,15},{17,18},{18,17},{19,20},{20,19},{21,22},{22,21},{2... | collective-permute-start | bytes 393224 | tf_op jit(solution)/shard_map/ppermute | solution.py:332
  3.7 6.0 %collective-permute-start = (bf16[8,64,128]{2,1,0:T(8,128)(2,1)S(1)}, bf16[8,64,128]{2,1,0:T(8,128)(2,1)S(1)}, u32[]{:S(2)}, u32[]{:S(2)}) collective-permute-start(bf16[8,64,128]{2,1,0:T(8,128)(2,1)S(1)} %get-tuple-element.23), channel_id=1, source_target_pairs={{0,1},{1,0},{2,3},{3,2},{4,5},{5,4},{6,7},{7,6},{8,9},{9,8},{10,11... | collective-permute-start | bytes 393224 | tf_op jit(solution)/shard_map/ppermute | solution.py:321
  4.3 1.2 %copy-start.5 = (bf16[3,3,3,128,128]{4,3,2,1,0:T(8,128)(2,1)S(1)}, bf16[3,3,3,128,128]{4,3,2,1,0:T(8,128)(2,1)}, u32[]{:S(2)}) copy-start(bf16[3,3,3,128,128]{4,3,2,1,0:T(8,128)(2,1)} %weight.15) | copy-start | bytes 2654212
  5.4 8.8 %copy-start.7 = (bf16[2,2,2,128,256]{4,3,2,1,0:T(8,128)(2,1)S(1)}, bf16[2,2,2,128,256]{4,3,2,1,0:T(8,128)(2,1)}, u32[]{:S(2)}) copy-start(bf16[2,2,2,128,256]{4,3,2,1,0:T(8,128)(2,1)} %down.1) | copy-start | bytes 1572868
  9.7 2.9 %collective-permute-start.2 = (bf16[4,64,128]{2,1,0:T(8,128)(2,1)S(1)}, bf16[4,64,128]{2,1,0:T(8,128)(2,1)S(1)}, u32[]{:S(2)}, u32[]{:S(2)}) collective-permute-start(bf16[4,64,128]{2,1,0:T(8,128)(2,1)S(1)} %pad_maximum_fusion.2), channel_id=1, source_target_pairs={{0,32},{32,0},{64,96},{96,64},{128,160},{160,128},{192,224},{224,1... | collective-permute-start | bytes 196616 | tf_op jit(solution)/shard_map/ppermute | solution.py:351
  9.9 4.4 %collective-permute-start.3 = (bf16[4,64,128]{2,1,0:T(8,128)(2,1)S(1)}, bf16[4,64,128]{2,1,0:T(8,128)(2,1)S(1)}, u32[]{:S(2)}, u32[]{:S(2)}) collective-permute-start(bf16[4,64,128]{2,1,0:T(8,128)(2,1)S(1)} %pad_maximum_fusion.3), channel_id=1, source_target_pairs={{0,4},{1,5},{2,6},{3,7},{4,0},{5,1},{6,2},{7,3},{8,12},{9,13},{10,... | collective-permute-start | bytes 196616 | tf_op jit(solution)/shard_map/ppermute | solution.py:352
  10.8 1.2 %copy-start.6 = (bf16[3,3,3,128,128]{4,3,2,1,0:T(8,128)(2,1)S(1)}, bf16[3,3,3,128,128]{4,3,2,1,0:T(8,128)(2,1)}, u32[]{:S(2)}) copy-start(bf16[3,3,3,128,128]{4,3,2,1,0:T(8,128)(2,1)} %weight.15) | copy-start | bytes 2654212
  12.6 10.5 %copy-start.1 = (bf16[3,3,3,256,256]{4,3,2,1,0:T(8,128)(2,1)S(1)}, bf16[3,3,3,256,256]{4,3,2,1,0:T(8,128)(2,1)}, u32[]{:S(2)}) copy-start(bf16[3,3,3,256,256]{4,3,2,1,0:T(8,128)(2,1)} %weight.17) | copy-start | bytes 10616836
  14.9 7.7 %collective-permute-start.5 = (bf16[4,32,256]{2,1,0:T(8,128)(2,1)S(1)}, bf16[4,32,256]{2,1,0:T(8,128)(2,1)S(1)}, u32[]{:S(2)}, u32[]{:S(2)}) collective-permute-start(bf16[4,32,256]{2,1,0:T(8,128)(2,1)S(1)} %get-tuple-element.30.own), channel_id=1, source_target_pairs={{15,16},{16,15},{17,18},{18,17},{19,20},{20,19},{21,22},{22,21},{2... | collective-permute-start | bytes 196616 | tf_op jit(solution)/shard_map/ppermute | solution.py:332
  17.5 5.0 %collective-permute-start.4 = (bf16[4,32,256]{2,1,0:T(8,128)(2,1)S(1)}, bf16[4,32,256]{2,1,0:T(8,128)(2,1)S(1)}, u32[]{:S(2)}, u32[]{:S(2)}) collective-permute-start(bf16[4,32,256]{2,1,0:T(8,128)(2,1)S(1)} %get-tuple-element.30.own), channel_id=1, source_target_pairs={{0,1},{1,0},{2,3},{3,2},{4,5},{5,4},{6,7},{7,6},{8,9},{9,8},{10,11... | collective-permute-start | bytes 196616 | tf_op jit(solution)/shard_map/ppermute | solution.py:321
  17.5 8.6 %collective-permute-start.12 = (bf16[8,64,128]{2,1,0:T(8,128)(2,1)S(1)}, bf16[8,64,128]{2,1,0:T(8,128)(2,1)S(1)}, u32[]{:S(2)}, u32[]{:S(2)}) collective-permute-start(bf16[8,64,128]{2,1,0:T(8,128)(2,1)S(1)} %get-tuple-element.47), channel_id=1, source_target_pairs={{15,16},{16,15},{17,18},{18,17},{19,20},{20,19},{21,22},{22,21},{2... | collective-permute-start | bytes 393224 | tf_op jit(solution)/shard_map/ppermute | solution.py:332
  20.4 5.8 %collective-permute-start.11 = (bf16[8,64,128]{2,1,0:T(8,128)(2,1)S(1)}, bf16[8,64,128]{2,1,0:T(8,128)(2,1)S(1)}, u32[]{:S(2)}, u32[]{:S(2)}) collective-permute-start(bf16[8,64,128]{2,1,0:T(8,128)(2,1)S(1)} %get-tuple-element.48), channel_id=1, source_target_pairs={{0,1},{1,0},{2,3},{3,2},{4,5},{5,4},{6,7},{7,6},{8,9},{9,8},{10,11... | collective-permute-start | bytes 393224 | tf_op jit(solution)/shard_map/ppermute | solution.py:321
  22.6 3.6 %collective-permute-start.6 = (bf16[3,3,32,256]{3,2,1,0:T(8,128)(2,1)S(1)}, bf16[3,3,32,256]{3,2,1,0:T(8,128)(2,1)S(1)}, u32[]{:S(2)}, u32[]{:S(2)}) collective-permute-start(bf16[3,3,32,256]{3,2,1,0:T(8,128)(2,1)S(1)} %pad_maximum_fusion), channel_id=1, source_target_pairs={{0,32},{32,0},{64,96},{96,64},{128,160},{160,128},{192,224},{224,1... | collective-permute-start | bytes 442376 | tf_op jit(solution)/shard_map/ppermute | solution.py:351
  22.8 14.1 %copy-start.2 = (bf16[3,3,3,256,128]{4,3,2,1,0:T(8,128)(2,1)S(1)}, bf16[3,3,3,256,128]{4,3,2,1,0:T(8,128)(2,1)}, u32[]{:S(2)}) copy-start(bf16[3,3,3,256,128]{4,3,2,1,0:T(8,128)(2,1)} %weight.25) | copy-start | bytes 5308420
  22.8 5.2 %collective-permute-start.7 = (bf16[3,3,32,256]{3,2,1,0:T(8,128)(2,1)S(1)}, bf16[3,3,32,256]{3,2,1,0:T(8,128)(2,1)S(1)}, u32[]{:S(2)}, u32[]{:S(2)}) collective-permute-start(bf16[3,3,32,256]{3,2,1,0:T(8,128)(2,1)S(1)} %pad_maximum_fusion.1), channel_id=1, source_target_pairs={{0,4},{1,5},{2,6},{3,7},{4,0},{5,1},{6,2},{7,3},{8,12},{9,13},{10,... | collective-permute-start | bytes 442376 | tf_op jit(solution)/shard_map/ppermute | solution.py:352
  28.7 5.6 %collective-permute-start.9 = (bf16[8,32,256]{2,1,0:T(8,128)(2,1)S(1)}, bf16[8,32,256]{2,1,0:T(8,128)(2,1)S(1)}, u32[]{:S(2)}, u32[]{:S(2)}) collective-permute-start(bf16[8,32,256]{2,1,0:T(8,128)(2,1)S(1)} %first_last.1.own), channel_id=1, source_target_pairs={{0,1},{1,0},{2,3},{3,2},{4,5},{5,4},{6,7},{7,6},{8,9},{9,8},{10,11... | collective-permute-start | bytes 393224 | tf_op jit(solution)/shard_map/ppermute | solution.py:321
  28.8 9.9 %collective-permute-start.8 = (bf16[8,32,256]{2,1,0:T(8,128)(2,1)S(1)}, bf16[8,32,256]{2,1,0:T(8,128)(2,1)S(1)}, u32[]{:S(2)}, u32[]{:S(2)}) collective-permute-start(bf16[8,32,256]{2,1,0:T(8,128)(2,1)S(1)} %first_last.1.own), channel_id=1, source_target_pairs={{15,16},{16,15},{17,18},{18,17},{19,20},{20,19},{21,22},{22,21},{2... | collective-permute-start | bytes 393224 | tf_op jit(solution)/shard_map/ppermute | solution.py:332
  31.5 6.6 %copy-start = (bf16[3,3,3,256,256]{4,3,2,1,0:T(8,128)(2,1)S(1)}, bf16[3,3,3,256,256]{4,3,2,1,0:T(8,128)(2,1)}, u32[]{:S(2)}) copy-start(bf16[3,3,3,256,256]{4,3,2,1,0:T(8,128)(2,1)} %weight.23) | copy-start | bytes 10616836
  31.5 8.5 %collective-permute-start.13 = (bf16[4,64,128]{2,1,0:T(8,128)(2,1)S(1)}, bf16[4,64,128]{2,1,0:T(8,128)(2,1)S(1)}, u32[]{:S(2)}, u32[]{:S(2)}) collective-permute-start(bf16[4,64,128]{2,1,0:T(8,128)(2,1)S(1)} %get-tuple-element.36), channel_id=1, source_target_pairs={{0,32},{32,0},{64,96},{96,64},{128,160},{160,128},{192,224},{224,1... | collective-permute-start | bytes 196616 | tf_op jit(solution)/shard_map/ppermute | solution.py:351
  31.5 8.5 %collective-permute-start.14 = (bf16[4,64,128]{2,1,0:T(8,128)(2,1)S(1)}, bf16[4,64,128]{2,1,0:T(8,128)(2,1)S(1)}, u32[]{:S(2)}, u32[]{:S(2)}) collective-permute-start(bf16[4,64,128]{2,1,0:T(8,128)(2,1)S(1)} %get-tuple-element.37), channel_id=1, source_target_pairs={{0,4},{1,5},{2,6},{3,7},{4,0},{5,1},{6,2},{7,3},{8,12},{9,13},{10,... | collective-permute-start | bytes 196616 | tf_op jit(solution)/shard_map/ppermute | solution.py:352
  34.3 8.3 %collective-permute-start.15 = (bf16[8,32,256]{2,1,0:T(8,128)(2,1)S(1)}, bf16[8,32,256]{2,1,0:T(8,128)(2,1)S(1)}, u32[]{:S(2)}, u32[]{:S(2)}) collective-permute-start(bf16[8,32,256]{2,1,0:T(8,128)(2,1)S(1)} %collective-permute-done.9.y_near), channel_id=1, source_target_pairs={{15,16},{16,15},{17,18},{18,17},{19,20},{20,19},{21,22},{22,21},{2... | collective-permute-start | bytes 393224 | tf_op jit(solution)/shard_map/ppermute | solution.py:332
  38.8 1.3 %copy-start.3 = (bf16[2,2,2,256,128]{4,3,2,1,0:T(8,128)(2,1)S(1)}, bf16[2,2,2,256,128]{4,3,2,1,0:T(8,128)(2,1)}, u32[]{:S(2)}) copy-start(bf16[2,2,2,256,128]{4,3,2,1,0:T(8,128)(2,1)} %up.5) | copy-start | bytes 1572868
  39.2 4.7 %collective-permute-start.10 = (bf16[6,32,256]{2,1,0:T(8,128)(2,1)S(1)}, bf16[6,32,256]{2,1,0:T(8,128)(2,1)S(1)}, u32[]{:S(2)}, u32[]{:S(2)}) collective-permute-start(bf16[6,32,256]{2,1,0:T(8,128)(2,1)S(1)} %second_far.1.own), channel_id=1, source_target_pairs={{0,1},{1,0},{2,3},{3,2},{4,5},{5,4},{6,7},{7,6},{8,9},{9,8},{10,11... | collective-permute-start | bytes 294920 | tf_op jit(solution)/shard_map/ppermute | solution.py:321
